TPU v7x, 128 devices: a whole 4x4x4 slice. The times are simulated.
128 devices in a mesh: seg: 32 (over y, z, core), sub: 4 (over x).
Axes of the slice: x: 4, y: 4, z: 4, core: 2. Of those that a mesh axis runs over, the one named last changes fastest.
Arguments:
- populations: float32 [2560, 19, 4096], P(('seg', 'sub')), as said below
- neighbours: int32 [2560, 18], P(('seg', 'sub')), may hold values from -1 to 2559, as said below
- site_flags: int32 [2560, 4096], P(('seg', 'sub')), may hold values from 0 to 3, as said below
Outputs:
- populations_out: float32 [2560, 19, 4096], P(('seg', 'sub'))
Inputs may be any that keep to these rules, and one draw needn't show every extreme that they name: `populations`: every entry is positive. `neighbours`: -1 marks an absent brick. Otherwise the named brick lies at most 20 places from this brick along the brick order, and its entry in the opposite direction names this brick. `site_flags`: 0 fluid, 1 wall, 2 inlet, 3 outlet; every kind occurs.
All inputs are finite; a program needn't handle non-finite values.
Results may differ from a plain program's by a relative error of at most 0.0003.
Values sent between devices are 32-bit elements; how exact they have to be, the bound alone decides.
No kernel may reach another device: no remote copies, remote signals or barrier semaphores. Data moves between devices by JAX's collectives and lax.ppermute only.
A program may use at most 256 MiB of HBM per device.

v0:
```python
import jax
import jax.numpy as jnp
import numpy as np
from jax import lax
from jax.sharding import PartitionSpec as P

BRICK = 16
STEPS = 2
REACH = 20


inlet_speed = 0.1


def with_halo(block, sides, width):
    for axis, dim in sides:
        count = lax.axis_size(axis)
        forward = [(i, i + 1) for i in range(count - 1)]
        backward = [(target, source) for source, target in forward]
        low = lax.ppermute(
            lax.slice_in_dim(block, block.shape[dim] - width, None, axis=dim), axis, forward
        )
        high = lax.ppermute(lax.slice_in_dim(block, 0, width, axis=dim), axis, backward)
        block = jnp.concatenate([low, block, high], axis=dim)
    return block


def lattice_speeds():
    return [
        [0, 0, 0],
        [1, 0, 0],
        [-1, 0, 0],
        [0, 1, 0],
        [0, -1, 0],
        [0, 0, 1],
        [0, 0, -1],
        [1, 1, 0],
        [-1, -1, 0],
        [1, -1, 0],
        [-1, 1, 0],
        [1, 0, 1],
        [-1, 0, -1],
        [1, 0, -1],
        [-1, 0, 1],
        [0, 1, 1],
        [0, -1, -1],
        [0, 1, -1],
        [0, -1, 1],
    ]


def lattice_weights():
    return [1.0 / 3.0] + [1.0 / 18.0] * 6 + [1.0 / 36.0] * 12


def opposite_list():
    return [0, 2, 1, 4, 3, 6, 5, 8, 7, 10, 9, 12, 11, 14, 13, 16, 15, 18, 17]


def relax_matrix():
    speeds = np.array(lattice_speeds()) * 1.0
    along_x = speeds[:, 0]
    along_y = speeds[:, 1]
    along_z = speeds[:, 2]
    monomials = [
        np.ones(19),
        along_x,
        along_y,
        along_z,
        along_x * along_x,
        along_y * along_y,
        along_z * along_z,
        along_x * along_y,
        along_x * along_z,
        along_y * along_z,
        along_x * along_x * along_y,
        along_x * along_x * along_z,
        along_y * along_y * along_x,
        along_y * along_y * along_z,
        along_z * along_z * along_x,
        along_z * along_z * along_y,
        along_x * along_x * along_y * along_y,
        along_x * along_x * along_z * along_z,
        along_y * along_y * along_z * along_z,
    ]
    orthonormal = []
    for vector in monomials:
        for earlier in orthonormal:
            vector = vector - np.dot(vector, earlier) * earlier
        orthonormal.append(vector / np.sqrt(np.dot(vector, vector)))
    moments = np.stack(orthonormal)
    rate_list = np.array([0.0] * 4 + [1.6] * 6 + [1.2] * 6 + [1.4] * 3)
    return np.dot(moments.T * rate_list[None, :], moments)


def face_members():
    speeds = np.array(lattice_speeds())
    members = []
    for face_id in range(6):
        normal = speeds[face_id + 1]
        members.append([member for member in range(19) if int(np.dot(speeds[member], normal)) == 1])
    return members


def equilibrium(density, velocity_field):
    speeds = jnp.asarray(lattice_speeds(), dtype=jnp.float32)
    weights = jnp.asarray(lattice_weights(), dtype=jnp.float32)
    projected = jnp.einsum("ic,bcs->bis", speeds, velocity_field, precision=lax.Precision.HIGHEST)
    square = jnp.sum(velocity_field * velocity_field, axis=1)[:, None, :]
    return (
        weights[None, :, None]
        * density[:, None, :]
        * (1.0 + 3.0 * projected + 4.5 * projected * projected - 1.5 * square)
    )


def collide(states, density, site_kinds, mean_density):
    speeds = jnp.asarray(lattice_speeds(), dtype=jnp.float32)
    momentum = jnp.einsum("ic,bis->bcs", speeds, states, precision=lax.Precision.HIGHEST)
    velocity_field = momentum / density[:, None, :]
    at_inlet = (site_kinds == 2)[:, None, :]
    axis_rows = lax.broadcasted_iota(jnp.int32, velocity_field.shape, 1)
    inlet_field = jnp.where(axis_rows == 0, inlet_speed, 0.0).astype(jnp.float32)
    chosen_field = jnp.where(at_inlet, inlet_field, velocity_field)
    chosen_density = jnp.where(site_kinds == 3, mean_density, density)
    balanced = equilibrium(chosen_density, chosen_field)
    relaxation = jnp.asarray(relax_matrix(), dtype=jnp.float32)
    relaxed = states - jnp.einsum(
        "ij,bjs->bis", relaxation, states - balanced, precision=lax.Precision.HIGHEST
    )
    bounced = states[:, np.array(opposite_list()), :]
    flag_rows = site_kinds[:, None, :]
    return jnp.where(flag_rows == 1, bounced, jnp.where(flag_rows == 0, relaxed, balanced))


def layer_flat(states):
    bricks = states.shape[0]
    plane = BRICK * BRICK
    brick_cube = states.reshape(bricks, 19, BRICK, plane)
    face_layers = []
    for face_id, members in enumerate(face_members()):
        dimension = face_id // 2
        position = BRICK - 1 if face_id % 2 == 0 else 0
        chosen = brick_cube[:, np.array(members)]
        if dimension == 0:
            sheet_out = chosen[:, :, position, :]
        elif dimension == 1:
            sheet_out = chosen[:, :, :, position * BRICK : (position + 1) * BRICK]
        else:
            sheet_out = chosen[:, :, :, position::BRICK]
        face_layers.append(sheet_out.reshape(bricks, 5, plane))
    return jnp.stack(face_layers, axis=1)


def expand_plane(values, dimension, bricks):
    plane = BRICK * BRICK
    if dimension == 0:
        return values.reshape(bricks, 1, plane)
    if dimension == 1:
        return jnp.tile(values, (1, 1, BRICK))
    return jnp.repeat(values, BRICK, axis=2)


def expand_line(line, free_dim):
    if free_dim == 0:
        return line[:, :, None]
    if free_dim == 1:
        return jnp.repeat(line, BRICK, axis=1)[:, None, :]
    return jnp.tile(line, (1, BRICK))[:, None, :]


def stream_flat(posted, rim_table, source, absent):
    bricks = posted.shape[0]
    plane = BRICK * BRICK
    brick_cube = posted.reshape(bricks, 19, BRICK, plane)
    first_coord = lax.broadcasted_iota(jnp.int32, (BRICK, plane), 0)
    merged = lax.broadcasted_iota(jnp.int32, (BRICK, plane), 1)
    coords = [first_coord, merged // BRICK, merged % BRICK]
    speeds = lattice_speeds()
    opposite = opposite_list()
    members = face_members()
    outputs = [brick_cube[:, 0]]
    for member in range(1, 19):
        stride = speeds[member]
        shifted = brick_cube[:, member]
        if stride[0] != 0:
            shifted = jnp.roll(shifted, stride[0], axis=1)
        lane_step = stride[1] * BRICK + stride[2]
        if lane_step != 0:
            shifted = jnp.roll(shifted, lane_step, axis=2)
        mirror = brick_cube[:, opposite[member]]
        crossed = [dimension for dimension in range(3) if stride[dimension] != 0]
        for dimension in crossed:
            heading = stride[dimension]
            toward = 2 * dimension + (1 if heading > 0 else 0)
            face_id = 2 * dimension + (0 if heading > 0 else 1)
            slot_id = members[face_id].index(member)
            incoming = rim_table[source[:, toward], face_id, slot_id].reshape(bricks, BRICK, BRICK)
            others = [other for other in range(3) if other != dimension]
            incoming = jnp.roll(incoming, (stride[others[0]], stride[others[1]]), axis=(1, 2))
            target = 0 if heading > 0 else BRICK - 1
            spread_in = expand_plane(incoming, dimension, bricks)
            chosen = jnp.where(absent[:, toward][:, None, None], mirror, spread_in)
            shifted = jnp.where((coords[dimension] == target)[None], chosen, shifted)
        if len(crossed) == 2:
            leading, second = crossed
            toward = opposite[member] - 1
            face_id = 2 * leading + (0 if stride[leading] > 0 else 1)
            slot_id = members[face_id].index(member)
            incoming = rim_table[source[:, toward], face_id, slot_id].reshape(bricks, BRICK, BRICK)
            others = [other for other in range(3) if other != leading]
            edge_place = BRICK - 1 if stride[second] > 0 else 0
            edge_line = lax.index_in_dim(
                incoming, edge_place, others.index(second) + 1, keepdims=False
            )
            free_dim = [other for other in range(3) if other not in crossed][0]
            targets = [
                0 if stride[leading] > 0 else BRICK - 1,
                0 if stride[second] > 0 else BRICK - 1,
            ]
            edge_mask = (coords[leading] == targets[0]) & (coords[second] == targets[1])
            chosen = jnp.where(
                absent[:, toward][:, None, None], mirror, expand_line(edge_line, free_dim)
            )
            shifted = jnp.where(edge_mask[None], chosen, shifted)
        outputs.append(shifted)
    return jnp.stack(outputs, axis=1).reshape(bricks, 19, BRICK * BRICK * BRICK)


def advance(current, site_flags, source, absent):
    density = jnp.sum(current, axis=1)
    fluid_sites = site_flags != 1
    summed, counted = lax.psum(
        (jnp.sum(jnp.where(fluid_sites, density, 0.0)), jnp.sum(fluid_sites.astype(jnp.float32))),
        ("seg", "sub"),
    )
    posted = collide(current, density, site_flags, summed / counted)
    ghosted = with_halo(posted, ((("seg", "sub"), 0),), REACH)
    rim_table = layer_flat(ghosted)
    return stream_flat(posted, rim_table, source, absent)


def on_device(populations, neighbours, site_flags):
    bricks = populations.shape[0]
    offset = lax.axis_index(("seg", "sub")) * bricks - REACH
    absent = neighbours < 0
    source = jnp.where(absent, 0, neighbours - offset)
    current = populations
    for repeat in range(STEPS):
        current = advance(current, site_flags, source, absent)
    return current


def solution(mesh):
    in_specs = (P(("seg", "sub"), None, None), P(("seg", "sub"), None), P(("seg", "sub"), None))
    out_specs = P(("seg", "sub"), None, None)
    return jax.shard_map(
        on_device, mesh=mesh, in_specs=in_specs, out_specs=out_specs, check_vma=False
    )
```

profile of v0, /device:TPU:1, one launch (start us, length us, event | category | flops | bytes accessed | tf_op | source)
XLA Modules:
  0.0 1526.9 jit_solution(4542468371667199112)
XLA Ops:
  1.3 3.6 reduce_sum.150
  6.3 12.0 multiply_reduce_fusion.1
  18.4 11.1 fusion.221
  29.5 7.2 gather_fusion
  36.8 68.7 %all-reduce.7 = (f32[]{:T(128)}, f32[]{:T(128)}) all-reduce(f32[]{:T(128)} %get-tuple-element.6, f32[]{:T(128)} %get-tuple-element.5), channel_id=1, replica_groups=mesh['seg'=32,'sub'=4] {'seg','sub'}, use_global_device_ids=true, to_apply=%region_2.3 | all-reduce | flops 2 | bytes 16 | tf_op jit(solution)/shard_map/psum | solution.py:233
  107.5 45.2 %fusion.10 = f32[20,19,4096]{2,1,0:T(8,128)} fusion(f32[19,20,4096]{2,1,0:T(8,128)} %gather_fusion, f32[19,19,1]{1,0,2:T(8,128)S(1)} %copy-done.185, f32[20,4096,19]{1,2,0:T(8,128)} %fusion.221, f32[20,19,4096]{2,0,1:T(8,128)} %param.39, f32[20,4096]{1,0:T(8,128)S(1)} %get-tuple-element.196, f32[20,4096]{1,0:T(8,128)S(1)} %get-tuple-element.88, ...), kind=kOutput, calls=%fused_computation.115 | convolution fusion | flops 386007040 | bytes 25724400 | tf_op jit(solution)/shard_map/ij,bjs->bis/dot_general | solution.py:128
  152.8 10.0 copy.722
  164.8 4.7 collective-permute-start.1
  169.5 8.6 reshape.2463
  179.8 5.0 slice_bitcast_fusion.41
  228.8 99.8 %collective-permute-done = f32[20,19,4096]{2,0,1:T(8,128)} collective-permute-done((f32[20,19,4096]{2,0,1:T(8,128)}, f32[20,19,4096]{2,0,1:T(8,128)}, u32[]{:S(2)}, u32[]{:S(2)}) %collective-permute-start) | collective-permute-done | bytes 6225952 | tf_op jit(solution)/shard_map/ppermute | solution.py:20
  328.6 7.0 copy.724
  335.6 7.4 copy.725
  343.0 8.2 pad_maximum_fusion
  351.2 22.3 %reshape.2464 = f32[60,19,16,256]{3,2,1,0:T(8,128)} reshape(f32[60,19,4096]{2,1,0:T(8,128)} %pad_maximum_fusion) | data formatting | bytes 37355520 | tf_op jit(solution)/shard_map/reshape | solution.py:139
  373.5 15.2 copy.841
  388.7 9.4 gather_fusion.1
  400.1 9.4 gather_fusion.2
  412.1 9.4 gather_fusion.3
  421.6 3.8 slice.1721
  428.3 9.4 gather_fusion.4
  437.7 3.4 slice.1722
  444.0 9.4 gather_fusion.5
  453.4 20.3 %slice.1133 = f32[60,5,16,16]{3,2,0,1:T(8,128)} slice(f32[60,5,16,256]{3,2,0,1:T(8,128)} %bitcast.1018), slice={[0:60:1], [0:5:1], [0:16:1], [15:256:16]} | slice | bytes 614400 | tf_op jit(solution)/shard_map/slice | solution.py:150
  477.3 9.4 gather_fusion.6
  486.7 20.1 %slice.1134 = f32[60,5,16,16]{3,2,0,1:T(8,128)} slice(f32[60,5,16,256]{3,2,0,1:T(8,128)} %bitcast.1015), slice={[0:60:1], [0:5:1], [0:16:1], [0:256:16]} | slice | bytes 614400 | tf_op jit(solution)/shard_map/slice | solution.py:150
  544.1 3.3 tile.291
  550.5 3.4 reshape.1777
  568.4 3.3 tile.275
  598.5 3.6 reshape.1753
  632.2 3.3 reshape.1765
  652.8 3.4 reshape.1773
  659.0 3.3 tile.289
  677.1 3.3 tile.262
  683.0 3.4 tile.265
  754.1 10.5 add_bitcast_fusion
  765.6 63.9 %psum.26 = f32[]{:T(128)} all-reduce(f32[]{:T(128)} %get-tuple-element.69), channel_id=1, replica_groups=mesh['seg'=32,'sub'=4] {'seg','sub'}, use_global_device_ids=true, to_apply=%region_7.8 | all-reduce | flops 1 | bytes 8 | tf_op jit(solution)/shard_map/psum | solution.py:233
  858.1 22.0 %stack.144 = f32[20,19,4096]{2,1,0:T(8,128)} concatenate(f32[20,1,4096]{2,1,0:T(1,128)S(1)} %copy-done.18, f32[20,1,4096]{2,1,0:T(1,128)S(1)} %stack.126, f32[20,1,4096]{2,1,0:T(1,128)S(1)} %stack.127, f32[20,1,4096]{2,1,0:T(1,128)S(1)} %stack.128, f32[20,1,4096]{2,1,0:T(1,128)S(1)} %stack.129, f32[20,1,4096]{2,1,0:T(1,128)S(1)} %stack.130, f32[20,1,4096]{2,1,0:T(1,128)S(1)} %stack.131, ...), dimensions={1} | concatenate | bytes 12451840 | tf_op jit(solution)/shard_map/stack | solution.py:227
  880.1 10.1 copy.779
  890.3 7.3 multiply_reduce_fusion
  897.6 11.5 fusion.222
  909.2 7.4 gather_fusion.49
  916.6 26.9 %fusion.7 = f32[20,19,4096]{2,1,0:T(8,128)} fusion(f32[20,19,4096]{2,1,0:T(8,128)} %stack.144, f32[19,20,4096]{2,1,0:T(8,128)} %gather_fusion.49, f32[19,19,1]{1,0,2:T(8,128)S(1)} %copy-done.186, f32[20,4096,19]{1,2,0:T(8,128)} %fusion.222, f32[20,4096]{1,0:T(8,128)S(1)} %broadcast_multiply_fusion, f32[20,4096]{1,0:T(8,128)S(1)} %broadcast_select_fusion, ...), kind=kOutput, calls=%fused_computation.110 | convolution fusion | flops 386007040 | bytes 25724400 | tf_op jit(solution)/shard_map/ij,bjs->bis/dot_general | solution.py:128
  943.5 10.0 copy.782
  956.2 4.1 collective-permute-start.3
  960.3 8.6 reshape.2465
  968.9 5.0 slice_bitcast_fusion.23
  1020.1 99.4 %collective-permute-done.2 = f32[20,19,4096]{2,0,1:T(8,128)} collective-permute-done((f32[20,19,4096]{2,0,1:T(8,128)}, f32[20,19,4096]{2,0,1:T(8,128)}, u32[]{:S(2)}, u32[]{:S(2)}) %collective-permute-start.2) | collective-permute-done | bytes 6225952 | tf_op jit(solution)/shard_map/ppermute | solution.py:20
  1119.6 7.0 copy.784
  1126.5 7.4 copy.785
  1133.9 8.2 pad_maximum_fusion.1
  1142.1 22.3 %reshape.2466 = f32[60,19,16,256]{3,2,1,0:T(8,128)} reshape(f32[60,19,4096]{2,1,0:T(8,128)} %pad_maximum_fusion.1) | data formatting | bytes 37355520 | tf_op jit(solution)/shard_map/reshape | solution.py:139
  1164.5 15.2 copy.855
  1179.7 9.5 gather_fusion.50
  1189.2 9.6 gather_fusion.51
  1198.8 9.5 gather_fusion.52
  1208.2 9.5 gather_fusion.53
  1217.7 9.6 gather_fusion.54
  1227.3 9.5 gather_fusion.55
  1245.0 3.4 slice.1892
  1251.3 20.3 %slice.1305 = f32[60,5,16,16]{3,2,0,1:T(8,128)} slice(f32[60,5,16,256]{3,2,0,1:T(8,128)} %bitcast.1012), slice={[0:60:1], [0:5:1], [0:16:1], [15:256:16]} | slice | bytes 614400 | tf_op jit(solution)/shard_map/slice | solution.py:150
  1275.2 20.1 %slice.1306 = f32[60,5,16,16]{3,2,0,1:T(8,128)} slice(f32[60,5,16,256]{3,2,0,1:T(8,128)} %bitcast.1011), slice={[0:60:1], [0:5:1], [0:16:1], [0:256:16]} | slice | bytes 614400 | tf_op jit(solution)/shard_map/slice | solution.py:150
  1494.3 22.1 %stack.165 = f32[20,19,4096]{2,1,0:T(8,128)} concatenate(f32[20,1,4096]{2,1,0:T(1,128)S(1)} %copy-done.19, f32[20,1,4096]{2,1,0:T(1,128)S(1)} %stack.147, f32[20,1,4096]{2,1,0:T(1,128)} %stack.148, f32[20,1,4096]{2,1,0:T(1,128)} %stack.149, f32[20,1,4096]{2,1,0:T(1,128)} %stack.150, f32[20,1,4096]{2,1,0:T(1,128)} %stack.151, f32[20,1,4096]{2,1,0:T(1,128)} %stack.152, ...), dimensions={1} | concatenate | bytes 12451840 | tf_op jit(solution)/shard_map/stack | solution.py:227
  1516.4 10.0 copy.839
  (1059 shorter events, 569.2 us)
Async XLA Ops:
  1.2 106.3 %copy-start.124 = (pred[20,4096]{1,0:T(8,128)(4,1)}, pred[20,4096]{1,0:T(8,128)(4,1)S(1)}, u32[]{:S(2)}) copy-start(pred[20,4096]{1,0:T(8,128)(4,1)S(1)} %get-tuple-element.141) | copy-start | bytes 245764
  1.2 106.3 %copy-start.126 = (pred[20,4096]{1,0:T(8,128)(4,1)}, pred[20,4096]{1,0:T(8,128)(4,1)S(1)}, u32[]{:S(2)}) copy-start(pred[20,4096]{1,0:T(8,128)(4,1)S(1)} %get-tuple-element.142) | copy-start | bytes 245764
  29.5 78.0 %copy-start.185 = (f32[19,19,1]{1,0,2:T(8,128)S(1)}, f32[19,19,1]{1,0,2:T(8,128)}, u32[]{:S(2)}) copy-start(f32[19,19,1]{1,0,2:T(8,128)} %constant.2100) | copy-start | bytes 4336
  29.5 78.0 %copy-start.189 = (f32[19]{0:T(128)S(1)}, f32[19]{0:T(128)}, u32[]{:S(2)}) copy-start(f32[19]{0:T(128)} %constant.119.clone) | copy-start | bytes 232
  162.7 165.9 %collective-permute-start = (f32[20,19,4096]{2,0,1:T(8,128)}, f32[20,19,4096]{2,0,1:T(8,128)}, u32[]{:S(2)}, u32[]{:S(2)}) collective-permute-start(f32[20,19,4096]{2,0,1:T(8,128)} %copy.722), channel_id=1, source_target_pairs={{0,1},{1,2},{2,3},{3,4},{4,5},{5,6},{6,7},{7,8},{8,9},{9,10},{10,1... | collective-permute-start | bytes 18677768 | tf_op jit(solution)/shard_map/ppermute | solution.py:20
  164.8 170.8 %collective-permute-start.1 = (f32[20,19,4096]{2,0,1:T(8,128)}, f32[20,19,4096]{2,0,1:T(8,128)}, u32[]{:S(2)}, u32[]{:S(2)}) collective-permute-start(f32[20,19,4096]{2,0,1:T(8,128)} %copy.722), channel_id=1, source_target_pairs={{1,0},{2,1},{3,2},{4,3},{5,4},{6,5},{7,6},{8,7},{9,8},{10,9},{11,1... | collective-permute-start | bytes 18677768 | tf_op jit(solution)/shard_map/ppermute | solution.py:23
  200.3 188.4 %copy-start.175 = (s32[1024]{0:T(1024)}, s32[1024]{0:T(1024)S(1)}, u32[]{:S(2)}) copy-start(s32[1024]{0:T(1024)S(1)} %get-tuple-element.195) | copy-start | bytes 12292
  200.3 199.8 %copy-start.173 = (s32[1024]{0:T(1024)}, s32[1024]{0:T(1024)S(1)}, u32[]{:S(2)}) copy-start(s32[1024]{0:T(1024)S(1)} %get-tuple-element.194) | copy-start | bytes 12292
  201.0 211.2 %copy-start.176 = (s32[1024]{0:T(1024)}, s32[1024]{0:T(1024)S(1)}, u32[]{:S(2)}) copy-start(s32[1024]{0:T(1024)S(1)} %get-tuple-element.193) | copy-start | bytes 12292
  201.0 227.3 %copy-start.174 = (s32[1024]{0:T(1024)}, s32[1024]{0:T(1024)S(1)}, u32[]{:S(2)}) copy-start(s32[1024]{0:T(1024)S(1)} %get-tuple-element.192) | copy-start | bytes 12292
  201.0 243.0 %copy-start.178 = (s32[1024]{0:T(1024)}, s32[1024]{0:T(1024)S(1)}, u32[]{:S(2)}) copy-start(s32[1024]{0:T(1024)S(1)} %get-tuple-element.191) | copy-start | bytes 12292
  201.0 276.3 %copy-start.177 = (s32[1024]{0:T(1024)}, s32[1024]{0:T(1024)S(1)}, u32[]{:S(2)}) copy-start(s32[1024]{0:T(1024)S(1)} %get-tuple-element.190) | copy-start | bytes 12292
  205.9 307.6 %copy-start.55 = (s32[20]{0:T(128)}, s32[20]{0:T(128)S(1)}, u32[]{:S(2)}) copy-start(s32[20]{0:T(128)S(1)} %get-tuple-element.16) | copy-start | bytes 244
  205.9 309.8 %copy-start.57 = (s32[20]{0:T(128)}, s32[20]{0:T(128)S(1)}, u32[]{:S(2)}) copy-start(s32[20]{0:T(128)S(1)} %get-tuple-element.8) | copy-start | bytes 244
  206.0 314.2 %copy-start.61 = (s32[20]{0:T(128)}, s32[20]{0:T(128)S(1)}, u32[]{:S(2)}) copy-start(s32[20]{0:T(128)S(1)} %get-tuple-element.13) | copy-start | bytes 244
  206.0 316.4 %copy-start.73 = (s32[20]{0:T(128)}, s32[20]{0:T(128)S(1)}, u32[]{:S(2)}) copy-start(s32[20]{0:T(128)S(1)} %get-tuple-element.24) | copy-start | bytes 244
  206.0 318.6 %copy-start.35 = (s32[20]{0:T(128)}, s32[20]{0:T(128)S(1)}, u32[]{:S(2)}) copy-start(s32[20]{0:T(128)S(1)} %get-tuple-element.21) | copy-start | bytes 244
  206.0 320.8 %copy-start.47 = (s32[20]{0:T(128)}, s32[20]{0:T(128)S(1)}, u32[]{:S(2)}) copy-start(s32[20]{0:T(128)S(1)} %get-tuple-element.23) | copy-start | bytes 244
  206.0 326.5 %copy-start.45 = (s32[20]{0:T(128)}, s32[20]{0:T(128)S(1)}, u32[]{:S(2)}) copy-start(s32[20]{0:T(128)S(1)} %get-tuple-element.19) | copy-start | bytes 244
  206.0 332.0 %copy-start.43 = (s32[20]{0:T(128)}, s32[20]{0:T(128)S(1)}, u32[]{:S(2)}) copy-start(s32[20]{0:T(128)S(1)} %get-tuple-element.7) | copy-start | bytes 244
  206.0 335.2 %copy-start.49 = (s32[20]{0:T(128)}, s32[20]{0:T(128)S(1)}, u32[]{:S(2)}) copy-start(s32[20]{0:T(128)S(1)} %get-tuple-element.15) | copy-start | bytes 244
  206.0 352.0 %copy-start.51 = (s32[20]{0:T(128)}, s32[20]{0:T(128)S(1)}, u32[]{:S(2)}) copy-start(s32[20]{0:T(128)S(1)} %get-tuple-element.12) | copy-start | bytes 244
  206.0 367.3 %copy-start.59 = (s32[20]{0:T(128)}, s32[20]{0:T(128)S(1)}, u32[]{:S(2)}) copy-start(s32[20]{0:T(128)S(1)} %get-tuple-element.17) | copy-start | bytes 244
  206.0 383.4 %copy-start.63 = (s32[20]{0:T(128)}, s32[20]{0:T(128)S(1)}, u32[]{:S(2)}) copy-start(s32[20]{0:T(128)S(1)} %get-tuple-element.9) | copy-start | bytes 244
  206.1 388.1 %copy-start.67 = (s32[20]{0:T(128)}, s32[20]{0:T(128)S(1)}, u32[]{:S(2)}) copy-start(s32[20]{0:T(128)S(1)} %get-tuple-element.20) | copy-start | bytes 244
  206.1 406.8 %copy-start.75 = (s32[20]{0:T(128)}, s32[20]{0:T(128)S(1)}, u32[]{:S(2)}) copy-start(s32[20]{0:T(128)S(1)} %get-tuple-element.10) | copy-start | bytes 244
  206.1 411.7 %copy-start.33 = (s32[20]{0:T(128)}, s32[20]{0:T(128)S(1)}, u32[]{:S(2)}) copy-start(s32[20]{0:T(128)S(1)} %get-tuple-element.25) | copy-start | bytes 244
  206.1 429.3 %copy-start.37 = (s32[20]{0:T(128)}, s32[20]{0:T(128)S(1)}, u32[]{:S(2)}) copy-start(s32[20]{0:T(128)S(1)} %get-tuple-element.11) | copy-start | bytes 244
  206.1 431.2 %copy-start.39 = (s32[20]{0:T(128)}, s32[20]{0:T(128)S(1)}, u32[]{:S(2)}) copy-start(s32[20]{0:T(128)S(1)} %get-tuple-element.22) | copy-start | bytes 244
  206.1 437.5 %copy-start.41 = (s32[20]{0:T(128)}, s32[20]{0:T(128)S(1)}, u32[]{:S(2)}) copy-start(s32[20]{0:T(128)S(1)} %get-tuple-element.14) | copy-start | bytes 244
  213.6 304.4 %copy-start.77 = (s32[20]{0:T(128)}, s32[20]{0:T(128)S(1)}, u32[]{:S(2)}) copy-start(s32[20]{0:T(128)S(1)} %get-tuple-element.156) | copy-start | bytes 244
  213.6 333.9 %copy-start.69 = (s32[20]{0:T(128)}, s32[20]{0:T(128)S(1)}, u32[]{:S(2)}) copy-start(s32[20]{0:T(128)S(1)} %get-tuple-element.159) | copy-start | bytes 244
  213.6 340.4 %copy-start.65 = (s32[20]{0:T(128)}, s32[20]{0:T(128)S(1)}, u32[]{:S(2)}) copy-start(s32[20]{0:T(128)S(1)} %get-tuple-element.161) | copy-start | bytes 244
  213.6 350.4 %copy-start.71 = (s32[20]{0:T(128)}, s32[20]{0:T(128)S(1)}, u32[]{:S(2)}) copy-start(s32[20]{0:T(128)S(1)} %get-tuple-element.157) | copy-start | bytes 244
  213.6 388.5 %copy-start.79 = (s32[20]{0:T(128)}, s32[20]{0:T(128)S(1)}, u32[]{:S(2)}) copy-start(s32[20]{0:T(128)S(1)} %get-tuple-element.155) | copy-start | bytes 244
  213.6 411.7 %copy-start.53 = (s32[20]{0:T(128)}, s32[20]{0:T(128)S(1)}, u32[]{:S(2)}) copy-start(s32[20]{0:T(128)S(1)} %get-tuple-element.44) | copy-start | bytes 244
  215.1 324.2 %copy-start.100 = (pred[16,256]{1,0:T(8,128)(4,1)}, pred[16,256]{1,0:T(8,128)(4,1)S(1)}, u32[]{:S(2)}) copy-start(pred[16,256]{1,0:T(8,128)(4,1)S(1)} %get-tuple-element.182) | copy-start | bytes 12292
  215.1 324.2 %copy-start.104 = (pred[16,256]{1,0:T(8,128)(4,1)}, pred[16,256]{1,0:T(8,128)(4,1)S(1)}, u32[]{:S(2)}) copy-start(pred[16,256]{1,0:T(8,128)(4,1)S(1)} %get-tuple-element.185) | copy-start | bytes 12292
  215.1 324.2 %copy-start.135 = (pred[16,256]{1,0:T(8,128)(4,1)}, pred[16,256]{1,0:T(8,128)(4,1)S(1)}, u32[]{:S(2)}) copy-start(pred[16,256]{1,0:T(8,128)(4,1)S(1)} %get-tuple-element.162) | copy-start | bytes 12292
  686.4 67.6 %copy-start.32 = (f32[20,1,16,255]{3,2,0,1:T(8,128)S(1)}, f32[20,1,16,255]{3,2,0,1:T(8,128)}, u32[]{:S(2)}) copy-start(f32[20,1,16,255]{3,2,0,1:T(8,128)} %fusion.52) | copy-start | bytes 979204
  686.5 67.6 %copy-start.101 = (pred[16,256]{1,0:T(8,128)(4,1)S(1)}, pred[16,256]{1,0:T(8,128)(4,1)}, u32[]{:S(2)}) copy-start(pred[16,256]{1,0:T(8,128)(4,1)} %copy-done.100) | copy-start | bytes 12292
  686.5 67.5 %copy-start.105 = (pred[16,256]{1,0:T(8,128)(4,1)S(1)}, pred[16,256]{1,0:T(8,128)(4,1)}, u32[]{:S(2)}) copy-start(pred[16,256]{1,0:T(8,128)(4,1)} %copy-done.104) | copy-start | bytes 12292
  686.5 67.5 %copy-start.139 = (pred[16,256]{1,0:T(8,128)(4,1)S(1)}, pred[16,256]{1,0:T(8,128)(4,1)}, u32[]{:S(2)}) copy-start(pred[16,256]{1,0:T(8,128)(4,1)} %get-tuple-element.178) | copy-start | bytes 12292
  686.5 67.5 %copy-start.141 = (pred[16,256]{1,0:T(8,128)(4,1)S(1)}, pred[16,256]{1,0:T(8,128)(4,1)}, u32[]{:S(2)}) copy-start(pred[16,256]{1,0:T(8,128)(4,1)} %get-tuple-element.174) | copy-start | bytes 12292
  686.5 67.5 %copy-start.143 = (pred[16,256]{1,0:T(8,128)(4,1)S(1)}, pred[16,256]{1,0:T(8,128)(4,1)}, u32[]{:S(2)}) copy-start(pred[16,256]{1,0:T(8,128)(4,1)} %get-tuple-element.164) | copy-start | bytes 12292
  686.5 67.5 %copy-start.145 = (pred[16,256]{1,0:T(8,128)(4,1)S(1)}, pred[16,256]{1,0:T(8,128)(4,1)}, u32[]{:S(2)}) copy-start(pred[16,256]{1,0:T(8,128)(4,1)} %get-tuple-element.163) | copy-start | bytes 12292
  686.5 67.5 %copy-start.147 = (pred[16,256]{1,0:T(8,128)(4,1)S(1)}, pred[16,256]{1,0:T(8,128)(4,1)}, u32[]{:S(2)}) copy-start(pred[16,256]{1,0:T(8,128)(4,1)} %get-tuple-element.181) | copy-start | bytes 12292
  686.5 67.5 %copy-start.149 = (pred[16,256]{1,0:T(8,128)(4,1)S(1)}, pred[16,256]{1,0:T(8,128)(4,1)}, u32[]{:S(2)}) copy-start(pred[16,256]{1,0:T(8,128)(4,1)} %get-tuple-element.177) | copy-start | bytes 12292
  686.5 67.5 %copy-start.151 = (pred[16,256]{1,0:T(8,128)(4,1)S(1)}, pred[16,256]{1,0:T(8,128)(4,1)}, u32[]{:S(2)}) copy-start(pred[16,256]{1,0:T(8,128)(4,1)} %get-tuple-element.180) | copy-start | bytes 12292
  686.5 67.5 %copy-start.153 = (pred[16,256]{1,0:T(8,128)(4,1)S(1)}, pred[16,256]{1,0:T(8,128)(4,1)}, u32[]{:S(2)}) copy-start(pred[16,256]{1,0:T(8,128)(4,1)} %get-tuple-element.176) | copy-start | bytes 12292
  953.5 166.0 %collective-permute-start.2 = (f32[20,19,4096]{2,0,1:T(8,128)}, f32[20,19,4096]{2,0,1:T(8,128)}, u32[]{:S(2)}, u32[]{:S(2)}) collective-permute-start(f32[20,19,4096]{2,0,1:T(8,128)} %copy.782), channel_id=1, source_target_pairs={{0,1},{1,2},{2,3},{3,4},{4,5},{5,6},{6,7},{7,8},{8,9},{9,10},{10,1... | collective-permute-start | bytes 18677768 | tf_op jit(solution)/shard_map/ppermute | solution.py:20
  956.2 170.4 %collective-permute-start.3 = (f32[20,19,4096]{2,0,1:T(8,128)}, f32[20,19,4096]{2,0,1:T(8,128)}, u32[]{:S(2)}, u32[]{:S(2)}) collective-permute-start(f32[20,19,4096]{2,0,1:T(8,128)} %copy.782), channel_id=1, source_target_pairs={{1,0},{2,1},{3,2},{4,3},{5,4},{6,5},{7,6},{8,7},{9,8},{10,9},{11,1... | collective-permute-start | bytes 18677768 | tf_op jit(solution)/shard_map/ppermute | solution.py:23
  1299.0 31.9 %copy-start.50 = (s32[20]{0:T(128)S(1)}, s32[20]{0:T(128)}, u32[]{:S(2)}) copy-start(s32[20]{0:T(128)} %copy-done.49) | copy-start | bytes 244
  1300.0 32.4 %copy-start.70 = (s32[20]{0:T(128)S(1)}, s32[20]{0:T(128)}, u32[]{:S(2)}) copy-start(s32[20]{0:T(128)} %copy-done.69) | copy-start | bytes 244
  1300.1 35.3 %copy-start.66 = (s32[20]{0:T(128)S(1)}, s32[20]{0:T(128)}, u32[]{:S(2)}) copy-start(s32[20]{0:T(128)} %copy-done.65) | copy-start | bytes 244
  1300.1 36.8 %copy-start.48 = (s32[20]{0:T(128)S(1)}, s32[20]{0:T(128)}, u32[]{:S(2)}) copy-start(s32[20]{0:T(128)} %copy-done.47) | copy-start | bytes 244
  1300.1 38.3 %copy-start.46 = (s32[20]{0:T(128)S(1)}, s32[20]{0:T(128)}, u32[]{:S(2)}) copy-start(s32[20]{0:T(128)} %copy-done.45) | copy-start | bytes 244
  1300.1 41.3 %copy-start.44 = (s32[20]{0:T(128)S(1)}, s32[20]{0:T(128)}, u32[]{:S(2)}) copy-start(s32[20]{0:T(128)} %copy-done.43) | copy-start | bytes 244
  1302.1 46.9 %copy-start.42 = (s32[20]{0:T(128)S(1)}, s32[20]{0:T(128)}, u32[]{:S(2)}) copy-start(s32[20]{0:T(128)} %copy-done.41) | copy-start | bytes 244
  1302.2 48.5 %copy-start.40 = (s32[20]{0:T(128)S(1)}, s32[20]{0:T(128)}, u32[]{:S(2)}) copy-start(s32[20]{0:T(128)} %copy-done.39) | copy-start | bytes 244
  1303.9 51.2 %copy-start.38 = (s32[20]{0:T(128)S(1)}, s32[20]{0:T(128)}, u32[]{:S(2)}) copy-start(s32[20]{0:T(128)} %copy-done.37) | copy-start | bytes 244
  1304.0 52.0 %copy-start.36 = (s32[20]{0:T(128)S(1)}, s32[20]{0:T(128)}, u32[]{:S(2)}) copy-start(s32[20]{0:T(128)} %copy-done.35) | copy-start | bytes 244
  1311.5 49.0 %copy-start.54 = (s32[20]{0:T(128)S(1)}, s32[20]{0:T(128)}, u32[]{:S(2)}) copy-start(s32[20]{0:T(128)} %copy-done.53) | copy-start | bytes 244
  1312.3 49.7 %copy-start.34 = (s32[20]{0:T(128)S(1)}, s32[20]{0:T(128)}, u32[]{:S(2)}) copy-start(s32[20]{0:T(128)} %copy-done.33) | copy-start | bytes 244
  (135 other events, 1521.7 us)
where the time goes:
time: 1550 us; the launch traced here: 1530 us
  local copies, waits for them, and re-layouts  954 us (62%)
  waiting for transfers between devices  199 us (13%)
  blocking collectives  133 us (9%)
  matrix products  114 us (7%)
  other arithmetic  106 us (7%)
    ppermute x2, waiting for transfers between devices, with_halo(): lax.ppermute(lax.slice_in_dim(block, block.shape[dim] - width, None, axis...  199 us
    psum x2, blocking collectives, advance(): lax.psum((jnp.sum(jnp.where(fluid_sites, density, 0.0)), jnp.sum(fluid_si...  133 us
    another operation x42, local copies, waits for them, and re-layouts, stream_flat(): return jnp.stack(outputs, axis=1).reshape(bricks, 19, BRICK * BRICK * BRICK)  114 us
    gather x12, local copies, waits for them, and re-layouts, layer_flat(): chosen = brick_cube[:, np.array(members)]  114 us
    gather x84, local copies, waits for them, and re-layouts, stream_flat(): rim_table[source[:, toward], face_id, slot_id].reshape(bricks, BRICK, BRICK)  104 us
    slice x8, local copies, waits for them, and re-layouts, layer_flat(): sheet_out = chosen[:, :, :, position::BRICK]  91.4 us
    reshape x4, local copies, waits for them, and re-layouts, layer_flat(): brick_cube = states.reshape(bricks, 19, BRICK, plane)  75.1 us
    another operation x44, local copies, waits for them, and re-layouts, expand_plane(): return jnp.tile(values, (1, 1, BRICK))  75 us
  transfers between devices with their start and end apart: 4, of which 2 were waited for; matrix products, arithmetic and copies ran while one was open for 9% of the time, Pallas kernels for 0%

commit v1 on v0

v1 whole, which is shorter than its diff:
```python
import functools

import jax
import jax.numpy as jnp
import numpy as np
from jax import lax
from jax.experimental import pallas as pl
from jax.experimental.pallas import tpu as pltpu
from jax.sharding import PartitionSpec as P

BRICK = 16
PLANE = 256
SITES = 4096
GROUP = 4
AXES = ("seg", "sub")
INLET = 0.1

SPEEDS = [
    (0, 0, 0),
    (1, 0, 0), (-1, 0, 0), (0, 1, 0), (0, -1, 0), (0, 0, 1), (0, 0, -1),
    (1, 1, 0), (-1, -1, 0), (1, -1, 0), (-1, 1, 0),
    (1, 0, 1), (-1, 0, -1), (1, 0, -1), (-1, 0, 1),
    (0, 1, 1), (0, -1, -1), (0, 1, -1), (0, -1, 1),
]
OPP = [0, 2, 1, 4, 3, 6, 5, 8, 7, 10, 9, 12, 11, 14, 13, 16, 15, 18, 17]


def face_of(speed, dim):
    return 2 * dim + (0 if speed[dim] > 0 else 1)


MEMBERS = [[i for i in range(19) if any(face_of(SPEEDS[i], d) == f and SPEEDS[i][d] for d in range(3))]
           for f in range(6)]
COLUMN_FACE = []
for _d in range(18):
    _m = SPEEDS[OPP[_d + 1]]
    _lead = [k for k in range(3) if _m[k]][0]
    COLUMN_FACE.append(face_of(_m, _lead))


def iota(shape, dim):
    return lax.broadcasted_iota(jnp.int32, shape, dim)


def roll(x, shift, axis):
    shift = shift % x.shape[axis]
    return x if shift == 0 else pltpu.roll(x, shift, axis)


def collide(f, kind, mean):
    fluid = kind == 0
    wall = kind == 1
    inlet = kind == 2
    outlet = kind == 3
    even = [f[2 * k + 1] + f[2 * k + 2] for k in range(9)]
    odd = [f[2 * k + 1] - f[2 * k + 2] for k in range(9)]
    density = f[0] + ((even[0] + even[1]) + (even[2] + even[3])) + (
        (even[4] + even[5]) + (even[6] + even[7])) + even[8]
    inverse = 1.0 / density
    ux = (odd[0] + odd[3] + odd[4] + odd[5] + odd[6]) * inverse
    uy = (odd[1] + odd[3] - odd[4] + odd[7] + odd[8]) * inverse
    uz = (odd[2] + odd[5] - odd[6] + odd[7] - odd[8]) * inverse
    ux = jnp.where(inlet, INLET, ux)
    uy = jnp.where(inlet, 0.0, uy)
    uz = jnp.where(inlet, 0.0, uz)
    rho = jnp.where(outlet, mean, density)
    base = 1.0 - 1.5 * (ux * ux + uy * uy + uz * uz)
    along = [ux, uy, uz, ux + uy, ux - uy, ux + uz, ux - uz, uy + uz, uy - uz]
    keep_even = jnp.where(fluid, -0.3, jnp.where(wall, 0.5, 0.0))
    take_even = jnp.where(fluid, 0.8, jnp.where(wall, 0.0, 0.5))
    keep_odd = jnp.where(fluid, -0.1, jnp.where(wall, -0.5, 0.0))
    take_odd = jnp.where(fluid, 0.6, jnp.where(wall, 0.0, 0.5))
    fourth = jnp.where(fluid, 0.2 / 12.0, 0.0)
    rho9 = rho * (1.0 / 9.0)
    rho18 = rho * (1.0 / 18.0)
    eq_even = []
    for k in range(9):
        scale = rho9 if k < 3 else rho18
        eq_even.append(scale * (base + 4.5 * along[k] * along[k]))
    eq_rest = (rho * (1.0 / 3.0)) * base
    g_rest = f[0] - eq_rest
    g = [even[k] - eq_even[k] for k in range(9)]
    four = 4.0 * g_rest
    gx, gy, gz = 2.0 * g[0], 2.0 * g[1], 2.0 * g[2]
    ta = four - gx - gy + (g[3] + g[4])
    tb = four - gx - gz + (g[5] + g[6])
    tc = four - gy - gz + (g[7] + g[8])
    shared = (2.0 / 7.0) * (ta + tb + tc)
    ka = (ta - shared) * fourth
    kb = (tb - shared) * fourth
    kc = (tc - shared) * fourth
    kab, kac, kbc = ka + kb, ka + kc, kb + kc
    modes = [-2.0 * kab, -2.0 * kac, -2.0 * kbc, ka, ka, kb, kb, kc, kc]
    odd9 = rho * take_odd * (1.0 / 3.0)
    odd18 = rho * take_odd * (1.0 / 6.0)
    out = [2.0 * (keep_even * f[0] + take_even * eq_rest) + 4.0 * (kab + kc)]
    for k in range(9):
        half_even = keep_even * even[k] + take_even * eq_even[k] + modes[k]
        half_odd = keep_odd * odd[k] + (odd9 if k < 3 else odd18) * along[k]
        out.append(half_even + half_odd)
        out.append(half_even - half_odd)
    return out, density


def cyclic(halves, speed):
    lane = iota((BRICK, 128), 1)
    cx, cy, cz = speed
    low, high = halves
    if cx:
        low, high = roll(low, cx, 0), roll(high, cx, 0)
    if cy:
        first, second = roll(low, 16 * cy, 1), roll(high, 16 * cy, 1)
        carried = lane < 16 if cy > 0 else lane >= 112
        low, high = jnp.where(carried, second, first), jnp.where(carried, first, second)
    if cz:
        wrapped = (lane & 15) == (0 if cz > 0 else 15)
        low = jnp.where(wrapped, roll(low, -15 * cz, 1), roll(low, cz, 1))
        high = jnp.where(wrapped, roll(high, -15 * cz, 1), roll(high, cz, 1))
    return low, high


def pack_faces(table, row, values):
    lane = iota((BRICK, 128), 1)
    for face in range(6):
        dim = face // 2
        place = 0 if face % 2 == 0 else 15
        packed = None
        for slot, member in enumerate(MEMBERS[face]):
            low, high = values(member, face)
            if dim == 0:
                table[row, face, slot:slot + 1, :] = low[place:place + 1, :]
                table[row, face, 8 + slot:9 + slot, :] = high[place:place + 1, :]
            elif dim == 1:
                piece = low if place == 0 else high
                moved = roll(piece, 16 * slot - (0 if place == 0 else 112), 1)
                packed = moved if packed is None else jnp.where((lane >> 4) == slot, moved, packed)
            else:
                first, second = roll(low, slot - place, 1), roll(high, 8 + slot - place, 1)
                packed = first if packed is None else jnp.where((lane & 15) == slot, first, packed)
                packed = jnp.where((lane & 15) == 8 + slot, second, packed)
        if dim != 0:
            table[row, face] = packed


def shift_and_pack(posted, q, moved, faces, mirrors):
    def halves(member):
        return posted[member, :, 0:128], posted[member, :, 128:256]

    for member in range(19):
        low, high = cyclic(halves(member), SPEEDS[member])
        moved[q, member, :, 0:128] = low
        moved[q, member, :, 128:256] = high
    pack_faces(faces, q, lambda m, face: (moved[q, m, :, 0:128], moved[q, m, :, 128:256]))
    pack_faces(mirrors, q, lambda m, face: halves(OPP[m]))


def arrive(moved, q, member, table, source):
    lane = iota((BRICK, 128), 1)
    sub = iota((BRICK, 128), 0)
    speed = SPEEDS[member]
    cx, cy, cz = speed
    parts = [moved[q, member, :, 0:128], moved[q, member, :, 128:256]]

    def column(dim):
        return 2 * dim + (1 if speed[dim] > 0 else 0)

    edge = OPP[member] - 1
    if cy:
        face = face_of(speed, 1)
        slot = MEMBERS[face].index(member)
        place = 0 if cy > 0 else 15
        half = place // 8
        shift = (0 if place == 0 else 112) - 16 * slot
        here = (lane >> 4) == place % 8
        block = table[source(column(1))]
        if cz:
            corner = here & ((lane & 15) == (0 if cz > 0 else 15))
        parts[half] = jnp.where(here, roll(block, shift, 1), parts[half])
    if cz:
        face = face_of(speed, 2)
        slot = MEMBERS[face].index(member)
        place = 0 if cz > 0 else 15
        here = (lane & 15) == place
        block = table[source(column(2))]
        parts[0] = jnp.where(here, roll(block, place - slot, 1), parts[0])
        parts[1] = jnp.where(here, roll(block, place - slot - 8, 1), parts[1])
    if cy and cz:
        face = face_of(speed, 1)
        slot = MEMBERS[face].index(member)
        place = 0 if cy > 0 else 15
        shift = (0 if place == 0 else 112) - 16 * slot
        half = place // 8
        parts[half] = jnp.where(corner, roll(table[source(edge)], shift, 1), parts[half])
    if cx:
        face = face_of(speed, 0)
        slot = MEMBERS[face].index(member)
        place = 0 if cx > 0 else 15
        row_lane = iota((1, 128), 1)
        for half in range(2):
            line = table[source(column(0)), 8 * half + slot:8 * half + slot + 1, :]
            spot = None
            if cy:
                across = 0 if cy > 0 else 15
                if across // 8 == half:
                    spot = (row_lane >> 4) == across % 8
            elif cz:
                spot = (row_lane & 15) == (0 if cz > 0 else 15)
            if spot is not None:
                other = table[source(edge), 8 * half + slot:8 * half + slot + 1, :]
                line = jnp.where(spot, other, line)
            parts[half] = jnp.where(sub == place, jnp.broadcast_to(line, (BRICK, 128)), parts[half])
    return parts


def mean_of(gathered):
    total = jnp.sum(gathered[...], axis=0, keepdims=True)
    ratio = total / pltpu.roll(total, 64, 1)
    return jnp.broadcast_to(ratio[:, 0:1], (8, 128))


def collide_brick(load, kinds, q, posted, mean):
    for g in range(2):
        for h in range(2):
            rows, lanes = slice(8 * g, 8 * g + 8), slice(128 * h, 128 * h + 128)
            f = [load(i, g, h) for i in range(19)]
            out, _ = collide(f, kinds[q, rows, lanes], mean)
            for i in range(19):
                posted[i, rows, lanes] = out[i]


def first_kernel(gathered, pops, kinds, moved, faces, mirrors, tiles, posted):
    mean = mean_of(gathered)

    def brick(q, carry):
        for r in range(3):
            high = 8 if r < 2 else 3
            for c in range(32):
                start = (r * 32 + c) * 8
                tiles[start:start + high, :] = pops[q, 8 * r:8 * r + high, 128 * c:128 * c + 128]

        def load(i, g, h):
            start = ((i // 8) * 32 + 16 * g + h) * 8 + i % 8
            return tiles[pl.ds(start, 8, stride=16), :]

        collide_brick(load, kinds, q, posted, mean)
        shift_and_pack(posted, q, moved, faces, mirrors)
        return carry

    lax.fori_loop(0, GROUP, brick, 0)


def later_kernel(gathered, pops, kinds, moved, faces, mirrors, posted):
    mean = mean_of(gathered)

    def brick(q, carry):
        def load(i, g, h):
            return pops[q, i, 8 * g:8 * g + 8, 128 * h:128 * h + 128]

        collide_brick(load, kinds, q, posted, mean)
        shift_and_pack(posted, q, moved, faces, mirrors)
        return carry

    lax.fori_loop(0, GROUP, brick, 0)


def fill_table(pieces, table, sems):
    copies = []
    start = 0
    for k, piece in enumerate(pieces):
        count = piece.shape[0]
        copies.append(pltpu.make_async_copy(piece, table.at[pl.ds(start, count)], sems.at[k]))
        start += count
    for copy in copies:
        copy.start()
    for copy in copies:
        copy.wait()


def arrive_sum_kernel(index, moved, kinds, own, mirror, even, odd, pops, sums, table, sems):
    step = pl.program_id(0)

    @pl.when(step == 0)
    def _():
        fill_table((own, mirror, even, odd), table, sems)
        sums[...] = jnp.zeros_like(sums)

    def brick(q, carry):
        base = (step * GROUP + q) * 18
        source = lambda column: index[base + column]
        total = [None, None]
        for member in range(19):
            parts = arrive(moved, q, member, table, source)
            for h in range(2):
                pops[q, member, :, 128 * h:128 * h + 128] = parts[h]
                total[h] = parts[h] if total[h] is None else total[h] + parts[h]
        for h in range(2):
            open_site = kinds[q, :, 128 * h:128 * h + 128] != 1
            sums[0] += jnp.where(open_site, total[h], 0.0)
            sums[1] += jnp.where(open_site, 1.0, 0.0)
        return carry

    lax.fori_loop(0, GROUP, brick, 0)


def arrive_out_kernel(index, moved, own, mirror, even, odd, out, table, tiles, sems):
    step = pl.program_id(0)

    @pl.when(step == 0)
    def _():
        fill_table((own, mirror, even, odd), table, sems)

    def brick(q, carry):
        base = (step * GROUP + q) * 18
        source = lambda column: index[base + column]
        for member in range(19):
            parts = arrive(moved, q, member, table, source)
            for g in range(2):
                for h in range(2):
                    start = ((member // 8) * 32 + 16 * g + h) * 8 + member % 8
                    tiles[pl.ds(start, 8, stride=16), :] = parts[h][8 * g:8 * g + 8, :]
        for r in range(3):
            high = 8 if r < 2 else 3
            for c in range(32):
                start = (r * 32 + c) * 8
                out[q, 8 * r:8 * r + high, 128 * c:128 * c + 128] = tiles[start:start + high, :]
        return carry

    lax.fori_loop(0, GROUP, brick, 0)


def params():
    return pltpu.CompilerParams(
        dimension_semantics=("arbitrary",), vmem_limit_bytes=48 * 1024 * 1024)


def brick_spec(*shape):
    return pl.BlockSpec((GROUP,) + shape, lambda i: (i,) + (0,) * len(shape))


def whole_spec(*shape):
    return pl.BlockSpec(shape, lambda i: (0,) * len(shape))


MOVED = (19, BRICK, PLANE)
LAYERS = (6, BRICK, 128)
F32 = jnp.float32


def collide_call(gathered, pops, kinds, native):
    bricks = pops.shape[0]
    scratch = [pltpu.VMEM((768, 128), F32)] if native else []
    return pl.pallas_call(
        first_kernel if native else later_kernel,
        grid=(bricks // GROUP,),
        in_specs=[whole_spec(*gathered.shape),
                  brick_spec(19, SITES) if native else brick_spec(*MOVED),
                  brick_spec(BRICK, PLANE)],
        out_specs=[brick_spec(*MOVED), brick_spec(*LAYERS), brick_spec(*LAYERS)],
        out_shape=[jax.ShapeDtypeStruct((bricks,) + MOVED, F32),
                   jax.ShapeDtypeStruct((bricks,) + LAYERS, F32),
                   jax.ShapeDtypeStruct((bricks,) + LAYERS, F32)],
        scratch_shapes=scratch + [pltpu.VMEM(MOVED, F32)],
        compiler_params=params(),
        name="collide_shift",
    )(gathered, pops, kinds)


def table_rows(pieces):
    return sum(piece.shape[0] for piece in pieces)


def arrive_sum_call(index, moved, kinds, pieces):
    bricks = moved.shape[0]
    anywhere = pl.BlockSpec(memory_space=pl.ANY)
    return pl.pallas_call(
        arrive_sum_kernel,
        grid=(bricks // GROUP,),
        in_specs=[pl.BlockSpec(memory_space=pltpu.SMEM), brick_spec(*MOVED),
                  brick_spec(BRICK, PLANE)] + [anywhere] * 4,
        out_specs=[brick_spec(*MOVED), whole_spec(2, BRICK, 128)],
        out_shape=[jax.ShapeDtypeStruct((bricks,) + MOVED, F32),
                   jax.ShapeDtypeStruct((2, BRICK, 128), F32)],
        scratch_shapes=[pltpu.VMEM((table_rows(pieces), BRICK, 128), F32),
                        pltpu.SemaphoreType.DMA((4,))],
        compiler_params=params(),
        name="arrive_sum",
    )(index, moved, kinds, *pieces)


def arrive_out_call(index, moved, pieces):
    bricks = moved.shape[0]
    anywhere = pl.BlockSpec(memory_space=pl.ANY)
    return pl.pallas_call(
        arrive_out_kernel,
        grid=(bricks // GROUP,),
        in_specs=[pl.BlockSpec(memory_space=pltpu.SMEM), brick_spec(*MOVED)] + [anywhere] * 4,
        out_specs=brick_spec(19, SITES),
        out_shape=jax.ShapeDtypeStruct((bricks, 19, SITES), F32),
        scratch_shapes=[pltpu.VMEM((table_rows(pieces), BRICK, 128), F32),
                        pltpu.VMEM((768, 128), F32),
                        pltpu.SemaphoreType.DMA((4,))],
        compiler_params=params(),
        name="arrive_out",
    )(index, moved, *pieces)


def gather_sums(summed, counted, devices):
    left = iota((devices, 128), 1) < 64
    rows = jnp.where(left, summed, counted)
    return lax.all_to_all(rows, AXES, 0, 0, tiled=True)


def swap_layers(layers, devices):
    even_pairs = [(i, i ^ 1) for i in range(devices)]
    odd_pairs = [(i, i + 1) for i in range(1, devices - 1, 2)]
    odd_pairs = odd_pairs + [(b, a) for a, b in odd_pairs]
    return lax.ppermute(layers, AXES, even_pairs), lax.ppermute(layers, AXES, odd_pairs)


def on_device(devices, populations, neighbours, site_flags):
    bricks = populations.shape[0]
    blocks = bricks * 6
    kinds = site_flags.reshape(bricks, BRICK, PLANE)
    me = lax.axis_index(AXES)
    local = neighbours - me * bricks
    parity = me % 2
    after = jnp.where(parity == 0, 2 * blocks, 3 * blocks)
    before = jnp.where(parity == 0, 3 * blocks, 2 * blocks)
    brick_id = iota((bricks, 18), 0)
    place = jnp.where(local < 0, before + (local + bricks) * 6,
                      jnp.where(local >= bricks, after + (local - bricks) * 6, local * 6))
    place = jnp.where(neighbours < 0, blocks + brick_id * 6, place)
    index = (place + jnp.asarray(np.array(COLUMN_FACE, np.int32))[None, :]).reshape(-1)

    open_site = (site_flags != 1)[:, None, :]
    summed = jnp.sum(jnp.where(open_site, populations, 0.0))
    counted = jnp.sum((site_flags != 1).astype(F32))
    flat = lambda layers: layers.reshape(blocks, BRICK, 128)

    gathered = gather_sums(summed, counted, devices)
    moved, faces, mirrors = collide_call(gathered, populations, kinds, True)
    pieces = (flat(faces), flat(mirrors)) + swap_layers(flat(faces), devices)
    pops, sums = arrive_sum_call(index, moved, kinds, pieces)
    totals = jnp.sum(sums, axis=(1, 2))
    gathered = gather_sums(totals[0], totals[1], devices)
    moved, faces, mirrors = collide_call(gathered, pops, kinds, False)
    pieces = (flat(faces), flat(mirrors)) + swap_layers(flat(faces), devices)
    return arrive_out_call(index, moved, pieces)


def solution(mesh):
    devices = mesh.shape["seg"] * mesh.shape["sub"]
    in_specs = (P(AXES, None, None), P(AXES, None), P(AXES, None))
    return jax.shard_map(
        functools.partial(on_device, devices), mesh=mesh, in_specs=in_specs,
        out_specs=P(AXES, None, None), check_vma=False)
```

time: 1550 us -> 169 us (0.11); the launches traced: 1530 us -> 168 us
  local copies, waits for them, and re-layouts: 954 us -> 21.5 us
  waiting for transfers between devices: 199 us -> 45.8 us
  matrix products: 114 us -> 0 us
  blocking collectives: 133 us -> 19.1 us
  other arithmetic: 106 us -> 10 us
  Pallas kernels: 0 us -> 51.8 us
    gather x98 -> x0, local copies, waits for them, and re-layouts: 232 us -> none  [the longest x12 114 us: layer_flat(): chosen = brick_cube[:, np.array(members)]]
    another operation x124 -> x0, local copies, waits for them, and re-layouts: 215 us -> none  [the longest x42 114 us: stream_flat(): return jnp.stack(outputs, axis=1).reshape(bricks, 19, BRICK * BRICK * BRICK)]
    reshape x102 -> x2, local copies, waits for them, and re-layouts: 189 us -> 0.11 us  [the longest x1 0.09 us: on_device(): (place + jnp.asarray(np.array(COLUMN_FACE, np.int32))[None, :]).reshape(-1)]
    ppermute x4, waiting for transfers between devices: 199 us -> 45.8 us  [the longest x2 44.6 us: swap_layers(): lax.ppermute(layers, AXES, odd_pairs)]
    slice x133 -> x1, local copies, waits for them, and re-layouts: 151 us -> 0.65 us  [on_device(): gathered = gather_sums(totals[0], totals[1], devices)]
    psum x2 -> x0, blocking collectives: 133 us -> none  [advance(): lax.psum((jnp.sum(jnp.where(fluid_sites, density, 0.0)), jnp.sum(fluid_si...]
    dot_general x6 -> x0, matrix products: 114 us -> none  [the longest x2 72.1 us: collide(): jnp.einsum('ij,bjs->bis', relaxation, states - balanced, precision=lax.Pr...]
    concatenate x84 -> x0, other arithmetic: 60.9 us -> none  [the longest x24 27.6 us: stream_flat(): shifted = jnp.roll(shifted, lane_step, axis=2)]
  transfers between devices with their start and end apart: 4 -> 5, of which waited for: 2 -> 3; matrix products, arithmetic and copies ran while one was open for 9% -> 6% of each run, Pallas kernels for 0% -> 0%
where the time goes in v1:
time: 169 us; the launch traced here: 168 us
  Pallas kernels  51.8 us (31%)
  waiting for transfers between devices  45.8 us (27%)
  local copies, waits for them, and re-layouts  21.5 us (13%)
  starting transfers between devices  19.9 us (12%)
  blocking collectives  19.1 us (11%)
  other arithmetic  10 us (6%)
    ppermute x2, waiting for transfers between devices, swap_layers(): lax.ppermute(layers, AXES, odd_pairs)  44.6 us
    pallas_call x2, Pallas kernels, collide_call(): pl.pallas_call(first_kernel if native else later_kernel, grid=(bricks //...  30.4 us
    all_to_all x1, blocking collectives, gather_sums(): return lax.all_to_all(rows, AXES, 0, 0, tiled=True)  19.1 us
    all_to_all x1, starting transfers between devices, gather_sums(): return lax.all_to_all(rows, AXES, 0, 0, tiled=True)  11.5 us
    pallas_call x1, Pallas kernels, arrive_out_call(): pl.pallas_call(arrive_out_kernel, grid=(bricks // GROUP,), in_specs=[pl.B...  10.8 us
    pallas_call x1, Pallas kernels, arrive_sum_call(): pl.pallas_call(arrive_sum_kernel, grid=(bricks // GROUP,), in_specs=[pl.B...  10.6 us
    unnamed x8, local copies, waits for them, and re-layouts  10 us
    pallas_call x1, local copies, waits for them, and re-layouts, arrive_out_call(): pl.pallas_call(arrive_out_kernel, grid=(bricks // GROUP,), in_specs=[pl.B...  9.98 us
  transfers between devices with their start and end apart: 5, of which 3 were waited for; matrix products, arithmetic and copies ran while one was open for 6% of the time, Pallas kernels for 0%

profile of v1, /device:TPU:1, one launch (start us, length us, event | category | flops | bytes accessed | tf_op | source)
XLA Modules:
  0.0 168.3 jit_solution(18128691066405218146)
XLA Ops:
  0.0 1.7 %convert_reduce_fusion = (f32[]{:T(128)}, pred[20,4096]{1,0:T(8,128)(4,1)S(1)}) fusion(s32[20,4096]{1,0:T(8,128)} %param.6), kind=kLoop, calls=%fused_computation.1 | loop fusion | flops 245759 | bytes 409604 | tf_op jit(solution)/shard_map/reduce_sum | solution.py:437
  1.7 5.6 %select_reduce_fusion = f32[]{:T(128)} fusion(f32[20,19,4096]{2,0,1:T(8,128)} %param.4, pred[20,4096]{1,0:T(8,128)(4,1)S(1)} %get-tuple-element.22), kind=kLoop, calls=%fused_computation | loop fusion | flops 3112959 | bytes 6307844 | tf_op jit(solution)/shard_map/reduce_sum | solution.py:436
  7.3 1.2 compare_select_fusion.1
  8.6 0.7 iota.21
  9.2 11.5 %all-to-all-start = ((f32[128,1,128]{2,1,0:T(1,128)}), f32[128,1,128]{2,1,0:T(1,128)S(1)}, u32[]{:S(2)}, u32[]{:S(2)}) async-start(f32[128,1,128]{2,1,0:T(1,128)} %iota.21), calls=%async_computation | async-start | bytes 131072 | tf_op jit(solution)/shard_map/all_to_all | solution.py:410
  20.7 0.0 copy-start
  20.7 9.9 %copy.7.pops = f32[20,19,4096]{2,1,0:T(8,128)} copy(f32[20,19,4096]{2,0,1:T(8,128)} %param.4) | data formatting | bytes 12451840 | tf_op args[0]
  30.6 0.0 copy-start.1
  30.6 0.0 copy-start.2
  30.6 0.0 copy-done
  30.6 0.1 copy.9
  30.8 0.0 all-to-all-done
  30.8 16.1 %collide_shift.2 = (f32[20,19,16,256]{3,2,1,0:T(8,128)}, f32[20,6,16,128]{3,2,1,0:T(8,128)S(1)}, f32[20,6,16,128]{3,2,1,0:T(8,128)S(1)}) custom-call(f32[128,128]{1,0:T(8,128)S(1)} %bitcast.19, f32[20,19,4096]{2,1,0:T(8,128)} %copy.7.pops, s32[20,16,256]{2,1,0:T(8,128)S(1)} %slice.8.kinds), custom_call_target="tpu_custom_call" | custom-call | tf_op jit(solution)/shard_map/collide_shift/pallas_call | solution.py:352
  46.9 4.7 %collective-permute-start.1 = (f32[120,16,128]{2,1,0:T(8,128)S(1)}, f32[120,16,128]{2,1,0:T(8,128)S(1)}, u32[]{:S(2)}, u32[]{:S(2)}) collective-permute-start(f32[120,16,128]{2,1,0:T(8,128)S(1)} %bitcast.11), channel_id=1, source_target_pairs={{1,2},{3,4},{5,6},{7,8},{9,10},{11,12},{13,14},{15,16},{17,18},{19... | collective-permute-start | bytes 2949128 | tf_op jit(solution)/shard_map/ppermute | solution.py:417
  51.6 0.1 collective-permute-start
  51.7 0.0 copy-done.1
  51.7 0.0 copy-done.2
  51.8 0.1 select_add_fusion
  51.8 0.1 reshape.30.index
  51.9 21.2 %collective-permute-done.1.odd = f32[120,16,128]{2,1,0:T(8,128)S(1)} collective-permute-done((f32[120,16,128]{2,1,0:T(8,128)S(1)}, f32[120,16,128]{2,1,0:T(8,128)S(1)}, u32[]{:S(2)}, u32[]{:S(2)}) %collective-permute-start.1) | collective-permute-done | bytes 983072 | tf_op jit(solution)/shard_map/ppermute | solution.py:417
  73.1 1.2 collective-permute-done.even
  74.4 10.6 %arrive_sum.1 = (f32[20,19,16,256]{3,2,1,0:T(8,128)}, f32[2,16,128]{2,1,0:T(8,128)S(1)}) custom-call(s32[360]{0:T(512)S(1)} %reshape.30.index, f32[20,19,16,256]{3,2,1,0:T(8,128)} %get-tuple-element.13.moved, s32[20,16,256]{2,1,0:T(8,128)S(1)} %slice.8.kinds, f32[120,16,128]{2,1,0:T(8,128)S(1)} %bitcast.13, f32[120,16,128]{2,1,0:T(8,128)S(1)} %bitcast.14, ...), custom_call_target="tpu_custom_call" | custom-call | tf_op jit(solution)/shard_map/arrive_sum/pallas_call | solution.py:375
  84.9 0.1 reduce_sum.29
  85.0 0.7 fusion
  85.7 1.3 compare_select_fusion
  87.0 19.1 %all_to_all.16 = f32[128,1,128]{2,1,0:T(1,128)S(1)} all-to-all(f32[128,1,128]{2,1,0:T(1,128)S(1)} %iota.22), channel_id=1, replica_groups=mesh['seg'=32,'sub'=4] {'seg','sub'}, dimensions={0} | all-to-all | bytes 131072 | tf_op jit(solution)/shard_map/all_to_all | solution.py:410
  106.2 14.4 %collide_shift.3 = (f32[20,19,16,256]{3,2,1,0:T(8,128)}, f32[20,6,16,128]{3,2,1,0:T(8,128)S(1)}, f32[20,6,16,128]{3,2,1,0:T(8,128)S(1)}) custom-call(f32[128,128]{1,0:T(8,128)S(1)} %bitcast.20, f32[20,19,16,256]{3,2,1,0:T(8,128)} %get-tuple-element.17.pops, s32[20,16,256]{2,1,0:T(8,128)S(1)} %slice.8.kinds), custom_call_target="tpu_custom_call" | custom-call | tf_op jit(solution)/shard_map/collide_shift/pallas_call | solution.py:352
  120.6 3.3 %collective-permute-start.3 = (f32[120,16,128]{2,1,0:T(8,128)S(1)}, f32[120,16,128]{2,1,0:T(8,128)S(1)}, u32[]{:S(2)}, u32[]{:S(2)}) collective-permute-start(f32[120,16,128]{2,1,0:T(8,128)S(1)} %bitcast.15), channel_id=1, source_target_pairs={{1,2},{3,4},{5,6},{7,8},{9,10},{11,12},{13,14},{15,16},{17,18},{19... | collective-permute-start | bytes 2949128 | tf_op jit(solution)/shard_map/ppermute | solution.py:417
  123.9 0.3 collective-permute-start.2
  124.2 23.4 %collective-permute-done.3.odd = f32[120,16,128]{2,1,0:T(8,128)S(1)} collective-permute-done((f32[120,16,128]{2,1,0:T(8,128)S(1)}, f32[120,16,128]{2,1,0:T(8,128)S(1)}, u32[]{:S(2)}, u32[]{:S(2)}) %collective-permute-start.3) | collective-permute-done | bytes 983072 | tf_op jit(solution)/shard_map/ppermute | solution.py:417
  147.6 0.0 collective-permute-done.2.even
  147.6 10.8 %arrive_out.1 = f32[20,19,4096]{2,1,0:T(8,128)} custom-call(s32[360]{0:T(512)S(1)} %reshape.30.index, f32[20,19,16,256]{3,2,1,0:T(8,128)} %get-tuple-element.18.moved, f32[120,16,128]{2,1,0:T(8,128)S(1)} %bitcast.17, f32[120,16,128]{2,1,0:T(8,128)S(1)} %bitcast.18, f32[120,16,128]{2,1,0:T(8,128)S(1)} %collective-permute-done.2.even, ...), custom_call_target="tpu_custom_call" | custom-call | tf_op jit(solution)/shard_map/arrive_out/pallas_call | solution.py:393
  158.3 10.0 %copy.8 = f32[20,19,4096]{2,0,1:T(8,128)} copy(f32[20,19,4096]{2,1,0:T(8,128)} %arrive_out.1) | data formatting | bytes 12451840 | tf_op jit(solution)/shard_map/arrive_out/pallas_call | solution.py:393
  (3 shorter events, 0.1 us)
Async XLA Ops:
  9.2 21.6 %all-to-all-start = ((f32[128,1,128]{2,1,0:T(1,128)}), f32[128,1,128]{2,1,0:T(1,128)S(1)}, u32[]{:S(2)}, u32[]{:S(2)}) async-start(f32[128,1,128]{2,1,0:T(1,128)} %iota.21), calls=%async_computation | async-start | bytes 131072 | tf_op jit(solution)/shard_map/all_to_all | solution.py:410
  20.7 9.9 %copy-start = (s32[20,4096]{1,0:T(8,128)S(1)}, s32[20,4096]{1,0:T(8,128)}, u32[]{:S(2)}) copy-start(s32[20,4096]{1,0:T(8,128)} %param.6) | copy-start | bytes 983044
  30.6 21.1 %copy-start.1 = (s32[20,18]{1,0:T(8,128)S(1)}, s32[20,18]{1,0:T(8,128)}, u32[]{:S(2)}) copy-start(s32[20,18]{1,0:T(8,128)} %param.5) | copy-start | bytes 4324
  30.6 21.1 %copy-start.2 = (s32[18]{0:T(128)S(1)}, s32[18]{0:T(128)}, u32[]{:S(2)}) copy-start(s32[18]{0:T(128)} %constant.46.clone) | copy-start | bytes 220
  46.9 26.3 %collective-permute-start.1 = (f32[120,16,128]{2,1,0:T(8,128)S(1)}, f32[120,16,128]{2,1,0:T(8,128)S(1)}, u32[]{:S(2)}, u32[]{:S(2)}) collective-permute-start(f32[120,16,128]{2,1,0:T(8,128)S(1)} %bitcast.11), channel_id=1, source_target_pairs={{1,2},{3,4},{5,6},{7,8},{9,10},{11,12},{13,14},{15,16},{17,18},{19... | collective-permute-start | bytes 2949128 | tf_op jit(solution)/shard_map/ppermute | solution.py:417
  51.6 22.8 %collective-permute-start = (f32[120,16,128]{2,1,0:T(8,128)S(1)}, f32[120,16,128]{2,1,0:T(8,128)}, u32[]{:S(2)}, u32[]{:S(2)}) collective-permute-start(f32[120,16,128]{2,1,0:T(8,128)S(1)} %bitcast.12), channel_id=1, source_target_pairs={{0,1},{1,0},{2,3},{3,2},{4,5},{5,4},{6,7},{7,6},{8,9},{9,8},{10,11... | collective-permute-start | bytes 2949128 | tf_op jit(solution)/shard_map/ppermute | solution.py:417
  120.6 27.0 %collective-permute-start.3 = (f32[120,16,128]{2,1,0:T(8,128)S(1)}, f32[120,16,128]{2,1,0:T(8,128)S(1)}, u32[]{:S(2)}, u32[]{:S(2)}) collective-permute-start(f32[120,16,128]{2,1,0:T(8,128)S(1)} %bitcast.15), channel_id=1, source_target_pairs={{1,2},{3,4},{5,6},{7,8},{9,10},{11,12},{13,14},{15,16},{17,18},{19... | collective-permute-start | bytes 2949128 | tf_op jit(solution)/shard_map/ppermute | solution.py:417
  123.9 23.7 %collective-permute-start.2 = (f32[120,16,128]{2,1,0:T(8,128)S(1)}, f32[120,16,128]{2,1,0:T(8,128)S(1)}, u32[]{:S(2)}, u32[]{:S(2)}) collective-permute-start(f32[120,16,128]{2,1,0:T(8,128)S(1)} %bitcast.16), channel_id=1, source_target_pairs={{0,1},{1,0},{2,3},{3,2},{4,5},{5,4},{6,7},{7,6},{8,9},{9,8},{10,11... | collective-permute-start | bytes 2949128 | tf_op jit(solution)/shard_map/ppermute | solution.py:417

commit v2 on v1

v2 whole, which is shorter than its diff:
```python
import functools

import jax
import jax.numpy as jnp
import numpy as np
from jax import lax
from jax.experimental import pallas as pl
from jax.experimental.pallas import tpu as pltpu
from jax.sharding import PartitionSpec as P

BRICK = 16
PLANE = 256
SITES = 4096
GROUP = 8
CHUNKS = 32
AXES = ("seg", "sub")
INLET = 0.1

SPEEDS = [
    (0, 0, 0),
    (1, 0, 0), (-1, 0, 0), (0, 1, 0), (0, -1, 0), (0, 0, 1), (0, 0, -1),
    (1, 1, 0), (-1, -1, 0), (1, -1, 0), (-1, 1, 0),
    (1, 0, 1), (-1, 0, -1), (1, 0, -1), (-1, 0, 1),
    (0, 1, 1), (0, -1, -1), (0, 1, -1), (0, -1, 1),
]
OPP = [0, 2, 1, 4, 3, 6, 5, 8, 7, 10, 9, 12, 11, 14, 13, 16, 15, 18, 17]


def face_of(speed, dim):
    return 2 * dim + (0 if speed[dim] > 0 else 1)


MEMBERS = [[i for i in range(19) if any(face_of(SPEEDS[i], d) == f and SPEEDS[i][d] for d in range(3))]
           for f in range(6)]
COLUMN_FACE = []
for _d in range(18):
    _m = SPEEDS[OPP[_d + 1]]
    _lead = [k for k in range(3) if _m[k]][0]
    COLUMN_FACE.append(face_of(_m, _lead))


def iota(shape, dim):
    return lax.broadcasted_iota(jnp.int32, shape, dim)


def roll(x, shift, axis):
    shift = shift % x.shape[axis]
    return x if shift == 0 else pltpu.roll(x, shift, axis)


def collide(f, kind):
    fluid = kind == 0
    wall = kind == 1
    inlet = kind == 2
    outlet = kind == 3
    even = [f[2 * k + 1] + f[2 * k + 2] for k in range(9)]
    odd = [f[2 * k + 1] - f[2 * k + 2] for k in range(9)]
    density = f[0] + ((even[0] + even[1]) + (even[2] + even[3])) + (
        (even[4] + even[5]) + (even[6] + even[7])) + even[8]
    inverse = 1.0 / density
    ux = (odd[0] + odd[3] + odd[4] + odd[5] + odd[6]) * inverse
    uy = (odd[1] + odd[3] - odd[4] + odd[7] + odd[8]) * inverse
    uz = (odd[2] + odd[5] - odd[6] + odd[7] - odd[8]) * inverse
    ux = jnp.where(inlet, INLET, ux)
    uy = jnp.where(inlet, 0.0, uy)
    uz = jnp.where(inlet, 0.0, uz)
    rho = jnp.where(outlet, 1.0, density)
    base = 1.0 - 1.5 * (ux * ux + uy * uy + uz * uz)
    along = [ux, uy, uz, ux + uy, ux - uy, ux + uz, ux - uz, uy + uz, uy - uz]
    keep_even = jnp.where(fluid, -0.3, jnp.where(wall, 0.5, 0.0))
    take_even = jnp.where(fluid, 0.8, jnp.where(wall, 0.0, 0.5))
    keep_odd = jnp.where(fluid, -0.1, jnp.where(wall, -0.5, 0.0))
    take_odd = jnp.where(fluid, 0.6, jnp.where(wall, 0.0, 0.5))
    fourth = jnp.where(fluid, 0.2 / 12.0, 0.0)
    rho9 = rho * (1.0 / 9.0)
    rho18 = rho * (1.0 / 18.0)
    eq_even = []
    for k in range(9):
        scale = rho9 if k < 3 else rho18
        eq_even.append(scale * (base + 4.5 * along[k] * along[k]))
    eq_rest = (rho * (1.0 / 3.0)) * base
    g_rest = f[0] - eq_rest
    g = [even[k] - eq_even[k] for k in range(9)]
    four = 4.0 * g_rest
    gx, gy, gz = 2.0 * g[0], 2.0 * g[1], 2.0 * g[2]
    ta = four - gx - gy + (g[3] + g[4])
    tb = four - gx - gz + (g[5] + g[6])
    tc = four - gy - gz + (g[7] + g[8])
    shared = (2.0 / 7.0) * (ta + tb + tc)
    ka = (ta - shared) * fourth
    kb = (tb - shared) * fourth
    kc = (tc - shared) * fourth
    kab, kac, kbc = ka + kb, ka + kc, kb + kc
    modes = [-2.0 * kab, -2.0 * kac, -2.0 * kbc, ka, ka, kb, kb, kc, kc]
    odd9 = rho * take_odd * (1.0 / 3.0)
    odd18 = rho * take_odd * (1.0 / 6.0)
    out = [2.0 * (keep_even * f[0] + take_even * eq_rest) + 4.0 * (kab + kc)]
    for k in range(9):
        half_even = keep_even * even[k] + take_even * eq_even[k] + modes[k]
        half_odd = keep_odd * odd[k] + (odd9 if k < 3 else odd18) * along[k]
        out.append(half_even + half_odd)
        out.append(half_even - half_odd)
    return out, density


def side(heading):
    return (15, 0) if heading > 0 else (0, 15)


def slot_of(member, dim):
    return MEMBERS[face_of(SPEEDS[member], dim)].index(member)


def toward(member, dim):
    return 2 * dim + (1 if SPEEDS[member][dim] > 0 else 0)


def pack(value, layers, table, step):
    lane = iota((GROUP, 128), 1)
    for face in range(2):
        leave = 15 if face % 2 == 0 else 0
        for slot, member in enumerate(MEMBERS[face]):
            for h in range(2):
                row = (8 * h + slot) * 8
                layers[face, row:row + 8, :] = value(member, 2 * leave + h)

    def line(x, carry):
        rows = pl.ds(pl.multiple_of(8 * x, 8), 8)
        for face in range(2, 6):
            leave = 15 if face % 2 == 0 else 0
            packed = None
            for slot, member in enumerate(MEMBERS[face]):
                if face < 4:
                    piece = value(member, 2 * x + leave // 8)
                    piece = roll(piece, 16 * slot - 16 * (leave % 8), 1)
                    packed = piece if packed is None else jnp.where((lane >> 4) == slot, piece, packed)
                else:
                    for h in range(2):
                        piece = roll(value(member, 2 * x + h), 8 * h + slot - leave, 1)
                        packed = (piece if packed is None
                                  else jnp.where((lane & 15) == 8 * h + slot, piece, packed))
            layers[face, rows, :] = packed
        return carry

    lax.fori_loop(0, BRICK, line, 0)
    for face in range(6):
        for j in range(GROUP):
            table[(step * GROUP + j) * 6 + face] = layers[face, pl.ds(j, BRICK, stride=8), :]


def gather(index, step, table, marks, mean, arriving):
    wide = jnp.concatenate([mean, mean], axis=0)

    def brick(j, carry):
        base = (step * GROUP + j) * 18
        for column in range(18):
            at = index[base + column]
            block = table[at]
            arriving[column, pl.ds(j, BRICK, stride=8), :] = jnp.where(
                marks[at] != 0.0, block * wide, block)
        return carry

    lax.fori_loop(0, GROUP, brick, 0)


def stream(posted, kinds, absent, arriving, mean, put):
    lane = iota((GROUP, 128), 1)

    def scale(chunk):
        lanes = pl.ds(pl.multiple_of(128 * chunk, 128), 128)
        return jnp.where(kinds[:, lanes] == 3, mean, 1.0)

    def line(x, carry):
        before = (x + 15) & 15
        after = (x + 1) & 15
        place = {0: x, 1: before, -1: after}
        scales = {cx: (scale(2 * place[cx]), scale(2 * place[cx] + 1)) for cx in (0, 1, -1)}

        def load(member, cx, h):
            return posted[0, member, 2 * place[cx] + h] * scales[cx][h]

        for member in range(19):
            cx, cy, cz = SPEEDS[member]
            parts = [load(member, cx, h) for h in range(2)]
            mirror = [None, None]
            if cy or cz:
                mirror = [load(OPP[member], 0, h) for h in range(2)]
            if cy:
                first, second = roll(parts[0], 16 * cy, 1), roll(parts[1], 16 * cy, 1)
                carried = lane < 16 if cy > 0 else lane >= 112
                parts = [jnp.where(carried, second, first), jnp.where(carried, first, second)]
            if cz:
                parts = [roll(part, cz, 1) for part in parts]
            rows = pl.ds(pl.multiple_of(8 * place[cx], 8), 8)
            if cy:
                leave, enter = side(cy)
                column = toward(member, 1)
                half = enter // 8
                shift = 16 * (enter % 8) - 16 * slot_of(member, 1)
                here = (lane >> 4) == enter % 8
                new = roll(arriving[column, rows, :], shift + cz, 1)
                new = jnp.where(absent[column] != 0, mirror[half], new)
                parts[half] = jnp.where(here, new, parts[half])
            if cz:
                leave, enter = side(cz)
                column = toward(member, 2)
                slot = slot_of(member, 2)
                gone = absent[column] != 0
                here = (lane & 15) == enter
                block = arriving[column, rows, :]
                for h in range(2):
                    new = roll(block, 16 * cy + enter - slot - 8 * h, 1)
                    if cy and h == (1 if cy > 0 else 0):
                        other = roll(block, 16 * cy + enter - slot - 8 * (1 - h), 1)
                        new = jnp.where(lane < 16 if cy > 0 else lane >= 112, other, new)
                    new = jnp.where(gone, mirror[h], new)
                    parts[h] = jnp.where(here, new, parts[h])
            if cy and cz:
                leave, enter = side(cy)
                column = OPP[member] - 1
                half = enter // 8
                shift = 16 * (enter % 8) - 16 * slot_of(member, 1)
                corner = ((lane >> 4) == enter % 8) & ((lane & 15) == side(cz)[1])
                new = roll(arriving[column, rows, :], shift - 15 * cz, 1)
                new = jnp.where(absent[column] != 0, mirror[half], new)
                parts[half] = jnp.where(corner, new, parts[half])
            for h in range(2):
                put(member, 2 * x + h, parts[h])
        return carry

    lax.fori_loop(0, BRICK, line, 0)

    for member in range(19):
        cx, cy, cz = SPEEDS[member]
        if not cx:
            continue
        leave, enter = side(cx)
        slot = slot_of(member, 0)
        mirror = [posted[0, OPP[member], 2 * enter + h] * scale(2 * enter + h) for h in range(2)]

        def plane(column):
            parts = []
            for h in range(2):
                row = (8 * h + slot) * 8
                parts.append(arriving[column, row:row + 8, :])
            if cy:
                first, second = roll(parts[0], 16 * cy, 1), roll(parts[1], 16 * cy, 1)
                carried = lane < 16 if cy > 0 else lane >= 112
                parts = [jnp.where(carried, second, first), jnp.where(carried, first, second)]
            return [jnp.where(absent[column] != 0, mirror[h], parts[h]) for h in range(2)]

        def edge_plane(column):
            if cy:
                return plane(column)
            parts = []
            for h in range(2):
                row = (8 * h + slot) * 8
                parts.append(roll(arriving[column, row:row + 8, :], -15 * cz, 1))
            return [jnp.where(absent[column] != 0, mirror[h], parts[h]) for h in range(2)]

        parts = plane(toward(member, 0))
        if cz:
            column = toward(member, 0)
            parts = []
            for h in range(2):
                row = (8 * h + slot) * 8
                new = roll(arriving[column, row:row + 8, :], cz, 1)
                parts.append(jnp.where(absent[column] != 0, mirror[h], new))
        if cy or cz:
            edges = edge_plane(OPP[member] - 1)
            for h in range(2):
                if cy:
                    if side(cy)[1] // 8 != h:
                        continue
                    corner = (lane >> 4) == side(cy)[1] % 8
                else:
                    corner = (lane & 15) == side(cz)[1]
                parts[h] = jnp.where(corner, edges[h], parts[h])
        for h in range(2):
            put(member, 2 * enter + h, parts[h])


def mean_of(gathered):
    total = jnp.sum(gathered[...], axis=0, keepdims=True)
    ratio = total / pltpu.roll(total, 64, 1)
    return jnp.broadcast_to(ratio[:, 0:1], (GROUP, 128))


def collide_all(load, kinds, posted, sums, rows_out, step, bricks):
    real = iota((GROUP, 128), 0) + step * GROUP < bricks

    def chunk(c, carry):
        lanes = pl.ds(pl.multiple_of(128 * c, 128), 128)
        kind = kinds[:, lanes]
        out, density = collide([load(i, c) for i in range(19)], kind)
        for i in range(19):
            posted[0, i, c] = out[i]
        counted = real & (kind != 1)
        return (carry[0] + jnp.where(counted, density, 0.0),
                carry[1] + jnp.where(counted, 1.0, 0.0))

    zero = jnp.zeros((GROUP, 128), F32)
    total, count = lax.fori_loop(0, CHUNKS, chunk, (zero, zero))

    @pl.when(step == 0)
    def _():
        sums[0] = total
        sums[1] = count

    @pl.when(step > 0)
    def _():
        sums[0] += total
        sums[1] += count

    @pl.when(step == pl.num_programs(0) - 1)
    def _():
        left = iota(rows_out.shape, 1) < 64
        rows_out[...] = jnp.where(left, jnp.sum(sums[0]), jnp.sum(sums[1]))


def first_kernel(bricks, pops, kinds, posted, faces, marks, rows_out, layers, sums):
    step = pl.program_id(0)

    def load(i, c):
        return pops[i, :, pl.ds(pl.multiple_of(128 * c, 128), 128)]

    collide_all(load, kinds, posted, sums, rows_out, step, bricks)
    pack(lambda m, c: posted[0, m, c], layers, faces, step)

    def mark(m, c):
        lanes = pl.ds(pl.multiple_of(128 * c, 128), 128)
        return jnp.where(kinds[:, lanes] == 3, 1.0, 0.0)

    pack(mark, layers, marks, step)


def fill(pieces, table, sems):
    copies = []
    start = 0
    for k, piece in enumerate(pieces):
        count = piece.shape[0]
        copies.append(pltpu.make_async_copy(piece, table.at[pl.ds(start, count)], sems.at[k]))
        start += count
    return copies


def take_tables(refs, table, marks, sems):
    copies = fill(refs[:3], table, sems.at[0]) + fill(refs[3:], marks, sems.at[1])
    for copy in copies:
        copy.start()
    for copy in copies:
        copy.wait()


def middle_kernel(bricks, index, gathered, before, kinds, absent, own, even, odd, own_m, even_m, odd_m,
                  posted, faces, rows_out, table, marks, arriving, pops, layers, sums, sems):
    step = pl.program_id(0)

    @pl.when(step == 0)
    def _():
        take_tables((own, even, odd, own_m, even_m, odd_m), table, marks, sems)

    mean = mean_of(gathered)
    gather(index, step, table, marks, mean, arriving)

    def put(member, chunk, value):
        pops[member, chunk] = value

    stream(before, kinds, absent, arriving, mean, put)
    collide_all(lambda i, c: pops[i, c], kinds, posted, sums, rows_out, step, bricks)
    pack(lambda m, c: posted[0, m, c], layers, faces, step)


def last_kernel(index, gathered, before, kinds, absent, own, even, odd, own_m, even_m, odd_m,
                out, table, marks, arriving, sems):
    step = pl.program_id(0)

    @pl.when(step == 0)
    def _():
        take_tables((own, even, odd, own_m, even_m, odd_m), table, marks, sems)

    mean = mean_of(gathered)
    gather(index, step, table, marks, mean, arriving)

    def put(member, chunk, value):
        start = 128 * chunk
        if not isinstance(start, int):
            start = pl.multiple_of(start, 128)
        out[member, :, pl.ds(start, 128)] = value

    stream(before, kinds, absent, arriving, mean, put)


F32 = jnp.float32
BLOCK = (BRICK, 128)
POSTED = (19, CHUNKS, GROUP, 128)


def params():
    return pltpu.CompilerParams(
        dimension_semantics=("arbitrary",), vmem_limit_bytes=52 * 1024 * 1024)


def whole(*shape):
    return pl.BlockSpec(shape, lambda i: (0,) * len(shape))


SPEC_POPS = pl.BlockSpec((19, GROUP, SITES), lambda i: (0, i, 0))
SPEC_KINDS = pl.BlockSpec((GROUP, SITES), lambda i: (i, 0))
SPEC_POSTED = pl.BlockSpec((1,) + POSTED, lambda i: (i, 0, 0, 0, 0))
SPEC_ABSENT = pl.BlockSpec((18, GROUP, 128), lambda i: (0, i, 0))
SPEC_SMEM = pl.BlockSpec(memory_space=pltpu.SMEM)
SPEC_ANY = pl.BlockSpec(memory_space=pl.ANY)


def shape_of(*shape):
    return jax.ShapeDtypeStruct(shape, F32)


def first_call(pops, kinds, groups, devices):
    blocks = groups * GROUP * 6
    return pl.pallas_call(
        functools.partial(first_kernel, pops.shape[1]),
        grid=(groups,),
        in_specs=[SPEC_POPS, SPEC_KINDS],
        out_specs=[SPEC_POSTED, whole(blocks, *BLOCK), whole(blocks, *BLOCK), whole(devices, 128)],
        out_shape=[shape_of(groups, *POSTED), shape_of(blocks, *BLOCK), shape_of(blocks, *BLOCK),
                   shape_of(devices, 128)],
        scratch_shapes=[pltpu.VMEM((6, 128, 128), F32), pltpu.VMEM((2, GROUP, 128), F32)],
        compiler_params=params(),
        name="first_collide",
    )(pops, kinds)


def middle_call(bricks, index, gathered, before, kinds, absent, tables, groups, devices):
    blocks = groups * GROUP * 6
    rows = sum(t.shape[0] for t in tables[:3])
    return pl.pallas_call(
        functools.partial(middle_kernel, bricks),
        grid=(groups,),
        in_specs=[SPEC_SMEM, whole(devices, 128), SPEC_POSTED, SPEC_KINDS, SPEC_ABSENT] + [SPEC_ANY] * 6,
        out_specs=[SPEC_POSTED, whole(blocks, *BLOCK), whole(devices, 128)],
        out_shape=[shape_of(groups, *POSTED), shape_of(blocks, *BLOCK), shape_of(devices, 128)],
        scratch_shapes=[pltpu.VMEM((rows,) + BLOCK, F32), pltpu.VMEM((rows,) + BLOCK, F32),
                        pltpu.VMEM((18, 128, 128), F32), pltpu.VMEM(POSTED, F32),
                        pltpu.VMEM((6, 128, 128), F32), pltpu.VMEM((2, GROUP, 128), F32),
                        pltpu.SemaphoreType.DMA((2, 3))],
        compiler_params=params(),
        name="arrive_collide",
    )(index, gathered, before, kinds, absent, *tables)


def last_call(bricks, index, gathered, before, kinds, absent, tables, groups, devices):
    rows = sum(t.shape[0] for t in tables[:3])
    return pl.pallas_call(
        last_kernel,
        grid=(groups,),
        in_specs=[SPEC_SMEM, whole(devices, 128), SPEC_POSTED, SPEC_KINDS, SPEC_ABSENT] + [SPEC_ANY] * 6,
        out_specs=SPEC_POPS,
        out_shape=shape_of(19, bricks, SITES),
        scratch_shapes=[pltpu.VMEM((rows,) + BLOCK, F32), pltpu.VMEM((rows,) + BLOCK, F32),
                        pltpu.VMEM((18, 128, 128), F32), pltpu.SemaphoreType.DMA((2, 3))],
        compiler_params=params(),
        name="arrive_out",
    )(index, gathered, before, kinds, absent, *tables)


def share_sums(rows):
    return lax.all_to_all(rows, AXES, 0, 0, tiled=True)


def swap(layers, devices):
    even_pairs = [(i, i ^ 1) for i in range(devices)]
    odd_pairs = [(i, i + 1) for i in range(1, devices - 1, 2)]
    odd_pairs = odd_pairs + [(b, a) for a, b in odd_pairs]
    return (layers, lax.ppermute(layers, AXES, even_pairs), lax.ppermute(layers, AXES, odd_pairs))


def on_device(devices, populations, neighbours, site_flags):
    bricks = populations.shape[0]
    groups = -(-bricks // GROUP)
    padded = groups * GROUP
    blocks = padded * 6
    me = lax.axis_index(AXES)
    local = neighbours - me * bricks
    parity = me % 2
    after = jnp.where(parity == 0, blocks, 2 * blocks)
    before = jnp.where(parity == 0, 2 * blocks, blocks)
    place = jnp.where(local < 0, before + (local + bricks) * 6,
                      jnp.where(local >= bricks, after + (local - bricks) * 6, local * 6))
    index = jnp.where(neighbours < 0, 0, place + jnp.asarray(np.array(COLUMN_FACE, np.int32))[None, :])
    index = jnp.pad(index, ((0, padded - bricks), (0, 0))).reshape(-1)
    absent = jnp.pad((neighbours < 0).astype(jnp.int32), ((0, padded - bricks), (0, 0)))
    absent = jnp.broadcast_to(absent.T[:, :, None], (18, padded, 128))

    posted, faces, marks, rows = first_call(jnp.transpose(populations, (1, 0, 2)), site_flags, groups, devices)
    gathered = share_sums(rows)
    mark_tables = swap(marks, devices)
    tables = swap(faces, devices) + mark_tables
    posted, faces, rows = middle_call(
        bricks, index, gathered, posted, site_flags, absent, tables, groups, devices)
    gathered = share_sums(rows)
    tables = swap(faces, devices) + mark_tables
    out = last_call(bricks, index, gathered, posted, site_flags, absent, tables, groups, devices)
    return jnp.transpose(out, (1, 0, 2))


def solution(mesh):
    devices = mesh.shape["seg"] * mesh.shape["sub"]
    in_specs = (P(AXES, None, None), P(AXES, None), P(AXES, None))
    return jax.shard_map(
        functools.partial(on_device, devices), mesh=mesh, in_specs=in_specs,
        out_specs=P(AXES, None, None), check_vma=False)
```

time: 169 us -> 164 us (0.970)
  local copies, waits for them, and re-layouts: 21.5 us -> 3.65 us
  blocking collectives: 19.1 us -> 29.8 us
  other arithmetic: 10 us -> 0.03 us
  Pallas kernels: 51.8 us -> 60.3 us
  starting transfers between devices: 19.9 us -> 26.9 us
  waiting for transfers between devices: 45.8 us -> 43.4 us
    ppermute x4 -> x6, waiting for transfers between devices: 45.8 us -> 0.02 us  [the longest x3 0.01 us: swap(): lax.ppermute(layers, AXES, odd_pairs)]
    all_to_all x1, waiting for transfers between devices: 0.01 us -> 43.4 us  [share_sums(): return lax.all_to_all(rows, AXES, 0, 0, tiled=True)]
    all_to_all x1, blocking collectives: 19.1 us -> 29.8 us  [share_sums(): return lax.all_to_all(rows, AXES, 0, 0, tiled=True)]
    pallas_call x1 -> x0, local copies, waits for them, and re-layouts: 9.98 us -> none  [arrive_out_call(): pl.pallas_call(arrive_out_kernel, grid=(bricks // GROUP,), in_specs=[pl.B...]
    pallas_call x4 -> x3, Pallas kernels: 51.8 us -> 60.3 us  [the longest x1 26 us: middle_call(): pl.pallas_call(functools.partial(middle_kernel, bricks), grid=(groups,),...]
    reduce_sum x3 -> x0, other arithmetic: 7.44 us -> none  [the longest x1 5.64 us: on_device(): summed = jnp.sum(jnp.where(open_site, populations, 0.0))]
    ppermute x4 -> x6, starting transfers between devices: 8.44 us -> 15.3 us  [the longest x3 14 us: swap(): lax.ppermute(layers, AXES, odd_pairs)]
    unnamed x8 -> x16, local copies, waits for them, and re-layouts: 10 us -> 3.35 us
  transfers between devices with their start and end apart: 5 -> 7, of which waited for: 3 -> 1; matrix products, arithmetic and copies ran while one was open for 6% -> 0% of each run, Pallas kernels for 0% -> 0%
where the time goes in v2:
time: 164 us
  Pallas kernels  60.3 us (37%)
  waiting for transfers between devices  43.4 us (26%)
  blocking collectives  29.8 us (18%)
  starting transfers between devices  26.9 us (16%)
  local copies, waits for them, and re-layouts  3.65 us (2%)
    all_to_all x1, waiting for transfers between devices, share_sums(): return lax.all_to_all(rows, AXES, 0, 0, tiled=True)  43.4 us
    all_to_all x1, blocking collectives, share_sums(): return lax.all_to_all(rows, AXES, 0, 0, tiled=True)  29.8 us
    pallas_call x1, Pallas kernels, middle_call(): pl.pallas_call(functools.partial(middle_kernel, bricks), grid=(groups,),...  26 us
    pallas_call x1, Pallas kernels, first_call(): pl.pallas_call(functools.partial(first_kernel, pops.shape[1]), grid=(grou...  18.5 us
    pallas_call x1, Pallas kernels, last_call(): pl.pallas_call(last_kernel, grid=(groups,), in_specs=[SPEC_SMEM, whole(de...  15.8 us
    ppermute x3, starting transfers between devices, swap(): lax.ppermute(layers, AXES, odd_pairs)  14 us
    all_to_all x1, starting transfers between devices, share_sums(): return lax.all_to_all(rows, AXES, 0, 0, tiled=True)  11.6 us
    unnamed x16, local copies, waits for them, and re-layouts  3.35 us
  transfers between devices with their start and end apart: 7, of which 1 were waited for; matrix products, arithmetic and copies ran while one was open for 0% of the time, Pallas kernels for 0%

profile of v2, /device:TPU:1, one launch (start us, length us, event | category | flops | bytes accessed | tf_op | source)
XLA Modules:
  0.0 164.2 jit_solution(2530995360928672936)
XLA Ops:
  0.0 0.0 copy-start
  0.0 1.0 copy-done
  1.0 0.0 copy-start.6
  1.0 0.0 copy-start.7
  1.0 0.0 copy-start.1
  1.0 18.5 %first_collide.1 = (f32[3,19,32,8,128]{4,3,2,1,0:T(8,128)}, f32[144,16,128]{2,1,0:T(8,128)S(1)}, f32[144,16,128]{2,1,0:T(8,128)}, f32[128,128]{1,0:T(8,128)}) custom-call(f32[19,20,4096]{2,1,0:T(8,128)} %bitcast.15, s32[20,4096]{1,0:T(8,128)S(1)} %copy-done), custom_call_target="tpu_custom_call" | custom-call | tf_op jit(solution)/shard_map/first_collide/pallas_call | solution.py:422
  19.5 0.0 copy-start.2
  19.5 5.8 %collective-permute-start.1 = (f32[144,16,128]{2,1,0:T(8,128)S(1)}, f32[144,16,128]{2,1,0:T(8,128)}, u32[]{:S(2)}, u32[]{:S(2)}) collective-permute-start(f32[144,16,128]{2,1,0:T(8,128)S(1)} %get-tuple-element.14.own), channel_id=1, source_target_pairs={{1,2},{3,4},{5,6},{7,8},{9,10},{11,12},{13,14},{15,16},{17,18},{19... | collective-permute-start | bytes 3538952 | tf_op jit(solution)/shard_map/ppermute | solution.py:476
  25.3 0.1 collective-permute-start
  25.4 3.2 %collective-permute-start.3 = (f32[144,16,128]{2,1,0:T(8,128)}, f32[144,16,128]{2,1,0:T(8,128)S(1)}, u32[]{:S(2)}, u32[]{:S(2)}) collective-permute-start(f32[144,16,128]{2,1,0:T(8,128)} %get-tuple-element.15.own_m), channel_id=1, source_target_pairs={{1,2},{3,4},{5,6},{7,8},{9,10},{11,12},{13,14},{15,16},{17,18},{19... | collective-permute-start | bytes 3538952 | tf_op jit(solution)/shard_map/ppermute | solution.py:476
  28.6 1.1 collective-permute-start.2
  29.8 11.6 %all-to-all-start = ((f32[128,1,128]{2,1,0:T(1,128)}), f32[128,1,128]{2,1,0:T(1,128)S(1)}, u32[]{:S(2)}, u32[]{:S(2)}) async-start(f32[128,1,128]{2,1,0:T(1,128)} %bitcast.2), calls=%async_computation | async-start | bytes 131072 | tf_op jit(solution)/shard_map/all_to_all | solution.py:469
  41.3 0.0 copy-done.6
  41.4 0.0 copy-done.7
  41.4 0.1 copy.7
  41.5 0.1 reshape.9.index
  41.6 43.4 %all-to-all-done = f32[128,1,128]{2,1,0:T(1,128)S(1)} async-done(((f32[128,1,128]{2,1,0:T(1,128)}), f32[128,1,128]{2,1,0:T(1,128)S(1)}, u32[]{:S(2)}, u32[]{:S(2)}) %all-to-all-start) | async-done | bytes 65568 | tf_op jit(solution)/shard_map/all_to_all | solution.py:469
  85.0 0.0 collective-permute-done.1.odd
  85.0 0.0 collective-permute-done.even
  85.0 0.0 collective-permute-done.3.odd_m
  85.0 0.0 copy-start.3
  85.0 0.0 collective-permute-done.2.even_m
  85.0 0.1 broadcast_in_dim.4.absent
  85.2 0.0 copy-done.2
  85.2 0.9 copy-done.3
  86.0 0.0 copy-done.1
  86.0 26.0 %arrive_collide.1 = (f32[3,19,32,8,128]{4,3,2,1,0:T(8,128)}, f32[144,16,128]{2,1,0:T(8,128)S(1)}, f32[128,128]{1,0:T(8,128)S(1)}) custom-call(s32[432]{0:T(512)S(1)} %reshape.9.index, f32[128,128]{1,0:T(8,128)S(1)} %bitcast.12, f32[3,19,32,8,128]{4,3,2,1,0:T(8,128)} %get-tuple-element.13.before, s32[20,4096]{1,0:T(8,128)S(1)} %copy-done.1, ...), custom_call_target="tpu_custom_call" | custom-call | tf_op jit(solution)/shard_map/arrive_collide/pallas_call | solution.py:438
  112.1 5.0 %collective-permute-start.5 = (f32[144,16,128]{2,1,0:T(8,128)S(1)}, f32[144,16,128]{2,1,0:T(8,128)S(1)}, u32[]{:S(2)}, u32[]{:S(2)}) collective-permute-start(f32[144,16,128]{2,1,0:T(8,128)S(1)} %get-tuple-element.18.own), channel_id=1, source_target_pairs={{1,2},{3,4},{5,6},{7,8},{9,10},{11,12},{13,14},{15,16},{17,18},{19... | collective-permute-start | bytes 3538952 | tf_op jit(solution)/shard_map/ppermute | solution.py:476
  117.0 0.1 collective-permute-start.4
  117.1 29.8 %all_to_all.22 = f32[128,1,128]{2,1,0:T(1,128)S(1)} all-to-all(f32[128,1,128]{2,1,0:T(1,128)S(1)} %bitcast.14), channel_id=1, replica_groups=mesh['seg'=32,'sub'=4] {'seg','sub'}, dimensions={0} | all-to-all | bytes 131072 | tf_op jit(solution)/shard_map/all_to_all | solution.py:469
  146.9 0.0 collective-permute-done.5.odd
  146.9 0.0 copy-start.4
  146.9 0.0 collective-permute-done.4.even
  146.9 0.0 copy-start.5
  146.9 1.1 copy-done.4
  148.0 0.4 copy-done.5
  148.4 15.8 %arrive_out.1 = f32[19,20,4096]{2,1,0:T(8,128)} custom-call(s32[432]{0:T(512)S(1)} %reshape.9.index, f32[128,128]{1,0:T(8,128)S(1)} %bitcast.13, f32[3,19,32,8,128]{4,3,2,1,0:T(8,128)} %get-tuple-element.17.before, s32[20,4096]{1,0:T(8,128)S(1)} %copy-done.1, s32[18,24,128]{2,1,0:T(8,128)S(1)} %broadcast_in_dim.4.absent, ...), custom_call_target="tpu_custom_call" | custom-call | tf_op jit(solution)/shard_map/arrive_out/pallas_call | solution.py:455
  (4 shorter events, 0.0 us)
Async XLA Ops:
  0.0 1.0 copy-start
  1.0 40.4 %copy-start.6 = (s32[20,18]{1,0:T(8,128)S(1)}, s32[20,18]{1,0:T(8,128)}, u32[]{:S(2)}) copy-start(s32[20,18]{1,0:T(8,128)} %param.5) | copy-start | bytes 4324
  1.0 40.4 %copy-start.7 = (s32[18]{0:T(128)S(1)}, s32[18]{0:T(128)}, u32[]{:S(2)}) copy-start(s32[18]{0:T(128)} %constant.41.clone) | copy-start | bytes 220
  1.0 85.0 %copy-start.1 = (s32[20,4096]{1,0:T(8,128)S(1)}, s32[20,4096]{1,0:T(8,128)}, u32[]{:S(2)}) copy-start(s32[20,4096]{1,0:T(8,128)} %kinds.5) | copy-start | bytes 983044
  19.5 65.7 %copy-start.2 = (f32[144,16,128]{2,1,0:T(8,128)}, f32[144,16,128]{2,1,0:T(8,128)S(1)}, u32[]{:S(2)}) copy-start(f32[144,16,128]{2,1,0:T(8,128)S(1)} %get-tuple-element.14.own) | copy-start | bytes 3538948
  19.5 65.5 %collective-permute-start.1 = (f32[144,16,128]{2,1,0:T(8,128)S(1)}, f32[144,16,128]{2,1,0:T(8,128)}, u32[]{:S(2)}, u32[]{:S(2)}) collective-permute-start(f32[144,16,128]{2,1,0:T(8,128)S(1)} %get-tuple-element.14.own), channel_id=1, source_target_pairs={{1,2},{3,4},{5,6},{7,8},{9,10},{11,12},{13,14},{15,16},{17,18},{19... | collective-permute-start | bytes 3538952 | tf_op jit(solution)/shard_map/ppermute | solution.py:476
  25.3 59.7 %collective-permute-start = (f32[144,16,128]{2,1,0:T(8,128)S(1)}, f32[144,16,128]{2,1,0:T(8,128)}, u32[]{:S(2)}, u32[]{:S(2)}) collective-permute-start(f32[144,16,128]{2,1,0:T(8,128)S(1)} %get-tuple-element.14.own), channel_id=1, source_target_pairs={{0,1},{1,0},{2,3},{3,2},{4,5},{5,4},{6,7},{7,6},{8,9},{9,8},{10,11... | collective-permute-start | bytes 3538952 | tf_op jit(solution)/shard_map/ppermute | solution.py:476
  25.4 59.6 %collective-permute-start.3 = (f32[144,16,128]{2,1,0:T(8,128)}, f32[144,16,128]{2,1,0:T(8,128)S(1)}, u32[]{:S(2)}, u32[]{:S(2)}) collective-permute-start(f32[144,16,128]{2,1,0:T(8,128)} %get-tuple-element.15.own_m), channel_id=1, source_target_pairs={{1,2},{3,4},{5,6},{7,8},{9,10},{11,12},{13,14},{15,16},{17,18},{19... | collective-permute-start | bytes 3538952 | tf_op jit(solution)/shard_map/ppermute | solution.py:476
  28.6 56.4 %collective-permute-start.2 = (f32[144,16,128]{2,1,0:T(8,128)}, f32[144,16,128]{2,1,0:T(8,128)}, u32[]{:S(2)}, u32[]{:S(2)}) collective-permute-start(f32[144,16,128]{2,1,0:T(8,128)} %get-tuple-element.15.own_m), channel_id=1, source_target_pairs={{0,1},{1,0},{2,3},{3,2},{4,5},{5,4},{6,7},{7,6},{8,9},{9,8},{10,11... | collective-permute-start | bytes 3538952 | tf_op jit(solution)/shard_map/ppermute | solution.py:476
  29.8 55.3 %all-to-all-start = ((f32[128,1,128]{2,1,0:T(1,128)}), f32[128,1,128]{2,1,0:T(1,128)S(1)}, u32[]{:S(2)}, u32[]{:S(2)}) async-start(f32[128,1,128]{2,1,0:T(1,128)} %bitcast.2), calls=%async_computation | async-start | bytes 131072 | tf_op jit(solution)/shard_map/all_to_all | solution.py:469
  85.0 1.0 copy-start.3
  112.1 34.9 %collective-permute-start.5 = (f32[144,16,128]{2,1,0:T(8,128)S(1)}, f32[144,16,128]{2,1,0:T(8,128)S(1)}, u32[]{:S(2)}, u32[]{:S(2)}) collective-permute-start(f32[144,16,128]{2,1,0:T(8,128)S(1)} %get-tuple-element.18.own), channel_id=1, source_target_pairs={{1,2},{3,4},{5,6},{7,8},{9,10},{11,12},{13,14},{15,16},{17,18},{19... | collective-permute-start | bytes 3538952 | tf_op jit(solution)/shard_map/ppermute | solution.py:476
  117.0 29.9 %collective-permute-start.4 = (f32[144,16,128]{2,1,0:T(8,128)S(1)}, f32[144,16,128]{2,1,0:T(8,128)S(1)}, u32[]{:S(2)}, u32[]{:S(2)}) collective-permute-start(f32[144,16,128]{2,1,0:T(8,128)S(1)} %get-tuple-element.18.own), channel_id=1, source_target_pairs={{0,1},{1,0},{2,3},{3,2},{4,5},{5,4},{6,7},{7,6},{8,9},{9,8},{10,11... | collective-permute-start | bytes 3538952 | tf_op jit(solution)/shard_map/ppermute | solution.py:476
  146.9 1.1 copy-start.4
  146.9 1.5 copy-start.5

commit v3 on v2

--- a/solution.py
+++ b/solution.py
@@ -13,6 +13,7 @@
 SITES = 4096
 GROUP = 8
 CHUNKS = 32
+SLOTS = 32
 AXES = ("seg", "sub")
 INLET = 0.1
 
@@ -286,7 +287,7 @@
     return jnp.broadcast_to(ratio[:, 0:1], (GROUP, 128))
 
 
-def collide_all(load, kinds, posted, sums, rows_out, step, bricks):
+def collide_all(load, kinds, posted, sums, rows_out, step, bricks, excess):
     real = iota((GROUP, 128), 0) + step * GROUP < bricks
 
     def chunk(c, carry):
@@ -314,17 +315,33 @@
 
     @pl.when(step == pl.num_programs(0) - 1)
     def _():
-        left = iota(rows_out.shape, 1) < 64
-        rows_out[...] = jnp.where(left, jnp.sum(sums[0]), jnp.sum(sums[1]))
-
-
-def first_kernel(bricks, pops, kinds, posted, faces, marks, rows_out, layers, sums):
+        lane = iota(rows_out.shape, 1)
+        both = jnp.where(lane < 64, jnp.sum(sums[0]), jnp.sum(sums[1]))
+        rows_out[...] = jnp.where(lane == 127, excess, both)
+
+
+def select_blocks(lists, table, send, start):
+    slots = lists.shape[0] // 2 - 1
+
+    @pl.when(pl.program_id(0) == pl.num_programs(0) - 1)
+    def _():
+        def slot(s, carry):
+            for partner in range(2):
+                send[partner, start + s] = table[lists[partner * (slots + 1) + s]]
+            return carry
+
+        lax.fori_loop(0, slots, slot, 0)
+
+
+def first_kernel(bricks, lists, pops, kinds, posted, faces, marks, send, rows_out, layers, sums):
     step = pl.program_id(0)
+    slots = lists.shape[0] // 2 - 1
+    excess = (lists[slots] + lists[2 * slots + 1]).astype(F32)
 
     def load(i, c):
         return pops[i, :, pl.ds(pl.multiple_of(128 * c, 128), 128)]
 
-    collide_all(load, kinds, posted, sums, rows_out, step, bricks)
+    collide_all(load, kinds, posted, sums, rows_out, step, bricks, excess)
     pack(lambda m, c: posted[0, m, c], layers, faces, step)
 
     def mark(m, c):
@@ -332,33 +349,34 @@
         return jnp.where(kinds[:, lanes] == 3, 1.0, 0.0)
 
     pack(mark, layers, marks, step)
-
-
-def fill(pieces, table, sems):
-    copies = []
-    start = 0
-    for k, piece in enumerate(pieces):
-        count = piece.shape[0]
-        copies.append(pltpu.make_async_copy(piece, table.at[pl.ds(start, count)], sems.at[k]))
-        start += count
-    return copies
-
-
-def take_tables(refs, table, marks, sems):
-    copies = fill(refs[:3], table, sems.at[0]) + fill(refs[3:], marks, sems.at[1])
+    select_blocks(lists, faces, send, 0)
+    select_blocks(lists, marks, send, slots)
+
+
+def take_tables(slots, own, own_marks, sent, sent_before, table, marks, sems):
+    blocks = own.shape[0]
+    copies = [pltpu.make_async_copy(own, table.at[pl.ds(0, blocks)], sems.at[0]),
+              pltpu.make_async_copy(own_marks, marks.at[pl.ds(0, blocks)], sems.at[1])]
+    for partner in range(2):
+        rows = pl.ds(blocks + partner * slots, slots)
+        copies.append(pltpu.make_async_copy(
+            sent[partner].at[pl.ds(0, slots)], table.at[rows], sems.at[2 + partner]))
+        copies.append(pltpu.make_async_copy(
+            sent_before[partner].at[pl.ds(slots, slots)], marks.at[rows], sems.at[4 + partner]))
     for copy in copies:
         copy.start()
     for copy in copies:
         copy.wait()
 
 
-def middle_kernel(bricks, index, gathered, before, kinds, absent, own, even, odd, own_m, even_m, odd_m,
-                  posted, faces, rows_out, table, marks, arriving, pops, layers, sums, sems):
+def middle_kernel(bricks, lists, index, gathered, before, kinds, absent, own, own_m, even, odd,
+                  posted, faces, send, rows_out, table, marks, arriving, pops, layers, sums, sems):
     step = pl.program_id(0)
+    slots = lists.shape[0] // 2 - 1
 
     @pl.when(step == 0)
     def _():
-        take_tables((own, even, odd, own_m, even_m, odd_m), table, marks, sems)
+        take_tables(slots, own, own_m, (even, odd), (even, odd), table, marks, sems)
 
     mean = mean_of(gathered)
     gather(index, step, table, marks, mean, arriving)
@@ -367,17 +385,18 @@
         pops[member, chunk] = value
 
     stream(before, kinds, absent, arriving, mean, put)
-    collide_all(lambda i, c: pops[i, c], kinds, posted, sums, rows_out, step, bricks)
+    collide_all(lambda i, c: pops[i, c], kinds, posted, sums, rows_out, step, bricks, 0.0)
     pack(lambda m, c: posted[0, m, c], layers, faces, step)
-
-
-def last_kernel(index, gathered, before, kinds, absent, own, even, odd, own_m, even_m, odd_m,
+    select_blocks(lists, faces, send, 0)
+
+
+def last_kernel(slots, index, gathered, before, kinds, absent, own, own_m, even, odd, even_1, odd_1,
                 out, table, marks, arriving, sems):
     step = pl.program_id(0)
 
     @pl.when(step == 0)
     def _():
-        take_tables((own, even, odd, own_m, even_m, odd_m), table, marks, sems)
+        take_tables(slots, own, own_m, (even, odd), (even_1, odd_1), table, marks, sems)
 
     mean = mean_of(gathered)
     gather(index, step, table, marks, mean, arriving)
@@ -417,49 +436,54 @@
     return jax.ShapeDtypeStruct(shape, F32)
 
 
-def first_call(pops, kinds, groups, devices):
+def first_call(lists, pops, kinds, groups, devices):
     blocks = groups * GROUP * 6
+    slots = lists.shape[0] // 2 - 1
     return pl.pallas_call(
         functools.partial(first_kernel, pops.shape[1]),
         grid=(groups,),
-        in_specs=[SPEC_POPS, SPEC_KINDS],
-        out_specs=[SPEC_POSTED, whole(blocks, *BLOCK), whole(blocks, *BLOCK), whole(devices, 128)],
+        in_specs=[SPEC_SMEM, SPEC_POPS, SPEC_KINDS],
+        out_specs=[SPEC_POSTED, whole(blocks, *BLOCK), whole(blocks, *BLOCK),
+                   whole(2, 2 * slots, *BLOCK), whole(devices, 128)],
         out_shape=[shape_of(groups, *POSTED), shape_of(blocks, *BLOCK), shape_of(blocks, *BLOCK),
-                   shape_of(devices, 128)],
+                   shape_of(2, 2 * slots, *BLOCK), shape_of(devices, 128)],
         scratch_shapes=[pltpu.VMEM((6, 128, 128), F32), pltpu.VMEM((2, GROUP, 128), F32)],
         compiler_params=params(),
         name="first_collide",
-    )(pops, kinds)
-
-
-def middle_call(bricks, index, gathered, before, kinds, absent, tables, groups, devices):
+    )(lists, pops, kinds)
+
+
+def middle_call(bricks, lists, index, gathered, before, kinds, absent, tables, groups, devices):
     blocks = groups * GROUP * 6
-    rows = sum(t.shape[0] for t in tables[:3])
+    slots = lists.shape[0] // 2 - 1
+    rows = blocks + 2 * slots
     return pl.pallas_call(
         functools.partial(middle_kernel, bricks),
         grid=(groups,),
-        in_specs=[SPEC_SMEM, whole(devices, 128), SPEC_POSTED, SPEC_KINDS, SPEC_ABSENT] + [SPEC_ANY] * 6,
-        out_specs=[SPEC_POSTED, whole(blocks, *BLOCK), whole(devices, 128)],
-        out_shape=[shape_of(groups, *POSTED), shape_of(blocks, *BLOCK), shape_of(devices, 128)],
+        in_specs=[SPEC_SMEM, SPEC_SMEM, whole(devices, 128), SPEC_POSTED, SPEC_KINDS,
+                  SPEC_ABSENT] + [SPEC_ANY] * 4,
+        out_specs=[SPEC_POSTED, whole(blocks, *BLOCK), whole(2, slots, *BLOCK), whole(devices, 128)],
+        out_shape=[shape_of(groups, *POSTED), shape_of(blocks, *BLOCK), shape_of(2, slots, *BLOCK),
+                   shape_of(devices, 128)],
         scratch_shapes=[pltpu.VMEM((rows,) + BLOCK, F32), pltpu.VMEM((rows,) + BLOCK, F32),
                         pltpu.VMEM((18, 128, 128), F32), pltpu.VMEM(POSTED, F32),
                         pltpu.VMEM((6, 128, 128), F32), pltpu.VMEM((2, GROUP, 128), F32),
-                        pltpu.SemaphoreType.DMA((2, 3))],
+                        pltpu.SemaphoreType.DMA((6,))],
         compiler_params=params(),
         name="arrive_collide",
-    )(index, gathered, before, kinds, absent, *tables)
-
-
-def last_call(bricks, index, gathered, before, kinds, absent, tables, groups, devices):
-    rows = sum(t.shape[0] for t in tables[:3])
+    )(lists, index, gathered, before, kinds, absent, *tables)
+
+
+def last_call(bricks, slots, index, gathered, before, kinds, absent, tables, groups, devices):
+    rows = groups * GROUP * 6 + 2 * slots
     return pl.pallas_call(
-        last_kernel,
+        functools.partial(last_kernel, slots),
         grid=(groups,),
         in_specs=[SPEC_SMEM, whole(devices, 128), SPEC_POSTED, SPEC_KINDS, SPEC_ABSENT] + [SPEC_ANY] * 6,
         out_specs=SPEC_POPS,
         out_shape=shape_of(19, bricks, SITES),
         scratch_shapes=[pltpu.VMEM((rows,) + BLOCK, F32), pltpu.VMEM((rows,) + BLOCK, F32),
-                        pltpu.VMEM((18, 128, 128), F32), pltpu.SemaphoreType.DMA((2, 3))],
+                        pltpu.VMEM((18, 128, 128), F32), pltpu.SemaphoreType.DMA((6,))],
         compiler_params=params(),
         name="arrive_out",
     )(index, gathered, before, kinds, absent, *tables)
@@ -469,39 +493,91 @@
     return lax.all_to_all(rows, AXES, 0, 0, tiled=True)
 
 
-def swap(layers, devices):
+def swap(send, devices):
     even_pairs = [(i, i ^ 1) for i in range(devices)]
     odd_pairs = [(i, i + 1) for i in range(1, devices - 1, 2)]
     odd_pairs = odd_pairs + [(b, a) for a, b in odd_pairs]
-    return (layers, lax.ppermute(layers, AXES, even_pairs), lax.ppermute(layers, AXES, odd_pairs))
+    return lax.ppermute(send[0], AXES, even_pairs), lax.ppermute(send[1], AXES, odd_pairs)
+
+
+def rank(used):
+    count = used.shape[0]
+    return jnp.sum(jnp.where(iota((count, count), 1) < iota((count, count), 0), used[None, :], 0), axis=1)
+
+
+def exchange_plan(neighbours, slots, padded):
+    bricks = neighbours.shape[0]
+    blocks = bricks * 6
+    me = lax.axis_index(AXES)
+    local = neighbours - me * bricks
+    present = neighbours >= 0
+    following = present & (local >= bricks)
+    preceding = present & (local < 0)
+    first = me % 2 == 0
+    read = jnp.asarray(np.array(COLUMN_FACE, np.int32))
+    given = jnp.asarray(np.array([COLUMN_FACE[OPP[d + 1] - 1] for d in range(18)], np.int32))
+    faces = jnp.arange(6, dtype=jnp.int32)
+    index = local * 6 + read[None, :]
+    lists = []
+    for partner in range(2):
+        is_next = first if partner == 0 else ~first
+        there = jnp.where(is_next, following, preceding)
+        spot = (local + jnp.where(is_next, -bricks, bricks)) * 6 + read[None, :]
+        used = jnp.any(there[:, :, None] & (given[:, None] == faces[None, :])[None], axis=1)
+        used = used.astype(jnp.int32).reshape(-1)
+        order = jnp.where(used == 1, rank(used), blocks)
+        chosen = order[None, :] == iota((slots, blocks), 0)
+        lists.append(jnp.sum(jnp.where(chosen, iota((slots, blocks), 1), 0), axis=1))
+        lists.append(jnp.where(jnp.sum(used) > slots, 1, 0)[None])
+        flat = jnp.where(there, spot, -1).reshape(-1)
+        hits = flat[:, None] == iota((flat.shape[0], blocks), 1)
+        ranks = rank(jnp.any(hits, axis=0).astype(jnp.int32))
+        at = jnp.sum(jnp.where(hits, jnp.minimum(ranks, slots - 1)[None, :], 0), axis=1)
+        index = jnp.where(there, padded * 6 + partner * slots + at.reshape(bricks, 18), index)
+    index = jnp.where(present, index, 0)
+    index = jnp.pad(index, ((0, padded - bricks), (0, 0))).reshape(-1)
+    return jnp.concatenate(lists), index
+
+
+def begin(devices, slots, populations, neighbours, site_flags, absent):
+    bricks = populations.shape[1]
+    groups = absent.shape[1] // GROUP
+    lists, index = exchange_plan(neighbours, slots, groups * GROUP)
+    posted, faces, marks, send, rows = first_call(lists, populations, site_flags, groups, devices)
+    gathered = share_sums(rows)
+    sent_first = swap(send, devices)
+    excess = jnp.sum(gathered[:, 127])
+    posted, faces, send, rows = middle_call(
+        bricks, lists, index, gathered, posted, site_flags, absent,
+        (faces, marks) + sent_first, groups, devices)
+    gathered = share_sums(rows)
+    sent = swap(send, devices)
+    return excess, (index, gathered, posted, faces, marks) + sent + sent_first
+
+
+def finish(devices, slots, site_flags, absent, bricks, state):
+    index, gathered, posted, faces, marks = state[:5]
+    return last_call(bricks, slots, index, gathered, posted, site_flags, absent,
+                     (faces, marks) + state[5:], absent.shape[1] // GROUP, devices)
 
 
 def on_device(devices, populations, neighbours, site_flags):
     bricks = populations.shape[0]
-    groups = -(-bricks // GROUP)
-    padded = groups * GROUP
-    blocks = padded * 6
-    me = lax.axis_index(AXES)
-    local = neighbours - me * bricks
-    parity = me % 2
-    after = jnp.where(parity == 0, blocks, 2 * blocks)
-    before = jnp.where(parity == 0, 2 * blocks, blocks)
-    place = jnp.where(local < 0, before + (local + bricks) * 6,
-                      jnp.where(local >= bricks, after + (local - bricks) * 6, local * 6))
-    index = jnp.where(neighbours < 0, 0, place + jnp.asarray(np.array(COLUMN_FACE, np.int32))[None, :])
-    index = jnp.pad(index, ((0, padded - bricks), (0, 0))).reshape(-1)
+    padded = -(-bricks // GROUP) * GROUP
     absent = jnp.pad((neighbours < 0).astype(jnp.int32), ((0, padded - bricks), (0, 0)))
     absent = jnp.broadcast_to(absent.T[:, :, None], (18, padded, 128))
-
-    posted, faces, marks, rows = first_call(jnp.transpose(populations, (1, 0, 2)), site_flags, groups, devices)
-    gathered = share_sums(rows)
-    mark_tables = swap(marks, devices)
-    tables = swap(faces, devices) + mark_tables
-    posted, faces, rows = middle_call(
-        bricks, index, gathered, posted, site_flags, absent, tables, groups, devices)
-    gathered = share_sums(rows)
-    tables = swap(faces, devices) + mark_tables
-    out = last_call(bricks, index, gathered, posted, site_flags, absent, tables, groups, devices)
+    populations = jnp.transpose(populations, (1, 0, 2))
+    excess, state = begin(devices, SLOTS, populations, neighbours, site_flags, absent)
+
+    def enough(populations, neighbours, state):
+        return finish(devices, SLOTS, site_flags, absent, bricks, state)
+
+    def too_few(populations, neighbours, state):
+        every = bricks * 6
+        _, state = begin(devices, every, populations, neighbours, site_flags, absent)
+        return finish(devices, every, site_flags, absent, bricks, state)
+
+    out = lax.cond(excess > 0.0, too_few, enough, populations, neighbours, state)
     return jnp.transpose(out, (1, 0, 2))
 
 

time: 164 us -> 121 us (0.74)
  blocking collectives: 29.8 us -> 0 us
  waiting for transfers between devices: 43.4 us -> 19.8 us
  other arithmetic: 0.03 us -> 5.24 us
  starting transfers between devices: 26.9 us -> 31.6 us
  between operations: 0.17 us -> 2.29 us
    all_to_all x1 -> x2, waiting for transfers between devices: 43.4 us -> 10.8 us  [share_sums(): return lax.all_to_all(rows, AXES, 0, 0, tiled=True)]
    all_to_all x1 -> x0, blocking collectives: 29.8 us -> none  [share_sums(): return lax.all_to_all(rows, AXES, 0, 0, tiled=True)]
    all_to_all x1 -> x2, starting transfers between devices: 11.6 us -> 23.2 us  [share_sums(): return lax.all_to_all(rows, AXES, 0, 0, tiled=True)]
    ppermute x6 -> x4, waiting for transfers between devices: 0.02 us -> 8.99 us  [the longest x2 7.86 us: swap(): lax.ppermute(send[1], AXES, odd_pairs)]
    ppermute x6 -> x4, starting transfers between devices: 15.3 us -> 8.43 us  [the longest x2 8.26 us: swap(): lax.ppermute(send[1], AXES, odd_pairs)]
    unnamed x16, local copies, waits for them, and re-layouts: 3.35 us -> 0.74 us
    reduce_sum x0 -> x9, other arithmetic: none -> 2.41 us  [the longest x1 0.72 us: exchange_plan(): lists.append(jnp.where(jnp.sum(used) > slots, 1, 0)[None])]
  transfers between devices with their start and end apart: 7 -> 6, of which waited for: 1 -> 4; matrix products, arithmetic and copies ran while one was open for 0% -> 3% of each run, Pallas kernels for 0% -> 0%
where the time goes in v3:
time: 121 us
  Pallas kernels  59 us (49%)
  starting transfers between devices  31.6 us (26%)
  waiting for transfers between devices  19.8 us (16%)
  other arithmetic  5.24 us (4%)
  local copies, waits for them, and re-layouts  2.92 us (2%)
  between operations  2.29 us (2%)
    pallas_call x1, Pallas kernels, middle_call(): pl.pallas_call(functools.partial(middle_kernel, bricks), grid=(groups,),...  25.5 us
    all_to_all x2, starting transfers between devices, share_sums(): return lax.all_to_all(rows, AXES, 0, 0, tiled=True)  23.2 us
    pallas_call x1, Pallas kernels, first_call(): pl.pallas_call(functools.partial(first_kernel, pops.shape[1]), grid=(grou...  19.2 us
    pallas_call x1, Pallas kernels, last_call(): pl.pallas_call(functools.partial(last_kernel, slots), grid=(groups,), in_...  14.3 us
    all_to_all x2, waiting for transfers between devices, share_sums(): return lax.all_to_all(rows, AXES, 0, 0, tiled=True)  10.8 us
    ppermute x2, starting transfers between devices, swap(): lax.ppermute(send[1], AXES, odd_pairs)  8.26 us
    ppermute x2, waiting for transfers between devices, swap(): lax.ppermute(send[1], AXES, odd_pairs)  7.86 us
  transfers between devices with their start and end apart: 6, of which 4 were waited for; matrix products, arithmetic and copies ran while one was open for 3% of the time, Pallas kernels for 0%

profile of v3, /device:TPU:1, one launch (start us, length us, event | category | flops | bytes accessed | tf_op | source)
XLA Modules:
  0.0 120.9 jit_solution(3739805214279717160)
XLA Ops:
  0.0 0.7 iota_compare_fusion.11
  0.7 0.7 add_select_fusion.2
  1.4 0.7 add_select_fusion.3
  2.1 0.3 and_reduce_fusion.3
  2.4 0.7 convert_reduce_fusion.2
  4.5 0.1 copy.21
  4.6 0.1 reshape.170
  4.7 0.1 select_reduce_fusion.12
  4.8 0.1 copy.20
  4.9 0.1 reshape.169
  5.0 0.1 select_reduce_fusion.13
  5.1 0.1 select_reduce_fusion.14
  5.2 0.1 pad_add_fusion.1.lists
  5.3 19.2 %first_collide.3 = (f32[3,19,32,8,128]{4,3,2,1,0:T(8,128)}, f32[144,16,128]{2,1,0:T(8,128)}, f32[144,16,128]{2,1,0:T(8,128)}, f32[2,64,16,128]{3,2,1,0:T(8,128)S(1)}, f32[128,128]{1,0:T(8,128)}) custom-call(s32[66]{0:T(128)S(1)} %pad_add_fusion.1.lists, f32[19,20,4096]{2,1,0:T(8,128)} %bitcast.46, s32[20,4096]{1,0:T(8,128)} %kinds.3), custom_call_target="tpu_custom_call" | custom-call | tf_op jit(solution)/shard_map/first_collide/pallas_call | solution.py:442
  24.6 0.0 copy-start.9
  24.6 0.0 copy-start.10
  24.6 0.0 copy-start.1
  24.6 0.0 copy-start.3
  24.6 11.5 %all-to-all-start.2 = ((f32[128,1,128]{2,1,0:T(1,128)}), f32[128,1,128]{2,1,0:T(1,128)S(1)}, u32[]{:S(2)}, u32[]{:S(2)}) async-start(f32[128,1,128]{2,1,0:T(1,128)} %bitcast.20), calls=%async_computation.2 | async-start | bytes 131072 | tf_op jit(solution)/shard_map/all_to_all | solution.py:493
  36.1 1.1 slice_bitcast_fusion.4
  37.2 4.7 %collective-permute-start.5 = (f32[64,16,128]{2,1,0:T(8,128)}, f32[64,16,128]{2,1,0:T(8,128)S(1)}, u32[]{:S(2)}, u32[]{:S(2)}) collective-permute-start(f32[64,16,128]{2,1,0:T(8,128)} %get-tuple-element.133), channel_id=1, source_target_pairs={{1,2},{3,4},{5,6},{7,8},{9,10},{11,12},{13,14},{15,16},{17,18},{19... | collective-permute-start | bytes 1572872 | tf_op jit(solution)/shard_map/ppermute | solution.py:500
  42.0 0.1 collective-permute-start.4
  42.1 0.1 eq.170
  42.1 0.1 fusion.2
  42.3 0.1 select_reduce_fusion.10
  42.4 0.2 select_reduce_fusion.8
  42.7 0.1 add.121
  42.8 0.1 eq.167
  42.8 0.1 fusion.3
  43.0 0.1 select_reduce_fusion.11
  43.1 0.2 select_reduce_fusion.9
  43.4 0.1 add.116
  43.5 0.0 copy-done.9
  43.5 0.0 copy-done.10
  43.5 0.1 copy.23
  43.6 0.1 reshape.166.index
  43.7 2.3 %all-to-all-done.2 = f32[128,1,128]{2,1,0:T(1,128)S(1)} async-done(((f32[128,1,128]{2,1,0:T(1,128)}), f32[128,1,128]{2,1,0:T(1,128)S(1)}, u32[]{:S(2)}, u32[]{:S(2)}) %all-to-all-start.2) | async-done | bytes 65568 | tf_op jit(solution)/shard_map/all_to_all | solution.py:493
  46.0 7.9 %collective-permute-done.5.odd = f32[64,16,128]{2,1,0:T(8,128)S(1)} collective-permute-done((f32[64,16,128]{2,1,0:T(8,128)}, f32[64,16,128]{2,1,0:T(8,128)S(1)}, u32[]{:S(2)}, u32[]{:S(2)}) %collective-permute-start.5) | collective-permute-done | bytes 524320 | tf_op jit(solution)/shard_map/ppermute | solution.py:500
  53.9 0.0 copy-start.6
  53.9 1.1 collective-permute-done.4.even
  55.0 0.0 copy-start.7
  55.0 0.1 broadcast_in_dim.181.absent
  55.1 0.0 copy-done.6
  55.1 0.7 copy-done.7
  55.8 0.0 copy-done.1
  55.8 0.0 copy-done.3
  55.8 0.0 copy-start.5
  55.8 0.0 copy-start.11
  55.8 25.5 %arrive_collide.3 = (f32[3,19,32,8,128]{4,3,2,1,0:T(8,128)}, f32[144,16,128]{2,1,0:T(8,128)}, f32[2,32,16,128]{3,2,1,0:T(8,128)S(1)}, f32[128,128]{1,0:T(8,128)}) custom-call(s32[66]{0:T(128)S(1)} %pad_add_fusion.1.lists, s32[432]{0:T(512)S(1)} %reshape.166.index, f32[128,128]{1,0:T(8,128)S(1)} %bitcast.41, f32[3,19,32,8,128]{4,3,2,1,0:T(8,128)} %get-tuple-element.79.before, ...), custom_call_target="tpu_custom_call" | custom-call | tf_op jit(solution)/shard_map/arrive_collide/pallas_call | solution.py:460
  81.4 3.5 %collective-permute-start.7 = (f32[32,16,128]{2,1,0:T(8,128)S(1)}, f32[32,16,128]{2,1,0:T(8,128)S(1)}, u32[]{:S(2)}, u32[]{:S(2)}) collective-permute-start(f32[32,16,128]{2,1,0:T(8,128)S(1)} %get-tuple-element.135), channel_id=1, source_target_pairs={{1,2},{3,4},{5,6},{7,8},{9,10},{11,12},{13,14},{15,16},{17,18},{19... | collective-permute-start | bytes 786440 | tf_op jit(solution)/shard_map/ppermute | solution.py:500
  84.9 0.1 collective-permute-start.6
  85.0 11.7 %all-to-all-start.3 = ((f32[128,1,128]{2,1,0:T(1,128)}), f32[128,1,128]{2,1,0:T(1,128)S(1)}, u32[]{:S(2)}, u32[]{:S(2)}) async-start(f32[128,1,128]{2,1,0:T(1,128)} %bitcast.26), calls=%async_computation.3 | async-start | bytes 131072 | tf_op jit(solution)/shard_map/all_to_all | solution.py:493
  96.7 0.7 slice_reduce_fusion
  98.0 8.6 %all-to-all-done.3 = f32[128,1,128]{2,1,0:T(1,128)S(1)} async-done(((f32[128,1,128]{2,1,0:T(1,128)}), f32[128,1,128]{2,1,0:T(1,128)S(1)}, u32[]{:S(2)}, u32[]{:S(2)}) %all-to-all-start.3) | async-done | bytes 65568 | tf_op jit(solution)/shard_map/all_to_all | solution.py:493
  106.6 0.0 collective-permute-done.7
  106.6 0.0 collective-permute-done.6
  106.6 0.0 copy-done.5
  106.6 0.0 copy-done.11
  106.6 14.3 %conditional.1 = (f32[19,20,4096]{2,1,0:T(8,128)}) conditional(s32[]{:T(128)} %convert_element_type.106, (f32[128,1,128]{2,1,0:T(1,128)S(1)}, s32[432]{0:T(512)S(1)}, f32[3,19,32,8,128]{4,3,2,1,0:T(8,128)}, s32[20,4096]{1,0:T(8,128)S(1)}, s32[18,24,128]{2,1,0:T(8,128)S(1)}, /*index=5*/f32[144,16,128]{2,1,0:T(8,128)}, ...), branch_computations={%region_15.16_spmd, %region_16.31_spmd} | conditional | flops 709819 | bytes 57019992 | solution.py:580
  106.6 14.3 %arrive_out.2 = f32[19,20,4096]{2,1,0:T(8,128)} custom-call(s32[432]{0:T(512)S(1)} %get-tuple-element.43.index, f32[128,128]{1,0:T(8,128)S(1)} %bitcast.48, f32[3,19,32,8,128]{4,3,2,1,0:T(8,128)} %get-tuple-element.45.before, s32[20,4096]{1,0:T(8,128)S(1)} %get-tuple-element.46.kinds, s32[18,24,128]{2,1,0:T(8,128)S(1)} %get-tuple-element.47.absent, ...), custom_call_target="tpu_custom_call" | custom-call | tf_op jit(solution)/shard_map/cond/branch_0_fun/arrive_out/pallas_call | solution.py:479
  (15 shorter events, 0.1 us)
Async XLA Ops:
  24.6 18.9 %copy-start.9 = (s32[20,18]{1,0:T(8,128)S(1)}, s32[20,18]{1,0:T(8,128)}, u32[]{:S(2)}) copy-start(s32[20,18]{1,0:T(8,128)} %param.10) | copy-start | bytes 4324
  24.6 18.9 %copy-start.10 = (s32[18]{0:T(128)S(1)}, s32[18]{0:T(128)}, u32[]{:S(2)}) copy-start(s32[18]{0:T(128)} %constant.101.clone) | copy-start | bytes 220
  24.6 31.2 %copy-start.1 = (f32[144,16,128]{2,1,0:T(8,128)S(1)}, f32[144,16,128]{2,1,0:T(8,128)}, u32[]{:S(2)}) copy-start(f32[144,16,128]{2,1,0:T(8,128)} %get-tuple-element.80.own) | copy-start | bytes 3538948
  24.6 31.2 %copy-start.3 = (s32[20,4096]{1,0:T(8,128)S(1)}, s32[20,4096]{1,0:T(8,128)}, u32[]{:S(2)}) copy-start(s32[20,4096]{1,0:T(8,128)} %kinds.3) | copy-start | bytes 983044
  24.6 21.4 %all-to-all-start.2 = ((f32[128,1,128]{2,1,0:T(1,128)}), f32[128,1,128]{2,1,0:T(1,128)S(1)}, u32[]{:S(2)}, u32[]{:S(2)}) async-start(f32[128,1,128]{2,1,0:T(1,128)} %bitcast.20), calls=%async_computation.2 | async-start | bytes 131072 | tf_op jit(solution)/shard_map/all_to_all | solution.py:493
  37.2 16.6 %collective-permute-start.5 = (f32[64,16,128]{2,1,0:T(8,128)}, f32[64,16,128]{2,1,0:T(8,128)S(1)}, u32[]{:S(2)}, u32[]{:S(2)}) collective-permute-start(f32[64,16,128]{2,1,0:T(8,128)} %get-tuple-element.133), channel_id=1, source_target_pairs={{1,2},{3,4},{5,6},{7,8},{9,10},{11,12},{13,14},{15,16},{17,18},{19... | collective-permute-start | bytes 1572872 | tf_op jit(solution)/shard_map/ppermute | solution.py:500
  42.0 13.0 %collective-permute-start.4 = (f32[64,16,128]{2,1,0:T(8,128)}, f32[64,16,128]{2,1,0:T(8,128)S(1)}, u32[]{:S(2)}, u32[]{:S(2)}) collective-permute-start(f32[64,16,128]{2,1,0:T(8,128)} %get-tuple-element.134), channel_id=1, source_target_pairs={{0,1},{1,0},{2,3},{3,2},{4,5},{5,4},{6,7},{7,6},{8,9},{9,8},{10,11... | collective-permute-start | bytes 1572872 | tf_op jit(solution)/shard_map/ppermute | solution.py:500
  53.9 1.3 %copy-start.6 = (f32[64,16,128]{2,1,0:T(8,128)}, f32[64,16,128]{2,1,0:T(8,128)S(1)}, u32[]{:S(2)}) copy-start(f32[64,16,128]{2,1,0:T(8,128)S(1)} %collective-permute-done.5.odd) | copy-start | bytes 1572868
  55.0 0.8 copy-start.7
  55.8 50.8 %copy-start.5 = (f32[144,16,128]{2,1,0:T(8,128)S(1)}, f32[144,16,128]{2,1,0:T(8,128)}, u32[]{:S(2)}) copy-start(f32[144,16,128]{2,1,0:T(8,128)} %get-tuple-element.81.own_m) | copy-start | bytes 3538948
  55.8 50.8 %copy-start.11 = (s32[18]{0:T(128)S(1)}, s32[18]{0:T(128)}, u32[]{:S(2)}) copy-start(s32[18]{0:T(128)} %constant.102.clone) | copy-start | bytes 220
  81.4 25.2 %collective-permute-start.7 = (f32[32,16,128]{2,1,0:T(8,128)S(1)}, f32[32,16,128]{2,1,0:T(8,128)S(1)}, u32[]{:S(2)}, u32[]{:S(2)}) collective-permute-start(f32[32,16,128]{2,1,0:T(8,128)S(1)} %get-tuple-element.135), channel_id=1, source_target_pairs={{1,2},{3,4},{5,6},{7,8},{9,10},{11,12},{13,14},{15,16},{17,18},{19... | collective-permute-start | bytes 786440 | tf_op jit(solution)/shard_map/ppermute | solution.py:500
  84.9 21.7 %collective-permute-start.6 = (f32[32,16,128]{2,1,0:T(8,128)S(1)}, f32[32,16,128]{2,1,0:T(8,128)S(1)}, u32[]{:S(2)}, u32[]{:S(2)}) collective-permute-start(f32[32,16,128]{2,1,0:T(8,128)S(1)} %get-tuple-element.136), channel_id=1, source_target_pairs={{0,1},{1,0},{2,3},{3,2},{4,5},{5,4},{6,7},{7,6},{8,9},{9,8},{10,11... | collective-permute-start | bytes 786440 | tf_op jit(solution)/shard_map/ppermute | solution.py:500
  85.0 21.6 %all-to-all-start.3 = ((f32[128,1,128]{2,1,0:T(1,128)}), f32[128,1,128]{2,1,0:T(1,128)S(1)}, u32[]{:S(2)}, u32[]{:S(2)}) async-start(f32[128,1,128]{2,1,0:T(1,128)} %bitcast.26), calls=%async_computation.3 | async-start | bytes 131072 | tf_op jit(solution)/shard_map/all_to_all | solution.py:493

commit v4 on v3

--- a/solution.py
+++ b/solution.py
@@ -13,6 +13,7 @@
 SITES = 4096
 GROUP = 8
 CHUNKS = 32
+LIMIT = 52
 SLOTS = 32
 AXES = ("seg", "sub")
 INLET = 0.1
@@ -116,7 +117,7 @@
     return 2 * dim + (1 if SPEEDS[member][dim] > 0 else 0)
 
 
-def pack(value, layers, table, step):
+def pack(value, mark, layers, table, step):
     lane = iota((GROUP, 128), 1)
     for face in range(2):
         leave = 15 if face % 2 == 0 else 0
@@ -124,44 +125,63 @@
             for h in range(2):
                 row = (8 * h + slot) * 8
                 layers[face, row:row + 8, :] = value(member, 2 * leave + h)
+        for h in range(2):
+            row = (8 * h + 5) * 8
+            layers[face, row:row + 8, :] = mark(2 * leave + h)
 
     def line(x, carry):
         rows = pl.ds(pl.multiple_of(8 * x, 8), 8)
+        outlet = [mark(2 * x + h) for h in range(2)]
         for face in range(2, 6):
             leave = 15 if face % 2 == 0 else 0
             packed = None
-            for slot, member in enumerate(MEMBERS[face]):
+            for slot, member in enumerate(MEMBERS[face] + [None]):
                 if face < 4:
-                    piece = value(member, 2 * x + leave // 8)
+                    piece = outlet[leave // 8] if member is None else value(member, 2 * x + leave // 8)
                     piece = roll(piece, 16 * slot - 16 * (leave % 8), 1)
                     packed = piece if packed is None else jnp.where((lane >> 4) == slot, piece, packed)
                 else:
                     for h in range(2):
-                        piece = roll(value(member, 2 * x + h), 8 * h + slot - leave, 1)
+                        piece = outlet[h] if member is None else value(member, 2 * x + h)
+                        piece = roll(piece, 8 * h + slot - leave, 1)
                         packed = (piece if packed is None
                                   else jnp.where((lane & 15) == 8 * h + slot, piece, packed))
             layers[face, rows, :] = packed
         return carry
 
-    lax.fori_loop(0, BRICK, line, 0)
+    lax.fori_loop(0, BRICK, line, 0, unroll=4)
+    unpack(layers, table, step)
+
+
+def unpack(layers, table, step):
     for face in range(6):
         for j in range(GROUP):
             table[(step * GROUP + j) * 6 + face] = layers[face, pl.ds(j, BRICK, stride=8), :]
 
 
-def gather(index, step, table, marks, mean, arriving):
-    wide = jnp.concatenate([mean, mean], axis=0)
-
+def scaled(block, face, mean):
+    if face < 2:
+        parts = []
+        for h in range(2):
+            part = block[8 * h:8 * h + 8, :]
+            parts.append(jnp.where(jnp.broadcast_to(part[5:6, :], (8, 128)) != 0.0, part * mean, part))
+        return jnp.concatenate(parts, axis=0)
+    lane = iota(BLOCK, 1)
+    by = 16 if face < 4 else 1
+    slot = jnp.minimum(lane >> 4, 5) if face < 4 else jnp.minimum(lane & 7, 5)
+    marks = jnp.take_along_axis(block, lane + (5 - slot) * by, axis=1, mode="promise_in_bounds")
+    return jnp.where((slot < 5) & (marks != 0.0), block * jnp.concatenate([mean, mean], axis=0), block)
+
+
+def gather(bricks, index, step, table, mean, arriving):
     def brick(j, carry):
         base = (step * GROUP + j) * 18
         for column in range(18):
-            at = index[base + column]
-            block = table[at]
-            arriving[column, pl.ds(j, BRICK, stride=8), :] = jnp.where(
-                marks[at] != 0.0, block * wide, block)
+            block = scaled(table[index[base + column]], COLUMN_FACE[column], mean)
+            arriving[column, pl.ds(j, BRICK, stride=8), :] = block
         return carry
 
-    lax.fori_loop(0, GROUP, brick, 0)
+    lax.fori_loop(0, jnp.minimum(GROUP, bricks - step * GROUP), brick, 0)
 
 
 def stream(posted, kinds, absent, arriving, mean, put):
@@ -177,20 +197,26 @@
         place = {0: x, 1: before, -1: after}
         scales = {cx: (scale(2 * place[cx]), scale(2 * place[cx] + 1)) for cx in (0, 1, -1)}
 
-        def load(member, cx, h):
-            return posted[0, member, 2 * place[cx] + h] * scales[cx][h]
-
         for member in range(19):
+            if member % 2 == 1 or member == 0:
+                loaded = {}
+
+            def load(member, cx, h):
+                if (member, cx, h) not in loaded:
+                    loaded[member, cx, h] = posted[0, member, 2 * place[cx] + h] * scales[cx][h]
+                return loaded[member, cx, h]
+
             cx, cy, cz = SPEEDS[member]
             parts = [load(member, cx, h) for h in range(2)]
             mirror = [None, None]
             if cy or cz:
                 mirror = [load(OPP[member], 0, h) for h in range(2)]
             if cy:
-                first, second = roll(parts[0], 16 * cy, 1), roll(parts[1], 16 * cy, 1)
-                carried = lane < 16 if cy > 0 else lane >= 112
+                by = 16 * cy + cz
+                first, second = roll(parts[0], by, 1), roll(parts[1], by, 1)
+                carried = lane < by if cy > 0 else lane >= 128 + by
                 parts = [jnp.where(carried, second, first), jnp.where(carried, first, second)]
-            if cz:
+            elif cz:
                 parts = [roll(part, cz, 1) for part in parts]
             rows = pl.ds(pl.multiple_of(8 * place[cx], 8), 8)
             if cy:
@@ -229,7 +255,7 @@
                 put(member, 2 * x + h, parts[h])
         return carry
 
-    lax.fori_loop(0, BRICK, line, 0)
+    lax.fori_loop(0, BRICK, line, 0, unroll=2)
 
     for member in range(19):
         cx, cy, cz = SPEEDS[member]
@@ -301,7 +327,7 @@
                 carry[1] + jnp.where(counted, 1.0, 0.0))
 
     zero = jnp.zeros((GROUP, 128), F32)
-    total, count = lax.fori_loop(0, CHUNKS, chunk, (zero, zero))
+    total, count = lax.fori_loop(0, CHUNKS, chunk, (zero, zero), unroll=4)
 
     @pl.when(step == 0)
     def _():
@@ -320,20 +346,30 @@
         rows_out[...] = jnp.where(lane == 127, excess, both)
 
 
-def select_blocks(lists, table, send, start):
+def select_blocks(lists, table, send):
     slots = lists.shape[0] // 2 - 1
 
     @pl.when(pl.program_id(0) == pl.num_programs(0) - 1)
     def _():
         def slot(s, carry):
             for partner in range(2):
-                send[partner, start + s] = table[lists[partner * (slots + 1) + s]]
+                send[partner][s] = table[lists[partner * (slots + 1) + s]]
             return carry
 
-        lax.fori_loop(0, slots, slot, 0)
-
-
-def first_kernel(bricks, lists, pops, kinds, posted, faces, marks, send, rows_out, layers, sums):
+        lax.fori_loop(0, slots, slot, 0, unroll=4)
+
+
+def outlet_mark(kinds):
+    def mark(chunk):
+        start = 128 * chunk
+        if not isinstance(start, int):
+            start = pl.multiple_of(start, 128)
+        return jnp.where(kinds[:, pl.ds(start, 128)] == 3, 1.0, 0.0)
+
+    return mark
+
+
+def first_kernel(bricks, lists, pops, kinds, posted, faces, send_even, send_odd, rows_out, layers, sums):
     step = pl.program_id(0)
     slots = lists.shape[0] // 2 - 1
     excess = (lists[slots] + lists[2 * slots + 1]).astype(F32)
@@ -342,64 +378,52 @@
         return pops[i, :, pl.ds(pl.multiple_of(128 * c, 128), 128)]
 
     collide_all(load, kinds, posted, sums, rows_out, step, bricks, excess)
-    pack(lambda m, c: posted[0, m, c], layers, faces, step)
-
-    def mark(m, c):
-        lanes = pl.ds(pl.multiple_of(128 * c, 128), 128)
-        return jnp.where(kinds[:, lanes] == 3, 1.0, 0.0)
-
-    pack(mark, layers, marks, step)
-    select_blocks(lists, faces, send, 0)
-    select_blocks(lists, marks, send, slots)
-
-
-def take_tables(slots, own, own_marks, sent, sent_before, table, marks, sems):
-    blocks = own.shape[0]
-    copies = [pltpu.make_async_copy(own, table.at[pl.ds(0, blocks)], sems.at[0]),
-              pltpu.make_async_copy(own_marks, marks.at[pl.ds(0, blocks)], sems.at[1])]
-    for partner in range(2):
-        rows = pl.ds(blocks + partner * slots, slots)
-        copies.append(pltpu.make_async_copy(
-            sent[partner].at[pl.ds(0, slots)], table.at[rows], sems.at[2 + partner]))
-        copies.append(pltpu.make_async_copy(
-            sent_before[partner].at[pl.ds(slots, slots)], marks.at[rows], sems.at[4 + partner]))
+    pack(lambda m, c: posted[0, m, c], outlet_mark(kinds), layers, faces, step)
+    select_blocks(lists, faces, (send_even, send_odd))
+
+
+def take_table(pieces, table, sems):
+    copies = []
+    start = 0
+    for k, piece in enumerate(pieces):
+        count = piece.shape[0]
+        copies.append(pltpu.make_async_copy(piece, table.at[pl.ds(start, count)], sems.at[k]))
+        start += count
     for copy in copies:
         copy.start()
     for copy in copies:
         copy.wait()
 
 
-def middle_kernel(bricks, lists, index, gathered, before, kinds, absent, own, own_m, even, odd,
-                  posted, faces, send, rows_out, table, marks, arriving, pops, layers, sums, sems):
+def middle_kernel(bricks, lists, index, gathered, before, kinds, absent, own, even, odd,
+                  posted, faces, send_even, send_odd, rows_out, table, arriving, pops, layers, sums, sems):
     step = pl.program_id(0)
-    slots = lists.shape[0] // 2 - 1
 
     @pl.when(step == 0)
     def _():
-        take_tables(slots, own, own_m, (even, odd), (even, odd), table, marks, sems)
+        take_table((own, even, odd), table, sems)
 
     mean = mean_of(gathered)
-    gather(index, step, table, marks, mean, arriving)
+    gather(bricks, index, step, table, mean, arriving)
 
     def put(member, chunk, value):
         pops[member, chunk] = value
 
     stream(before, kinds, absent, arriving, mean, put)
     collide_all(lambda i, c: pops[i, c], kinds, posted, sums, rows_out, step, bricks, 0.0)
-    pack(lambda m, c: posted[0, m, c], layers, faces, step)
-    select_blocks(lists, faces, send, 0)
-
-
-def last_kernel(slots, index, gathered, before, kinds, absent, own, own_m, even, odd, even_1, odd_1,
-                out, table, marks, arriving, sems):
+    pack(lambda m, c: posted[0, m, c], outlet_mark(kinds), layers, faces, step)
+    select_blocks(lists, faces, (send_even, send_odd))
+
+
+def last_kernel(bricks, index, gathered, before, kinds, absent, own, even, odd, out, table, arriving, sems):
     step = pl.program_id(0)
 
     @pl.when(step == 0)
     def _():
-        take_tables(slots, own, own_m, (even, odd), (even_1, odd_1), table, marks, sems)
+        take_table((own, even, odd), table, sems)
 
     mean = mean_of(gathered)
-    gather(index, step, table, marks, mean, arriving)
+    gather(bricks, index, step, table, mean, arriving)
 
     def put(member, chunk, value):
         start = 128 * chunk
@@ -417,7 +441,7 @@
 
 def params():
     return pltpu.CompilerParams(
-        dimension_semantics=("arbitrary",), vmem_limit_bytes=52 * 1024 * 1024)
+        dimension_semantics=("arbitrary",), vmem_limit_bytes=LIMIT * 1024 * 1024)
 
 
 def whole(*shape):
@@ -443,10 +467,10 @@
         functools.partial(first_kernel, pops.shape[1]),
         grid=(groups,),
         in_specs=[SPEC_SMEM, SPEC_POPS, SPEC_KINDS],
-        out_specs=[SPEC_POSTED, whole(blocks, *BLOCK), whole(blocks, *BLOCK),
-                   whole(2, 2 * slots, *BLOCK), whole(devices, 128)],
-        out_shape=[shape_of(groups, *POSTED), shape_of(blocks, *BLOCK), shape_of(blocks, *BLOCK),
-                   shape_of(2, 2 * slots, *BLOCK), shape_of(devices, 128)],
+        out_specs=[SPEC_POSTED, whole(blocks, *BLOCK), whole(slots, *BLOCK), whole(slots, *BLOCK),
+                   whole(devices, 128)],
+        out_shape=[shape_of(groups, *POSTED), shape_of(blocks, *BLOCK), shape_of(slots, *BLOCK),
+                   shape_of(slots, *BLOCK), shape_of(devices, 128)],
         scratch_shapes=[pltpu.VMEM((6, 128, 128), F32), pltpu.VMEM((2, GROUP, 128), F32)],
         compiler_params=params(),
         name="first_collide",
@@ -456,34 +480,34 @@
 def middle_call(bricks, lists, index, gathered, before, kinds, absent, tables, groups, devices):
     blocks = groups * GROUP * 6
     slots = lists.shape[0] // 2 - 1
-    rows = blocks + 2 * slots
     return pl.pallas_call(
         functools.partial(middle_kernel, bricks),
         grid=(groups,),
         in_specs=[SPEC_SMEM, SPEC_SMEM, whole(devices, 128), SPEC_POSTED, SPEC_KINDS,
-                  SPEC_ABSENT] + [SPEC_ANY] * 4,
-        out_specs=[SPEC_POSTED, whole(blocks, *BLOCK), whole(2, slots, *BLOCK), whole(devices, 128)],
-        out_shape=[shape_of(groups, *POSTED), shape_of(blocks, *BLOCK), shape_of(2, slots, *BLOCK),
-                   shape_of(devices, 128)],
-        scratch_shapes=[pltpu.VMEM((rows,) + BLOCK, F32), pltpu.VMEM((rows,) + BLOCK, F32),
+                  SPEC_ABSENT] + [SPEC_ANY] * 3,
+        out_specs=[SPEC_POSTED, whole(blocks, *BLOCK), whole(slots, *BLOCK), whole(slots, *BLOCK),
+                   whole(devices, 128)],
+        out_shape=[shape_of(groups, *POSTED), shape_of(blocks, *BLOCK), shape_of(slots, *BLOCK),
+                   shape_of(slots, *BLOCK), shape_of(devices, 128)],
+        scratch_shapes=[pltpu.VMEM((blocks + 2 * slots,) + BLOCK, F32),
                         pltpu.VMEM((18, 128, 128), F32), pltpu.VMEM(POSTED, F32),
                         pltpu.VMEM((6, 128, 128), F32), pltpu.VMEM((2, GROUP, 128), F32),
-                        pltpu.SemaphoreType.DMA((6,))],
+                        pltpu.SemaphoreType.DMA((3,))],
         compiler_params=params(),
         name="arrive_collide",
     )(lists, index, gathered, before, kinds, absent, *tables)
 
 
 def last_call(bricks, slots, index, gathered, before, kinds, absent, tables, groups, devices):
-    rows = groups * GROUP * 6 + 2 * slots
+    blocks = groups * GROUP * 6
     return pl.pallas_call(
-        functools.partial(last_kernel, slots),
+        functools.partial(last_kernel, bricks),
         grid=(groups,),
-        in_specs=[SPEC_SMEM, whole(devices, 128), SPEC_POSTED, SPEC_KINDS, SPEC_ABSENT] + [SPEC_ANY] * 6,
+        in_specs=[SPEC_SMEM, whole(devices, 128), SPEC_POSTED, SPEC_KINDS, SPEC_ABSENT] + [SPEC_ANY] * 3,
         out_specs=SPEC_POPS,
         out_shape=shape_of(19, bricks, SITES),
-        scratch_shapes=[pltpu.VMEM((rows,) + BLOCK, F32), pltpu.VMEM((rows,) + BLOCK, F32),
-                        pltpu.VMEM((18, 128, 128), F32), pltpu.SemaphoreType.DMA((6,))],
+        scratch_shapes=[pltpu.VMEM((blocks + 2 * slots,) + BLOCK, F32),
+                        pltpu.VMEM((18, 128, 128), F32), pltpu.SemaphoreType.DMA((3,))],
         compiler_params=params(),
         name="arrive_out",
     )(index, gathered, before, kinds, absent, *tables)
@@ -543,22 +567,22 @@
     bricks = populations.shape[1]
     groups = absent.shape[1] // GROUP
     lists, index = exchange_plan(neighbours, slots, groups * GROUP)
-    posted, faces, marks, send, rows = first_call(lists, populations, site_flags, groups, devices)
-    gathered = share_sums(rows)
-    sent_first = swap(send, devices)
-    excess = jnp.sum(gathered[:, 127])
-    posted, faces, send, rows = middle_call(
-        bricks, lists, index, gathered, posted, site_flags, absent,
-        (faces, marks) + sent_first, groups, devices)
+    posted, faces, *send, rows = first_call(lists, populations, site_flags, groups, devices)
     gathered = share_sums(rows)
     sent = swap(send, devices)
-    return excess, (index, gathered, posted, faces, marks) + sent + sent_first
+    excess = jnp.sum(gathered[:, 127])
+    posted, faces, *send, rows = middle_call(
+        bricks, lists, index, gathered, posted, site_flags, absent,
+        (faces,) + sent, groups, devices)
+    gathered = share_sums(rows)
+    sent = swap(send, devices)
+    return excess, (index, gathered, posted, faces) + sent
 
 
 def finish(devices, slots, site_flags, absent, bricks, state):
-    index, gathered, posted, faces, marks = state[:5]
+    index, gathered, posted = state[:3]
     return last_call(bricks, slots, index, gathered, posted, site_flags, absent,
-                     (faces, marks) + state[5:], absent.shape[1] // GROUP, devices)
+                     state[3:], absent.shape[1] // GROUP, devices)
 
 
 def on_device(devices, populations, neighbours, site_flags):

time: 121 us -> 97.9 us (0.81)
  Pallas kernels: 59 us -> 41.9 us
  waiting for transfers between devices: 19.8 us -> 13.4 us
    pallas_call x1, Pallas kernels: 19.2 us -> 10.4 us  [first_call(): pl.pallas_call(functools.partial(first_kernel, pops.shape[1]), grid=(grou...]
    pallas_call x1, Pallas kernels: 25.5 us -> 19.7 us  [middle_call(): pl.pallas_call(functools.partial(middle_kernel, bricks), grid=(groups,),...]
    ppermute x2, waiting for transfers between devices: 7.86 us -> 2.28 us  [swap(): lax.ppermute(send[1], AXES, odd_pairs)]
    pallas_call x1, Pallas kernels: 14.3 us -> 11.7 us  [last_call(): pl.pallas_call(functools.partial(last_kernel, bricks), grid=(groups,), in...]
    ppermute x2, starting transfers between devices: 0.17 us -> 1.55 us  [swap(): lax.ppermute(send[0], AXES, even_pairs)]
  transfers between devices with their start and end apart: 6 -> 6, of which waited for: 4 -> 3; matrix products, arithmetic and copies ran while one was open for 3% -> 2% of each run, Pallas kernels for 0% -> 0%
where the time goes in v4:
time: 97.9 us; the launch traced here: 97.6 us
  Pallas kernels  41.9 us (43%)
  starting transfers between devices  32.6 us (33%)
  waiting for transfers between devices  13.4 us (14%)
  other arithmetic  5.29 us (5%)
  between operations  2.25 us (2%)
  local copies, waits for them, and re-layouts  2.11 us (2%)
    all_to_all x2, starting transfers between devices, share_sums(): return lax.all_to_all(rows, AXES, 0, 0, tiled=True)  22.3 us
    pallas_call x1, Pallas kernels, middle_call(): pl.pallas_call(functools.partial(middle_kernel, bricks), grid=(groups,),...  19.7 us
    pallas_call x1, Pallas kernels, last_call(): pl.pallas_call(functools.partial(last_kernel, bricks), grid=(groups,), in...  11.7 us
    all_to_all x2, waiting for transfers between devices, share_sums(): return lax.all_to_all(rows, AXES, 0, 0, tiled=True)  11.1 us
    pallas_call x1, Pallas kernels, first_call(): pl.pallas_call(functools.partial(first_kernel, pops.shape[1]), grid=(grou...  10.4 us
    ppermute x2, starting transfers between devices, swap(): lax.ppermute(send[1], AXES, odd_pairs)  8.83 us
    ppermute x2, waiting for transfers between devices, swap(): lax.ppermute(send[1], AXES, odd_pairs)  2.28 us
  transfers between devices with their start and end apart: 6, of which 3 were waited for; matrix products, arithmetic and copies ran while one was open for 2% of the time, Pallas kernels for 0%

profile of v4, /device:TPU:1, one launch (start us, length us, event | category | flops | bytes accessed | tf_op | source)
XLA Modules:
  0.0 97.6 jit_solution(4238625447374627504)
XLA Ops:
  0.0 0.0 copy-start.5
  0.0 0.0 copy-start.4
  0.0 0.0 copy-start.1
  0.0 0.7 iota_compare_fusion.11
  0.7 0.7 add_select_fusion.2
  1.5 0.7 add_select_fusion.3
  2.2 0.3 and_reduce_fusion.3
  2.5 0.7 convert_reduce_fusion.2
  4.6 0.1 copy.21
  4.7 0.1 reshape.170
  4.8 0.1 select_reduce_fusion.12
  4.9 0.1 copy.20
  5.0 0.1 reshape.169
  5.1 0.1 select_reduce_fusion.13
  5.2 0.1 select_reduce_fusion.14
  5.3 0.1 pad_add_fusion.1.lists
  5.4 0.0 copy-start.6
  5.4 10.4 %first_collide.3 = (f32[3,19,32,8,128]{4,3,2,1,0:T(8,128)}, f32[144,16,128]{2,1,0:T(8,128)S(1)}, f32[32,16,128]{2,1,0:T(8,128)S(1)}, f32[32,16,128]{2,1,0:T(8,128)S(1)}, f32[128,128]{1,0:T(8,128)}) custom-call(s32[66]{0:T(128)S(1)} %pad_add_fusion.1.lists, f32[19,20,4096]{2,1,0:T(8,128)} %bitcast.30, s32[20,4096]{1,0:T(8,128)} %kinds.3), custom_call_target="tpu_custom_call" | custom-call | tf_op jit(solution)/shard_map/first_collide/pallas_call | solution.py:466
  15.8 0.0 copy-start
  15.8 1.1 %copy-done = f32[144,16,128]{2,1,0:T(8,128)} copy-done((f32[144,16,128]{2,1,0:T(8,128)}, f32[144,16,128]{2,1,0:T(8,128)S(1)}, u32[]{:S(2)}) %copy-start) | copy-done | bytes 1179672
  16.9 11.5 %all-to-all-start.2 = ((f32[128,1,128]{2,1,0:T(1,128)}), f32[128,1,128]{2,1,0:T(1,128)S(1)}, u32[]{:S(2)}, u32[]{:S(2)}) async-start(f32[128,1,128]{2,1,0:T(1,128)} %bitcast.16), calls=%async_computation.2 | async-start | bytes 131072 | tf_op jit(solution)/shard_map/all_to_all | solution.py:517
  28.4 1.5 %collective-permute-start.4 = (f32[32,16,128]{2,1,0:T(8,128)S(1)}, f32[32,16,128]{2,1,0:T(8,128)S(1)}, u32[]{:S(2)}, u32[]{:S(2)}) collective-permute-start(f32[32,16,128]{2,1,0:T(8,128)S(1)} %get-tuple-element.74), channel_id=1, source_target_pairs={{0,1},{1,0},{2,3},{3,2},{4,5},{5,4},{6,7},{7,6},{8,9},{9,8},{10,11... | collective-permute-start | bytes 786440 | tf_op jit(solution)/shard_map/ppermute | solution.py:524
  29.9 4.2 %collective-permute-start.5 = (f32[32,16,128]{2,1,0:T(8,128)S(1)}, f32[32,16,128]{2,1,0:T(8,128)S(1)}, u32[]{:S(2)}, u32[]{:S(2)}) collective-permute-start(f32[32,16,128]{2,1,0:T(8,128)S(1)} %get-tuple-element.75), channel_id=1, source_target_pairs={{1,2},{3,4},{5,6},{7,8},{9,10},{11,12},{13,14},{15,16},{17,18},{19... | collective-permute-start | bytes 786440 | tf_op jit(solution)/shard_map/ppermute | solution.py:524
  34.1 0.1 eq.170
  34.2 0.1 fusion.2
  34.3 0.1 select_reduce_fusion.10
  34.4 0.2 select_reduce_fusion.8
  34.7 0.1 add.121
  34.8 0.1 eq.167
  34.9 0.1 fusion.3
  35.0 0.1 select_reduce_fusion.11
  35.2 0.2 select_reduce_fusion.9
  35.4 0.1 add.116
  35.5 0.0 copy-done.5
  35.5 0.0 copy-done.4
  35.6 0.1 copy.23
  35.6 0.1 reshape.166.index
  35.7 2.5 %all-to-all-done.2 = f32[128,1,128]{2,1,0:T(1,128)S(1)} async-done(((f32[128,1,128]{2,1,0:T(1,128)}), f32[128,1,128]{2,1,0:T(1,128)S(1)}, u32[]{:S(2)}, u32[]{:S(2)}) %all-to-all-start.2) | async-done | bytes 65568 | tf_op jit(solution)/shard_map/all_to_all | solution.py:517
  38.3 0.0 collective-permute-done.4.even
  38.3 2.3 %collective-permute-done.5.odd = f32[32,16,128]{2,1,0:T(8,128)S(1)} collective-permute-done((f32[32,16,128]{2,1,0:T(8,128)S(1)}, f32[32,16,128]{2,1,0:T(8,128)S(1)}, u32[]{:S(2)}, u32[]{:S(2)}) %collective-permute-start.5) | collective-permute-done | bytes 262176 | tf_op jit(solution)/shard_map/ppermute | solution.py:524
  40.6 0.1 broadcast_in_dim.181.absent
  40.7 0.0 copy-done.1
  40.7 19.7 %arrive_collide.3 = (f32[3,19,32,8,128]{4,3,2,1,0:T(8,128)}, f32[144,16,128]{2,1,0:T(8,128)S(1)}, f32[32,16,128]{2,1,0:T(8,128)S(1)}, f32[32,16,128]{2,1,0:T(8,128)S(1)}, f32[128,128]{1,0:T(8,128)}) custom-call(s32[66]{0:T(128)S(1)} %pad_add_fusion.1.lists, s32[432]{0:T(512)S(1)} %reshape.166.index, f32[128,128]{1,0:T(8,128)S(1)} %bitcast.25, ...), custom_call_target="tpu_custom_call" | custom-call | tf_op jit(solution)/shard_map/arrive_collide/pallas_call | solution.py:483
  60.5 0.1 collective-permute-start.6
  60.5 4.6 %collective-permute-start.7 = (f32[32,16,128]{2,1,0:T(8,128)S(1)}, f32[32,16,128]{2,1,0:T(8,128)S(1)}, u32[]{:S(2)}, u32[]{:S(2)}) collective-permute-start(f32[32,16,128]{2,1,0:T(8,128)S(1)} %get-tuple-element.80), channel_id=1, source_target_pairs={{1,2},{3,4},{5,6},{7,8},{9,10},{11,12},{13,14},{15,16},{17,18},{19... | collective-permute-start | bytes 786440 | tf_op jit(solution)/shard_map/ppermute | solution.py:524
  65.2 10.8 %all-to-all-start.3 = ((f32[128,1,128]{2,1,0:T(1,128)}), f32[128,1,128]{2,1,0:T(1,128)S(1)}, u32[]{:S(2)}, u32[]{:S(2)}) async-start(f32[128,1,128]{2,1,0:T(1,128)} %bitcast.20), calls=%async_computation.3 | async-start | bytes 131072 | tf_op jit(solution)/shard_map/all_to_all | solution.py:517
  75.9 0.7 slice_reduce_fusion
  77.3 8.5 %all-to-all-done.3 = f32[128,1,128]{2,1,0:T(1,128)S(1)} async-done(((f32[128,1,128]{2,1,0:T(1,128)}), f32[128,1,128]{2,1,0:T(1,128)S(1)}, u32[]{:S(2)}, u32[]{:S(2)}) %all-to-all-start.3) | async-done | bytes 65568 | tf_op jit(solution)/shard_map/all_to_all | solution.py:517
  85.8 0.0 collective-permute-done.6
  85.8 0.0 collective-permute-done.7
  85.8 0.0 copy-done.6
  85.8 11.7 %conditional.1 = (f32[19,20,4096]{2,1,0:T(8,128)}) conditional(s32[]{:T(128)} %convert_element_type.106, (f32[128,1,128]{2,1,0:T(1,128)S(1)}, s32[432]{0:T(512)S(1)}, f32[3,19,32,8,128]{4,3,2,1,0:T(8,128)}, s32[20,4096]{1,0:T(8,128)S(1)}, s32[18,24,128]{2,1,0:T(8,128)S(1)}, /*index=5*/f32[144,16,128]{2,1,0:T(8,128)S(1)}, ...), branch_computations={%region_15.16_spmd, %region_16.31_spmd} | conditional | flops 709819 | bytes 23989792 | solution.py:604
  85.8 11.7 %arrive_out.2 = f32[19,20,4096]{2,1,0:T(8,128)} custom-call(s32[432]{0:T(512)S(1)} %get-tuple-element.37.index, f32[128,128]{1,0:T(8,128)S(1)} %bitcast.32, f32[3,19,32,8,128]{4,3,2,1,0:T(8,128)} %get-tuple-element.39.before, s32[20,4096]{1,0:T(8,128)S(1)} %get-tuple-element.40.kinds, s32[18,24,128]{2,1,0:T(8,128)S(1)} %get-tuple-element.41.absent, ...), custom_call_target="tpu_custom_call" | custom-call | tf_op jit(solution)/shard_map/cond/branch_0_fun/arrive_out/pallas_call | solution.py:503
  (14 shorter events, 0.1 us)
Async XLA Ops:
  0.0 35.5 %copy-start.5 = (s32[18]{0:T(128)S(1)}, s32[18]{0:T(128)}, u32[]{:S(2)}) copy-start(s32[18]{0:T(128)} %constant.101.clone) | copy-start | bytes 220
  0.0 35.5 %copy-start.4 = (s32[20,18]{1,0:T(8,128)S(1)}, s32[20,18]{1,0:T(8,128)}, u32[]{:S(2)}) copy-start(s32[20,18]{1,0:T(8,128)} %param.10) | copy-start | bytes 4324
  0.0 40.7 %copy-start.1 = (s32[20,4096]{1,0:T(8,128)S(1)}, s32[20,4096]{1,0:T(8,128)}, u32[]{:S(2)}) copy-start(s32[20,4096]{1,0:T(8,128)} %kinds.3) | copy-start | bytes 983044
  5.4 80.4 %copy-start.6 = (s32[18]{0:T(128)S(1)}, s32[18]{0:T(128)}, u32[]{:S(2)}) copy-start(s32[18]{0:T(128)} %constant.102.clone) | copy-start | bytes 220
  15.8 1.1 %copy-start = (f32[144,16,128]{2,1,0:T(8,128)}, f32[144,16,128]{2,1,0:T(8,128)S(1)}, u32[]{:S(2)}) copy-start(f32[144,16,128]{2,1,0:T(8,128)S(1)} %get-tuple-element.73.own) | copy-start | bytes 3538948
  16.9 21.4 %all-to-all-start.2 = ((f32[128,1,128]{2,1,0:T(1,128)}), f32[128,1,128]{2,1,0:T(1,128)S(1)}, u32[]{:S(2)}, u32[]{:S(2)}) async-start(f32[128,1,128]{2,1,0:T(1,128)} %bitcast.16), calls=%async_computation.2 | async-start | bytes 131072 | tf_op jit(solution)/shard_map/all_to_all | solution.py:517
  28.4 9.9 %collective-permute-start.4 = (f32[32,16,128]{2,1,0:T(8,128)S(1)}, f32[32,16,128]{2,1,0:T(8,128)S(1)}, u32[]{:S(2)}, u32[]{:S(2)}) collective-permute-start(f32[32,16,128]{2,1,0:T(8,128)S(1)} %get-tuple-element.74), channel_id=1, source_target_pairs={{0,1},{1,0},{2,3},{3,2},{4,5},{5,4},{6,7},{7,6},{8,9},{9,8},{10,11... | collective-permute-start | bytes 786440 | tf_op jit(solution)/shard_map/ppermute | solution.py:524
  29.9 10.7 %collective-permute-start.5 = (f32[32,16,128]{2,1,0:T(8,128)S(1)}, f32[32,16,128]{2,1,0:T(8,128)S(1)}, u32[]{:S(2)}, u32[]{:S(2)}) collective-permute-start(f32[32,16,128]{2,1,0:T(8,128)S(1)} %get-tuple-element.75), channel_id=1, source_target_pairs={{1,2},{3,4},{5,6},{7,8},{9,10},{11,12},{13,14},{15,16},{17,18},{19... | collective-permute-start | bytes 786440 | tf_op jit(solution)/shard_map/ppermute | solution.py:524
  60.5 25.4 %collective-permute-start.6 = (f32[32,16,128]{2,1,0:T(8,128)S(1)}, f32[32,16,128]{2,1,0:T(8,128)S(1)}, u32[]{:S(2)}, u32[]{:S(2)}) collective-permute-start(f32[32,16,128]{2,1,0:T(8,128)S(1)} %get-tuple-element.79), channel_id=1, source_target_pairs={{0,1},{1,0},{2,3},{3,2},{4,5},{5,4},{6,7},{7,6},{8,9},{9,8},{10,11... | collective-permute-start | bytes 786440 | tf_op jit(solution)/shard_map/ppermute | solution.py:524
  60.5 25.3 %collective-permute-start.7 = (f32[32,16,128]{2,1,0:T(8,128)S(1)}, f32[32,16,128]{2,1,0:T(8,128)S(1)}, u32[]{:S(2)}, u32[]{:S(2)}) collective-permute-start(f32[32,16,128]{2,1,0:T(8,128)S(1)} %get-tuple-element.80), channel_id=1, source_target_pairs={{1,2},{3,4},{5,6},{7,8},{9,10},{11,12},{13,14},{15,16},{17,18},{19... | collective-permute-start | bytes 786440 | tf_op jit(solution)/shard_map/ppermute | solution.py:524
  65.2 20.6 %all-to-all-start.3 = ((f32[128,1,128]{2,1,0:T(1,128)}), f32[128,1,128]{2,1,0:T(1,128)S(1)}, u32[]{:S(2)}, u32[]{:S(2)}) async-start(f32[128,1,128]{2,1,0:T(1,128)} %bitcast.20), calls=%async_computation.3 | async-start | bytes 131072 | tf_op jit(solution)/shard_map/all_to_all | solution.py:517

commit v5 on v4

--- a/solution.py
+++ b/solution.py
@@ -39,6 +39,7 @@
     _m = SPEEDS[OPP[_d + 1]]
     _lead = [k for k in range(3) if _m[k]][0]
     COLUMN_FACE.append(face_of(_m, _lead))
+GIVEN = [COLUMN_FACE[OPP[_d + 1] - 1] for _d in range(18)]
 
 
 def iota(shape, dim):
@@ -173,15 +174,29 @@
     return jnp.where((slot < 5) & (marks != 0.0), block * jnp.concatenate([mean, mean], axis=0), block)
 
 
-def gather(bricks, index, step, table, mean, arriving):
-    def brick(j, carry):
-        base = (step * GROUP + j) * 18
-        for column in range(18):
-            block = scaled(table[index[base + column]], COLUMN_FACE[column], mean)
-            arriving[column, pl.ds(j, BRICK, stride=8), :] = block
-        return carry
-
-    lax.fori_loop(0, jnp.minimum(GROUP, bricks - step * GROUP), brick, 0)
+def gather(bricks, index, step, gathered, table, mean, arriving):
+    me = index[index.shape[0] - 1]
+    near = jnp.abs(iota(gathered.shape, 0) - me) <= 1
+    outlets = jnp.max(jnp.where(near & (iota(gathered.shape, 1) == 126), gathered[...], 0.0))
+    real = jnp.minimum(GROUP, bricks - step * GROUP)
+
+    def fetch(scale):
+        def brick(j, carry):
+            base = (step * GROUP + j) * 18
+            for column in range(18):
+                block = scale(table[index[base + column]], COLUMN_FACE[column])
+                arriving[column, pl.ds(j, BRICK, stride=8), :] = block
+            return carry
+
+        lax.fori_loop(0, real, brick, 0)
+
+    @pl.when(outlets > 0.0)
+    def _():
+        fetch(lambda block, face: scaled(block, face, mean))
+
+    @pl.when(outlets == 0.0)
+    def _():
+        fetch(lambda block, face: block)
 
 
 def stream(posted, kinds, absent, arriving, mean, put):
@@ -236,10 +251,12 @@
                 here = (lane & 15) == enter
                 block = arriving[column, rows, :]
                 for h in range(2):
-                    new = roll(block, 16 * cy + enter - slot - 8 * h, 1)
                     if cy and h == (1 if cy > 0 else 0):
-                        other = roll(block, 16 * cy + enter - slot - 8 * (1 - h), 1)
-                        new = jnp.where(lane < 16 if cy > 0 else lane >= 112, other, new)
+                        half_of = jnp.where(lane < 16 if cy > 0 else lane >= 112, 1 - h, h)
+                        origin = ((lane - 16 * cy) & 112) + slot + 8 * half_of
+                        new = jnp.take_along_axis(block, origin, axis=1, mode="promise_in_bounds")
+                    else:
+                        new = roll(block, 16 * cy + enter - slot - 8 * h, 1)
                     new = jnp.where(gone, mirror[h], new)
                     parts[h] = jnp.where(here, new, parts[h])
             if cy and cz:
@@ -324,36 +341,65 @@
             posted[0, i, c] = out[i]
         counted = real & (kind != 1)
         return (carry[0] + jnp.where(counted, density, 0.0),
-                carry[1] + jnp.where(counted, 1.0, 0.0))
+                carry[1] + jnp.where(counted, 1.0, 0.0),
+                carry[2] + jnp.where(real & (kind == 3), 1.0, 0.0))
 
     zero = jnp.zeros((GROUP, 128), F32)
-    total, count = lax.fori_loop(0, CHUNKS, chunk, (zero, zero), unroll=4)
+    total = lax.fori_loop(0, CHUNKS, chunk, (zero, zero, zero), unroll=4)
 
     @pl.when(step == 0)
     def _():
-        sums[0] = total
-        sums[1] = count
+        for k in range(3):
+            sums[k] = total[k]
 
     @pl.when(step > 0)
     def _():
-        sums[0] += total
-        sums[1] += count
+        for k in range(3):
+            sums[k] += total[k]
 
     @pl.when(step == pl.num_programs(0) - 1)
     def _():
         lane = iota(rows_out.shape, 1)
         both = jnp.where(lane < 64, jnp.sum(sums[0]), jnp.sum(sums[1]))
+        both = jnp.where(lane == 126, jnp.sum(sums[2]), both)
         rows_out[...] = jnp.where(lane == 127, excess, both)
 
 
+def plan_sends(neighbours, me, lists):
+    bricks = neighbours.shape[0]
+    low = me * bricks
+    high = low + bricks
+    following = (me & 1) * 128
+    preceding = 128 - following
+
+    def brick(b, counts):
+        ahead, behind = counts
+        near = [neighbours[b, c] for c in range(18)]
+        held = [jnp.where(v < 0, 1 << 30, v) for v in near]
+        for face in range(6):
+            columns = [c for c in range(18) if GIVEN[c] == face]
+            last = functools.reduce(jnp.maximum, [near[c] for c in columns])
+            first = functools.reduce(jnp.minimum, [held[c] for c in columns])
+            lists[following + ahead] = b * 6 + face
+            lists[preceding + behind] = b * 6 + face
+            ahead += jnp.where(last >= high, 1, 0)
+            behind += jnp.where(first < low, 1, 0)
+        return ahead, behind
+
+    ahead, behind = lax.fori_loop(0, bricks, brick, (jnp.int32(0), jnp.int32(0)))
+    lists[following + 127] = ahead
+    lists[preceding + 127] = behind
+
+
 def select_blocks(lists, table, send):
-    slots = lists.shape[0] // 2 - 1
+    slots = send[0].shape[0]
 
     @pl.when(pl.program_id(0) == pl.num_programs(0) - 1)
     def _():
         def slot(s, carry):
             for partner in range(2):
-                send[partner][s] = table[lists[partner * (slots + 1) + s]]
+                listed = s < lists[128 * partner + 127]
+                send[partner][s] = table[jnp.where(listed, lists[128 * partner + s], 0)]
             return carry
 
         lax.fori_loop(0, slots, slot, 0, unroll=4)
@@ -369,10 +415,16 @@
     return mark
 
 
-def first_kernel(bricks, lists, pops, kinds, posted, faces, send_even, send_odd, rows_out, layers, sums):
+def first_kernel(bricks, me, neighbours, pops, kinds, posted, faces, send_even, send_odd, rows_out, lists,
+                 layers, sums):
     step = pl.program_id(0)
-    slots = lists.shape[0] // 2 - 1
-    excess = (lists[slots] + lists[2 * slots + 1]).astype(F32)
+    slots = send_even.shape[0]
+
+    @pl.when(step == 0)
+    def _():
+        plan_sends(neighbours, me[0], lists)
+
+    excess = jnp.where(jnp.maximum(lists[127], lists[255]) > slots, 1.0, 0.0)
 
     def load(i, c):
         return pops[i, :, pl.ds(pl.multiple_of(128 * c, 128), 128)]
@@ -404,7 +456,7 @@
         take_table((own, even, odd), table, sems)
 
     mean = mean_of(gathered)
-    gather(bricks, index, step, table, mean, arriving)
+    gather(bricks, index, step, gathered, table, mean, arriving)
 
     def put(member, chunk, value):
         pops[member, chunk] = value
@@ -423,7 +475,7 @@
         take_table((own, even, odd), table, sems)
 
     mean = mean_of(gathered)
-    gather(bricks, index, step, table, mean, arriving)
+    gather(bricks, index, step, gathered, table, mean, arriving)
 
     def put(member, chunk, value):
         start = 128 * chunk
@@ -460,26 +512,25 @@
     return jax.ShapeDtypeStruct(shape, F32)
 
 
-def first_call(lists, pops, kinds, groups, devices):
+def first_call(slots, me, neighbours, pops, kinds, groups, devices):
     blocks = groups * GROUP * 6
-    slots = lists.shape[0] // 2 - 1
     return pl.pallas_call(
         functools.partial(first_kernel, pops.shape[1]),
         grid=(groups,),
-        in_specs=[SPEC_SMEM, SPEC_POPS, SPEC_KINDS],
+        in_specs=[SPEC_SMEM, SPEC_SMEM, SPEC_POPS, SPEC_KINDS],
         out_specs=[SPEC_POSTED, whole(blocks, *BLOCK), whole(slots, *BLOCK), whole(slots, *BLOCK),
-                   whole(devices, 128)],
-        out_shape=[shape_of(groups, *POSTED), shape_of(blocks, *BLOCK), shape_of(slots, *BLOCK),
-                   shape_of(slots, *BLOCK), shape_of(devices, 128)],
-        scratch_shapes=[pltpu.VMEM((6, 128, 128), F32), pltpu.VMEM((2, GROUP, 128), F32)],
+                   whole(devices, 128), SPEC_SMEM],
+        out_shape=[shape_of(groups, *POSTED), pltpu.HBM((blocks,) + BLOCK, F32), shape_of(slots, *BLOCK),
+                   shape_of(slots, *BLOCK), shape_of(devices, 128),
+                   jax.ShapeDtypeStruct((256,), jnp.int32)],
+        scratch_shapes=[pltpu.VMEM((6, 128, 128), F32), pltpu.VMEM((3, GROUP, 128), F32)],
         compiler_params=params(),
         name="first_collide",
-    )(lists, pops, kinds)
-
-
-def middle_call(bricks, lists, index, gathered, before, kinds, absent, tables, groups, devices):
+    )(me, neighbours, pops, kinds)
+
+
+def middle_call(bricks, slots, lists, index, gathered, before, kinds, absent, tables, groups, devices):
     blocks = groups * GROUP * 6
-    slots = lists.shape[0] // 2 - 1
     return pl.pallas_call(
         functools.partial(middle_kernel, bricks),
         grid=(groups,),
@@ -487,11 +538,11 @@
                   SPEC_ABSENT] + [SPEC_ANY] * 3,
         out_specs=[SPEC_POSTED, whole(blocks, *BLOCK), whole(slots, *BLOCK), whole(slots, *BLOCK),
                    whole(devices, 128)],
-        out_shape=[shape_of(groups, *POSTED), shape_of(blocks, *BLOCK), shape_of(slots, *BLOCK),
+        out_shape=[shape_of(groups, *POSTED), pltpu.HBM((blocks,) + BLOCK, F32), shape_of(slots, *BLOCK),
                    shape_of(slots, *BLOCK), shape_of(devices, 128)],
         scratch_shapes=[pltpu.VMEM((blocks + 2 * slots,) + BLOCK, F32),
                         pltpu.VMEM((18, 128, 128), F32), pltpu.VMEM(POSTED, F32),
-                        pltpu.VMEM((6, 128, 128), F32), pltpu.VMEM((2, GROUP, 128), F32),
+                        pltpu.VMEM((6, 128, 128), F32), pltpu.VMEM((3, GROUP, 128), F32),
                         pltpu.SemaphoreType.DMA((3,))],
         compiler_params=params(),
         name="arrive_collide",
@@ -529,7 +580,7 @@
     return jnp.sum(jnp.where(iota((count, count), 1) < iota((count, count), 0), used[None, :], 0), axis=1)
 
 
-def exchange_plan(neighbours, slots, padded):
+def arrival_plan(neighbours, slots, padded):
     bricks = neighbours.shape[0]
     blocks = bricks * 6
     me = lax.axis_index(AXES)
@@ -539,20 +590,11 @@
     preceding = present & (local < 0)
     first = me % 2 == 0
     read = jnp.asarray(np.array(COLUMN_FACE, np.int32))
-    given = jnp.asarray(np.array([COLUMN_FACE[OPP[d + 1] - 1] for d in range(18)], np.int32))
-    faces = jnp.arange(6, dtype=jnp.int32)
     index = local * 6 + read[None, :]
-    lists = []
     for partner in range(2):
         is_next = first if partner == 0 else ~first
         there = jnp.where(is_next, following, preceding)
         spot = (local + jnp.where(is_next, -bricks, bricks)) * 6 + read[None, :]
-        used = jnp.any(there[:, :, None] & (given[:, None] == faces[None, :])[None], axis=1)
-        used = used.astype(jnp.int32).reshape(-1)
-        order = jnp.where(used == 1, rank(used), blocks)
-        chosen = order[None, :] == iota((slots, blocks), 0)
-        lists.append(jnp.sum(jnp.where(chosen, iota((slots, blocks), 1), 0), axis=1))
-        lists.append(jnp.where(jnp.sum(used) > slots, 1, 0)[None])
         flat = jnp.where(there, spot, -1).reshape(-1)
         hits = flat[:, None] == iota((flat.shape[0], blocks), 1)
         ranks = rank(jnp.any(hits, axis=0).astype(jnp.int32))
@@ -560,19 +602,21 @@
         index = jnp.where(there, padded * 6 + partner * slots + at.reshape(bricks, 18), index)
     index = jnp.where(present, index, 0)
     index = jnp.pad(index, ((0, padded - bricks), (0, 0))).reshape(-1)
-    return jnp.concatenate(lists), index
+    return jnp.concatenate([index, me[None]])
 
 
 def begin(devices, slots, populations, neighbours, site_flags, absent):
     bricks = populations.shape[1]
     groups = absent.shape[1] // GROUP
-    lists, index = exchange_plan(neighbours, slots, groups * GROUP)
-    posted, faces, *send, rows = first_call(lists, populations, site_flags, groups, devices)
+    me = lax.axis_index(AXES).astype(jnp.int32).reshape(1)
+    index = arrival_plan(neighbours, slots, groups * GROUP)
+    posted, faces, *send, rows, lists = first_call(
+        slots, me, neighbours, populations, site_flags, groups, devices)
     gathered = share_sums(rows)
     sent = swap(send, devices)
     excess = jnp.sum(gathered[:, 127])
     posted, faces, *send, rows = middle_call(
-        bricks, lists, index, gathered, posted, site_flags, absent,
+        bricks, slots, lists, index, gathered, posted, site_flags, absent,
         (faces,) + sent, groups, devices)
     gathered = share_sums(rows)
     sent = swap(send, devices)

time: 97.9 us -> 94 us (0.960)
  other arithmetic: 5.29 us -> 1.79 us
  Pallas kernels: 41.9 us -> 44.4 us
  local copies, waits for them, and re-layouts: 2.11 us -> 0.67 us
  between operations: 2.25 us -> 0.86 us
    pallas_call x1, Pallas kernels: 10.4 us -> 13.2 us  [first_call(): pl.pallas_call(functools.partial(first_kernel, pops.shape[1]), grid=(grou...]
    select_n x5 -> x2, other arithmetic: 1.46 us -> 0.03 us  [the longest x1 0.02 us: arrival_plan(): index = jnp.where(present, index, 0)]
    unnamed x10 -> x6, local copies, waits for them, and re-layouts: 1.07 us -> 0.01 us
where the time goes in v5:
time: 94 us; the launch traced here: 93.7 us
  Pallas kernels  44.4 us (47%)
  starting transfers between devices  32.6 us (35%)
  waiting for transfers between devices  13.3 us (14%)
  other arithmetic  1.79 us (2%)
    all_to_all x2, starting transfers between devices, share_sums(): return lax.all_to_all(rows, AXES, 0, 0, tiled=True)  22.3 us
    pallas_call x1, Pallas kernels, middle_call(): pl.pallas_call(functools.partial(middle_kernel, bricks), grid=(groups,),...  19.3 us
    pallas_call x1, Pallas kernels, first_call(): pl.pallas_call(functools.partial(first_kernel, pops.shape[1]), grid=(grou...  13.2 us
    pallas_call x1, Pallas kernels, last_call(): pl.pallas_call(functools.partial(last_kernel, bricks), grid=(groups,), in...  11.9 us
    all_to_all x2, waiting for transfers between devices, share_sums(): return lax.all_to_all(rows, AXES, 0, 0, tiled=True)  11 us
    ppermute x2, starting transfers between devices, swap(): lax.ppermute(send[1], AXES, odd_pairs)  8.83 us
    ppermute x2, waiting for transfers between devices, swap(): lax.ppermute(send[1], AXES, odd_pairs)  2.28 us
  transfers between devices with their start and end apart: 6, of which 3 were waited for; matrix products, arithmetic and copies ran while one was open for 2% of the time, Pallas kernels for 0%

profile of v5, /device:TPU:1, one launch (start us, length us, event | category | flops | bytes accessed | tf_op | source)
XLA Modules:
  0.0 93.7 jit_solution(14413844162471848168)
XLA Ops:
  0.0 0.0 copy-start.4
  0.0 0.0 copy-start.3
  0.0 0.0 copy-start
  0.0 13.2 %first_collide.3 = (f32[3,19,32,8,128]{4,3,2,1,0:T(8,128)}, f32[144,16,128]{2,1,0:T(8,128)}, f32[32,16,128]{2,1,0:T(8,128)S(1)}, f32[32,16,128]{2,1,0:T(8,128)S(1)}, f32[128,128]{1,0:T(8,128)}, /*index=5*/s32[256]{0:T(256)S(1)}) custom-call(s32[1]{0:T(128)} %bitcast.11.me, s32[20,18]{1,0:T(8,128)} %neighbours.1, f32[19,20,4096]{2,1,0:T(8,128)} %bitcast.28, ...), custom_call_target="tpu_custom_call" | custom-call | tf_op jit(solution)/shard_map/first_collide/pallas_call | solution.py:517
  13.3 11.5 %all-to-all-start.2 = ((f32[128,1,128]{2,1,0:T(1,128)}), f32[128,1,128]{2,1,0:T(1,128)S(1)}, u32[]{:S(2)}, u32[]{:S(2)}) async-start(f32[128,1,128]{2,1,0:T(1,128)} %bitcast.14), calls=%async_computation.2 | async-start | bytes 131072 | tf_op jit(solution)/shard_map/all_to_all | solution.py:568
  24.8 1.5 %collective-permute-start.4 = (f32[32,16,128]{2,1,0:T(8,128)S(1)}, f32[32,16,128]{2,1,0:T(8,128)S(1)}, u32[]{:S(2)}, u32[]{:S(2)}) collective-permute-start(f32[32,16,128]{2,1,0:T(8,128)S(1)} %get-tuple-element.74), channel_id=1, source_target_pairs={{0,1},{1,0},{2,3},{3,2},{4,5},{5,4},{6,7},{7,6},{8,9},{9,8},{10,11... | collective-permute-start | bytes 786440 | tf_op jit(solution)/shard_map/ppermute | solution.py:575
  26.2 4.2 %collective-permute-start.5 = (f32[32,16,128]{2,1,0:T(8,128)S(1)}, f32[32,16,128]{2,1,0:T(8,128)S(1)}, u32[]{:S(2)}, u32[]{:S(2)}) collective-permute-start(f32[32,16,128]{2,1,0:T(8,128)S(1)} %get-tuple-element.75), channel_id=1, source_target_pairs={{1,2},{3,4},{5,6},{7,8},{9,10},{11,12},{13,14},{15,16},{17,18},{19... | collective-permute-start | bytes 786440 | tf_op jit(solution)/shard_map/ppermute | solution.py:575
  30.5 0.0 copy-done.3
  30.5 0.1 copy.16
  30.6 0.0 copy-done.4
  30.6 0.1 eq.53
  30.7 0.1 fusion.2
  30.9 0.1 select_reduce_fusion.6
  31.0 0.2 select_reduce_fusion.4
  31.2 0.1 eq.50
  31.3 0.1 fusion.3
  31.5 0.1 select_reduce_fusion.7
  31.6 0.2 select_reduce_fusion.5
  31.8 0.1 add.118
  31.9 0.1 add.123
  32.1 0.1 reshape.65
  32.2 0.1 pad_add_fusion.1.index
  32.2 2.4 %all-to-all-done.2 = f32[128,1,128]{2,1,0:T(1,128)S(1)} async-done(((f32[128,1,128]{2,1,0:T(1,128)}), f32[128,1,128]{2,1,0:T(1,128)S(1)}, u32[]{:S(2)}, u32[]{:S(2)}) %all-to-all-start.2) | async-done | bytes 65568 | tf_op jit(solution)/shard_map/all_to_all | solution.py:568
  34.7 0.0 collective-permute-done.4.even
  34.7 2.3 %collective-permute-done.5.odd = f32[32,16,128]{2,1,0:T(8,128)S(1)} collective-permute-done((f32[32,16,128]{2,1,0:T(8,128)S(1)}, f32[32,16,128]{2,1,0:T(8,128)S(1)}, u32[]{:S(2)}, u32[]{:S(2)}) %collective-permute-start.5) | collective-permute-done | bytes 262176 | tf_op jit(solution)/shard_map/ppermute | solution.py:575
  37.0 0.1 broadcast_in_dim.106.absent
  37.1 0.0 copy-done
  37.1 19.3 %arrive_collide.3 = (f32[3,19,32,8,128]{4,3,2,1,0:T(8,128)}, f32[144,16,128]{2,1,0:T(8,128)}, f32[32,16,128]{2,1,0:T(8,128)S(1)}, f32[32,16,128]{2,1,0:T(8,128)S(1)}, f32[128,128]{1,0:T(8,128)}) custom-call(s32[256]{0:T(256)S(1)} %get-tuple-element.71.lists, s32[433]{0:T(512)S(1)} %pad_add_fusion.1.index, f32[128,128]{1,0:T(8,128)S(1)} %bitcast.23, ...), custom_call_target="tpu_custom_call" | custom-call | tf_op jit(solution)/shard_map/arrive_collide/pallas_call | solution.py:534
  56.4 0.1 collective-permute-start.6
  56.5 4.6 %collective-permute-start.7 = (f32[32,16,128]{2,1,0:T(8,128)S(1)}, f32[32,16,128]{2,1,0:T(8,128)S(1)}, u32[]{:S(2)}, u32[]{:S(2)}) collective-permute-start(f32[32,16,128]{2,1,0:T(8,128)S(1)} %get-tuple-element.80), channel_id=1, source_target_pairs={{1,2},{3,4},{5,6},{7,8},{9,10},{11,12},{13,14},{15,16},{17,18},{19... | collective-permute-start | bytes 786440 | tf_op jit(solution)/shard_map/ppermute | solution.py:575
  61.1 10.8 %all-to-all-start.3 = ((f32[128,1,128]{2,1,0:T(1,128)}), f32[128,1,128]{2,1,0:T(1,128)S(1)}, u32[]{:S(2)}, u32[]{:S(2)}) async-start(f32[128,1,128]{2,1,0:T(1,128)} %bitcast.18), calls=%async_computation.3 | async-start | bytes 131072 | tf_op jit(solution)/shard_map/all_to_all | solution.py:568
  71.9 0.7 slice_reduce_fusion
  73.2 8.5 %all-to-all-done.3 = f32[128,1,128]{2,1,0:T(1,128)S(1)} async-done(((f32[128,1,128]{2,1,0:T(1,128)}), f32[128,1,128]{2,1,0:T(1,128)S(1)}, u32[]{:S(2)}, u32[]{:S(2)}) %all-to-all-start.3) | async-done | bytes 65568 | tf_op jit(solution)/shard_map/all_to_all | solution.py:568
  81.7 0.0 collective-permute-done.6
  81.7 0.0 collective-permute-done.7
  81.7 11.9 %conditional.1 = (f32[19,20,4096]{2,1,0:T(8,128)}) conditional(s32[]{:T(128)} %convert_element_type.32, (f32[128,1,128]{2,1,0:T(1,128)S(1)}, s32[433]{0:T(512)S(1)}, f32[3,19,32,8,128]{4,3,2,1,0:T(8,128)}, s32[20,4096]{1,0:T(8,128)S(1)}, s32[18,24,128]{2,1,0:T(8,128)S(1)}, /*index=5*/f32[144,16,128]{2,1,0:T(8,128)}, f32[32,16,128]{2,1,0:T(8,128)S(1)}, ...), branch_computations={%region_7.8_spmd, %region_8.15_spmd} | conditional | flops 529296 | bytes 23973626 | solution.py:648
  81.7 11.9 %arrive_out.2 = f32[19,20,4096]{2,1,0:T(8,128)} custom-call(s32[433]{0:T(512)S(1)} %get-tuple-element.35.index, f32[128,128]{1,0:T(8,128)S(1)} %bitcast.30, f32[3,19,32,8,128]{4,3,2,1,0:T(8,128)} %get-tuple-element.37.before, s32[20,4096]{1,0:T(8,128)S(1)} %get-tuple-element.38.kinds, s32[18,24,128]{2,1,0:T(8,128)S(1)} %get-tuple-element.39.absent, ...), custom_call_target="tpu_custom_call" | custom-call | tf_op jit(solution)/shard_map/cond/branch_0_fun/arrive_out/pallas_call | solution.py:554
  (11 shorter events, 0.1 us)
Async XLA Ops:
  0.0 30.6 %copy-start.4 = (s32[18]{0:T(128)S(1)}, s32[18]{0:T(128)}, u32[]{:S(2)}) copy-start(s32[18]{0:T(128)} %constant.89.clone) | copy-start | bytes 220
  0.0 30.5 %copy-start.3 = (s32[20,18]{1,0:T(8,128)S(1)}, s32[20,18]{1,0:T(8,128)}, u32[]{:S(2)}) copy-start(s32[20,18]{1,0:T(8,128)} %neighbours.1) | copy-start | bytes 4324
  0.0 37.1 %copy-start = (s32[20,4096]{1,0:T(8,128)S(1)}, s32[20,4096]{1,0:T(8,128)}, u32[]{:S(2)}) copy-start(s32[20,4096]{1,0:T(8,128)} %kinds.3) | copy-start | bytes 983044
  13.3 21.4 %all-to-all-start.2 = ((f32[128,1,128]{2,1,0:T(1,128)}), f32[128,1,128]{2,1,0:T(1,128)S(1)}, u32[]{:S(2)}, u32[]{:S(2)}) async-start(f32[128,1,128]{2,1,0:T(1,128)} %bitcast.14), calls=%async_computation.2 | async-start | bytes 131072 | tf_op jit(solution)/shard_map/all_to_all | solution.py:568
  24.8 9.9 %collective-permute-start.4 = (f32[32,16,128]{2,1,0:T(8,128)S(1)}, f32[32,16,128]{2,1,0:T(8,128)S(1)}, u32[]{:S(2)}, u32[]{:S(2)}) collective-permute-start(f32[32,16,128]{2,1,0:T(8,128)S(1)} %get-tuple-element.74), channel_id=1, source_target_pairs={{0,1},{1,0},{2,3},{3,2},{4,5},{5,4},{6,7},{7,6},{8,9},{9,8},{10,11... | collective-permute-start | bytes 786440 | tf_op jit(solution)/shard_map/ppermute | solution.py:575
  26.2 10.7 %collective-permute-start.5 = (f32[32,16,128]{2,1,0:T(8,128)S(1)}, f32[32,16,128]{2,1,0:T(8,128)S(1)}, u32[]{:S(2)}, u32[]{:S(2)}) collective-permute-start(f32[32,16,128]{2,1,0:T(8,128)S(1)} %get-tuple-element.75), channel_id=1, source_target_pairs={{1,2},{3,4},{5,6},{7,8},{9,10},{11,12},{13,14},{15,16},{17,18},{19... | collective-permute-start | bytes 786440 | tf_op jit(solution)/shard_map/ppermute | solution.py:575
  56.4 25.4 %collective-permute-start.6 = (f32[32,16,128]{2,1,0:T(8,128)S(1)}, f32[32,16,128]{2,1,0:T(8,128)S(1)}, u32[]{:S(2)}, u32[]{:S(2)}) collective-permute-start(f32[32,16,128]{2,1,0:T(8,128)S(1)} %get-tuple-element.79), channel_id=1, source_target_pairs={{0,1},{1,0},{2,3},{3,2},{4,5},{5,4},{6,7},{7,6},{8,9},{9,8},{10,11... | collective-permute-start | bytes 786440 | tf_op jit(solution)/shard_map/ppermute | solution.py:575
  56.5 25.3 %collective-permute-start.7 = (f32[32,16,128]{2,1,0:T(8,128)S(1)}, f32[32,16,128]{2,1,0:T(8,128)S(1)}, u32[]{:S(2)}, u32[]{:S(2)}) collective-permute-start(f32[32,16,128]{2,1,0:T(8,128)S(1)} %get-tuple-element.80), channel_id=1, source_target_pairs={{1,2},{3,4},{5,6},{7,8},{9,10},{11,12},{13,14},{15,16},{17,18},{19... | collective-permute-start | bytes 786440 | tf_op jit(solution)/shard_map/ppermute | solution.py:575
  61.1 20.6 %all-to-all-start.3 = ((f32[128,1,128]{2,1,0:T(1,128)}), f32[128,1,128]{2,1,0:T(1,128)S(1)}, u32[]{:S(2)}, u32[]{:S(2)}) async-start(f32[128,1,128]{2,1,0:T(1,128)} %bitcast.18), calls=%async_computation.3 | async-start | bytes 131072 | tf_op jit(solution)/shard_map/all_to_all | solution.py:568

commit v6 on v5

--- a/solution.py
+++ b/solution.py
@@ -13,6 +13,7 @@
 SITES = 4096
 GROUP = 8
 CHUNKS = 32
+AT_ONCE = 4
 LIMIT = 52
 SLOTS = 32
 AXES = ("seg", "sub")
@@ -150,7 +151,7 @@
             layers[face, rows, :] = packed
         return carry
 
-    lax.fori_loop(0, BRICK, line, 0, unroll=4)
+    lax.fori_loop(0, BRICK, line, 0, unroll=8)
     unpack(layers, table, step)
 
 
@@ -181,14 +182,16 @@
     real = jnp.minimum(GROUP, bricks - step * GROUP)
 
     def fetch(scale):
-        def brick(j, carry):
-            base = (step * GROUP + j) * 18
-            for column in range(18):
-                block = scale(table[index[base + column]], COLUMN_FACE[column])
-                arriving[column, pl.ds(j, BRICK, stride=8), :] = block
+        def some(k, carry):
+            for i in range(AT_ONCE):
+                j = k * AT_ONCE + i
+                base = (step * GROUP + j) * 18
+                for column in range(18):
+                    block = scale(table[index[base + column]], COLUMN_FACE[column])
+                    arriving[column, pl.ds(j, BRICK, stride=8), :] = block
             return carry
 
-        lax.fori_loop(0, real, brick, 0)
+        lax.fori_loop(0, (real + AT_ONCE - 1) // AT_ONCE, some, 0)
 
     @pl.when(outlets > 0.0)
     def _():
@@ -272,7 +275,7 @@
                 put(member, 2 * x + h, parts[h])
         return carry
 
-    lax.fori_loop(0, BRICK, line, 0, unroll=2)
+    lax.fori_loop(0, BRICK, line, 0, unroll=4)
 
     for member in range(19):
         cx, cy, cz = SPEEDS[member]
@@ -345,7 +348,7 @@
                 carry[2] + jnp.where(real & (kind == 3), 1.0, 0.0))
 
     zero = jnp.zeros((GROUP, 128), F32)
-    total = lax.fori_loop(0, CHUNKS, chunk, (zero, zero, zero), unroll=4)
+    total = lax.fori_loop(0, CHUNKS, chunk, (zero, zero, zero), unroll=8)
 
     @pl.when(step == 0)
     def _():
@@ -365,7 +368,7 @@
         rows_out[...] = jnp.where(lane == 127, excess, both)
 
 
-def plan_sends(neighbours, me, lists):
+def plan_sends(neighbours, me, lists, step):
     bricks = neighbours.shape[0]
     low = me * bricks
     high = low + bricks
@@ -386,7 +389,14 @@
             behind += jnp.where(first < low, 1, 0)
         return ahead, behind
 
-    ahead, behind = lax.fori_loop(0, bricks, brick, (jnp.int32(0), jnp.int32(0)))
+    @pl.when(step == 0)
+    def _():
+        lists[127] = 0
+        lists[255] = 0
+
+    start = step * GROUP
+    ahead, behind = lax.fori_loop(start, jnp.minimum(start + GROUP, bricks), brick,
+                                  (lists[following + 127], lists[preceding + 127]))
     lists[following + 127] = ahead
     lists[preceding + 127] = behind
 
@@ -420,10 +430,7 @@
     step = pl.program_id(0)
     slots = send_even.shape[0]
 
-    @pl.when(step == 0)
-    def _():
-        plan_sends(neighbours, me[0], lists)
-
+    plan_sends(neighbours, me[0], lists, step)
     excess = jnp.where(jnp.maximum(lists[127], lists[255]) > slots, 1.0, 0.0)
 
     def load(i, c):

time: 94 us -> 91 us (0.968)
  Pallas kernels: 44.4 us -> 41.5 us
    pallas_call x1, Pallas kernels: 19.3 us -> 17.7 us  [middle_call(): pl.pallas_call(functools.partial(middle_kernel, bricks), grid=(groups,),...]
  transfers between devices with their start and end apart: 6 -> 6, of which waited for: 3 -> 3; matrix products, arithmetic and copies ran while one was open for 2% -> 3% of each run, Pallas kernels for 0% -> 0%
where the time goes in v6:
time: 91 us; the launch traced here: 90.8 us
  Pallas kernels  41.5 us (46%)
  starting transfers between devices  32.6 us (36%)
  waiting for transfers between devices  13.3 us (15%)
  other arithmetic  1.79 us (2%)
    all_to_all x2, starting transfers between devices, share_sums(): return lax.all_to_all(rows, AXES, 0, 0, tiled=True)  22.3 us
    pallas_call x1, Pallas kernels, middle_call(): pl.pallas_call(functools.partial(middle_kernel, bricks), grid=(groups,),...  17.7 us
    pallas_call x1, Pallas kernels, first_call(): pl.pallas_call(functools.partial(first_kernel, pops.shape[1]), grid=(grou...  12.5 us
    pallas_call x1, Pallas kernels, last_call(): pl.pallas_call(functools.partial(last_kernel, bricks), grid=(groups,), in...  11.3 us
    all_to_all x2, waiting for transfers between devices, share_sums(): return lax.all_to_all(rows, AXES, 0, 0, tiled=True)  11 us
    ppermute x2, starting transfers between devices, swap(): lax.ppermute(send[1], AXES, odd_pairs)  8.83 us
    ppermute x2, waiting for transfers between devices, swap(): lax.ppermute(send[1], AXES, odd_pairs)  2.28 us
  transfers between devices with their start and end apart: 6, of which 3 were waited for; matrix products, arithmetic and copies ran while one was open for 3% of the time, Pallas kernels for 0%

profile of v6, /device:TPU:1, one launch (start us, length us, event | category | flops | bytes accessed | tf_op | source)
XLA Modules:
  0.0 90.8 jit_solution(4353865150879378620)
XLA Ops:
  0.0 0.0 copy-start.4
  0.0 0.0 copy-start.3
  0.0 0.0 copy-start
  0.0 12.5 %first_collide.3 = (f32[3,19,32,8,128]{4,3,2,1,0:T(8,128)}, f32[144,16,128]{2,1,0:T(8,128)}, f32[32,16,128]{2,1,0:T(8,128)S(1)}, f32[32,16,128]{2,1,0:T(8,128)S(1)}, f32[128,128]{1,0:T(8,128)}, /*index=5*/s32[256]{0:T(256)S(1)}) custom-call(s32[1]{0:T(128)} %bitcast.11.me, s32[20,18]{1,0:T(8,128)} %neighbours.1, f32[19,20,4096]{2,1,0:T(8,128)} %bitcast.28, ...), custom_call_target="tpu_custom_call" | custom-call | tf_op jit(solution)/shard_map/first_collide/pallas_call | solution.py:524
  12.6 11.5 %all-to-all-start.2 = ((f32[128,1,128]{2,1,0:T(1,128)}), f32[128,1,128]{2,1,0:T(1,128)S(1)}, u32[]{:S(2)}, u32[]{:S(2)}) async-start(f32[128,1,128]{2,1,0:T(1,128)} %bitcast.14), calls=%async_computation.2 | async-start | bytes 131072 | tf_op jit(solution)/shard_map/all_to_all | solution.py:575
  24.1 1.5 %collective-permute-start.4 = (f32[32,16,128]{2,1,0:T(8,128)S(1)}, f32[32,16,128]{2,1,0:T(8,128)S(1)}, u32[]{:S(2)}, u32[]{:S(2)}) collective-permute-start(f32[32,16,128]{2,1,0:T(8,128)S(1)} %get-tuple-element.74), channel_id=1, source_target_pairs={{0,1},{1,0},{2,3},{3,2},{4,5},{5,4},{6,7},{7,6},{8,9},{9,8},{10,11... | collective-permute-start | bytes 786440 | tf_op jit(solution)/shard_map/ppermute | solution.py:582
  25.5 4.2 %collective-permute-start.5 = (f32[32,16,128]{2,1,0:T(8,128)S(1)}, f32[32,16,128]{2,1,0:T(8,128)S(1)}, u32[]{:S(2)}, u32[]{:S(2)}) collective-permute-start(f32[32,16,128]{2,1,0:T(8,128)S(1)} %get-tuple-element.75), channel_id=1, source_target_pairs={{1,2},{3,4},{5,6},{7,8},{9,10},{11,12},{13,14},{15,16},{17,18},{19... | collective-permute-start | bytes 786440 | tf_op jit(solution)/shard_map/ppermute | solution.py:582
  29.8 0.0 copy-done.3
  29.8 0.1 copy.16
  29.9 0.0 copy-done.4
  29.9 0.1 eq.53
  30.0 0.1 fusion.2
  30.2 0.1 select_reduce_fusion.6
  30.3 0.2 select_reduce_fusion.4
  30.5 0.1 eq.50
  30.6 0.1 fusion.3
  30.8 0.1 select_reduce_fusion.7
  30.9 0.2 select_reduce_fusion.5
  31.1 0.1 add.118
  31.2 0.1 add.123
  31.4 0.1 reshape.65
  31.5 0.1 pad_add_fusion.1.index
  31.5 2.4 %all-to-all-done.2 = f32[128,1,128]{2,1,0:T(1,128)S(1)} async-done(((f32[128,1,128]{2,1,0:T(1,128)}), f32[128,1,128]{2,1,0:T(1,128)S(1)}, u32[]{:S(2)}, u32[]{:S(2)}) %all-to-all-start.2) | async-done | bytes 65568 | tf_op jit(solution)/shard_map/all_to_all | solution.py:575
  34.0 0.0 collective-permute-done.4.even
  34.0 2.3 %collective-permute-done.5.odd = f32[32,16,128]{2,1,0:T(8,128)S(1)} collective-permute-done((f32[32,16,128]{2,1,0:T(8,128)S(1)}, f32[32,16,128]{2,1,0:T(8,128)S(1)}, u32[]{:S(2)}, u32[]{:S(2)}) %collective-permute-start.5) | collective-permute-done | bytes 262176 | tf_op jit(solution)/shard_map/ppermute | solution.py:582
  36.3 0.1 broadcast_in_dim.106.absent
  36.4 0.0 copy-done
  36.4 17.7 %arrive_collide.3 = (f32[3,19,32,8,128]{4,3,2,1,0:T(8,128)}, f32[144,16,128]{2,1,0:T(8,128)}, f32[32,16,128]{2,1,0:T(8,128)S(1)}, f32[32,16,128]{2,1,0:T(8,128)S(1)}, f32[128,128]{1,0:T(8,128)}) custom-call(s32[256]{0:T(256)S(1)} %get-tuple-element.71.lists, s32[433]{0:T(512)S(1)} %pad_add_fusion.1.index, f32[128,128]{1,0:T(8,128)S(1)} %bitcast.23, ...), custom_call_target="tpu_custom_call" | custom-call | tf_op jit(solution)/shard_map/arrive_collide/pallas_call | solution.py:541
  54.1 0.1 collective-permute-start.6
  54.2 4.6 %collective-permute-start.7 = (f32[32,16,128]{2,1,0:T(8,128)S(1)}, f32[32,16,128]{2,1,0:T(8,128)S(1)}, u32[]{:S(2)}, u32[]{:S(2)}) collective-permute-start(f32[32,16,128]{2,1,0:T(8,128)S(1)} %get-tuple-element.80), channel_id=1, source_target_pairs={{1,2},{3,4},{5,6},{7,8},{9,10},{11,12},{13,14},{15,16},{17,18},{19... | collective-permute-start | bytes 786440 | tf_op jit(solution)/shard_map/ppermute | solution.py:582
  58.8 10.8 %all-to-all-start.3 = ((f32[128,1,128]{2,1,0:T(1,128)}), f32[128,1,128]{2,1,0:T(1,128)S(1)}, u32[]{:S(2)}, u32[]{:S(2)}) async-start(f32[128,1,128]{2,1,0:T(1,128)} %bitcast.18), calls=%async_computation.3 | async-start | bytes 131072 | tf_op jit(solution)/shard_map/all_to_all | solution.py:575
  69.6 0.7 slice_reduce_fusion
  70.9 8.5 %all-to-all-done.3 = f32[128,1,128]{2,1,0:T(1,128)S(1)} async-done(((f32[128,1,128]{2,1,0:T(1,128)}), f32[128,1,128]{2,1,0:T(1,128)S(1)}, u32[]{:S(2)}, u32[]{:S(2)}) %all-to-all-start.3) | async-done | bytes 65568 | tf_op jit(solution)/shard_map/all_to_all | solution.py:575
  79.5 0.0 collective-permute-done.6
  79.5 0.0 collective-permute-done.7
  79.5 11.3 %conditional.1 = (f32[19,20,4096]{2,1,0:T(8,128)}) conditional(s32[]{:T(128)} %convert_element_type.32, (f32[128,1,128]{2,1,0:T(1,128)S(1)}, s32[433]{0:T(512)S(1)}, f32[3,19,32,8,128]{4,3,2,1,0:T(8,128)}, s32[20,4096]{1,0:T(8,128)S(1)}, s32[18,24,128]{2,1,0:T(8,128)S(1)}, /*index=5*/f32[144,16,128]{2,1,0:T(8,128)}, f32[32,16,128]{2,1,0:T(8,128)S(1)}, ...), branch_computations={%region_7.8_spmd, %region_8.15_spmd} | conditional | flops 529296 | bytes 23973626 | solution.py:655
  79.5 11.3 %arrive_out.2 = f32[19,20,4096]{2,1,0:T(8,128)} custom-call(s32[433]{0:T(512)S(1)} %get-tuple-element.35.index, f32[128,128]{1,0:T(8,128)S(1)} %bitcast.30, f32[3,19,32,8,128]{4,3,2,1,0:T(8,128)} %get-tuple-element.37.before, s32[20,4096]{1,0:T(8,128)S(1)} %get-tuple-element.38.kinds, s32[18,24,128]{2,1,0:T(8,128)S(1)} %get-tuple-element.39.absent, ...), custom_call_target="tpu_custom_call" | custom-call | tf_op jit(solution)/shard_map/cond/branch_0_fun/arrive_out/pallas_call | solution.py:561
  (11 shorter events, 0.1 us)
Async XLA Ops:
  0.0 29.9 %copy-start.4 = (s32[18]{0:T(128)S(1)}, s32[18]{0:T(128)}, u32[]{:S(2)}) copy-start(s32[18]{0:T(128)} %constant.89.clone) | copy-start | bytes 220
  0.0 29.8 %copy-start.3 = (s32[20,18]{1,0:T(8,128)S(1)}, s32[20,18]{1,0:T(8,128)}, u32[]{:S(2)}) copy-start(s32[20,18]{1,0:T(8,128)} %neighbours.1) | copy-start | bytes 4324
  0.0 36.4 %copy-start = (s32[20,4096]{1,0:T(8,128)S(1)}, s32[20,4096]{1,0:T(8,128)}, u32[]{:S(2)}) copy-start(s32[20,4096]{1,0:T(8,128)} %kinds.3) | copy-start | bytes 983044
  12.6 21.4 %all-to-all-start.2 = ((f32[128,1,128]{2,1,0:T(1,128)}), f32[128,1,128]{2,1,0:T(1,128)S(1)}, u32[]{:S(2)}, u32[]{:S(2)}) async-start(f32[128,1,128]{2,1,0:T(1,128)} %bitcast.14), calls=%async_computation.2 | async-start | bytes 131072 | tf_op jit(solution)/shard_map/all_to_all | solution.py:575
  24.1 9.9 %collective-permute-start.4 = (f32[32,16,128]{2,1,0:T(8,128)S(1)}, f32[32,16,128]{2,1,0:T(8,128)S(1)}, u32[]{:S(2)}, u32[]{:S(2)}) collective-permute-start(f32[32,16,128]{2,1,0:T(8,128)S(1)} %get-tuple-element.74), channel_id=1, source_target_pairs={{0,1},{1,0},{2,3},{3,2},{4,5},{5,4},{6,7},{7,6},{8,9},{9,8},{10,11... | collective-permute-start | bytes 786440 | tf_op jit(solution)/shard_map/ppermute | solution.py:582
  25.5 10.7 %collective-permute-start.5 = (f32[32,16,128]{2,1,0:T(8,128)S(1)}, f32[32,16,128]{2,1,0:T(8,128)S(1)}, u32[]{:S(2)}, u32[]{:S(2)}) collective-permute-start(f32[32,16,128]{2,1,0:T(8,128)S(1)} %get-tuple-element.75), channel_id=1, source_target_pairs={{1,2},{3,4},{5,6},{7,8},{9,10},{11,12},{13,14},{15,16},{17,18},{19... | collective-permute-start | bytes 786440 | tf_op jit(solution)/shard_map/ppermute | solution.py:582
  54.1 25.4 %collective-permute-start.6 = (f32[32,16,128]{2,1,0:T(8,128)S(1)}, f32[32,16,128]{2,1,0:T(8,128)S(1)}, u32[]{:S(2)}, u32[]{:S(2)}) collective-permute-start(f32[32,16,128]{2,1,0:T(8,128)S(1)} %get-tuple-element.79), channel_id=1, source_target_pairs={{0,1},{1,0},{2,3},{3,2},{4,5},{5,4},{6,7},{7,6},{8,9},{9,8},{10,11... | collective-permute-start | bytes 786440 | tf_op jit(solution)/shard_map/ppermute | solution.py:582
  54.2 25.3 %collective-permute-start.7 = (f32[32,16,128]{2,1,0:T(8,128)S(1)}, f32[32,16,128]{2,1,0:T(8,128)S(1)}, u32[]{:S(2)}, u32[]{:S(2)}) collective-permute-start(f32[32,16,128]{2,1,0:T(8,128)S(1)} %get-tuple-element.80), channel_id=1, source_target_pairs={{1,2},{3,4},{5,6},{7,8},{9,10},{11,12},{13,14},{15,16},{17,18},{19... | collective-permute-start | bytes 786440 | tf_op jit(solution)/shard_map/ppermute | solution.py:582
  58.8 20.6 %all-to-all-start.3 = ((f32[128,1,128]{2,1,0:T(1,128)}), f32[128,1,128]{2,1,0:T(1,128)S(1)}, u32[]{:S(2)}, u32[]{:S(2)}) async-start(f32[128,1,128]{2,1,0:T(1,128)} %bitcast.18), calls=%async_computation.3 | async-start | bytes 131072 | tf_op jit(solution)/shard_map/all_to_all | solution.py:575
